TPU v7x, 32 devices: a whole 2x2x4 slice. The times are simulated.
32 devices in a mesh: shot: 8 (over y, x, core), slab: 4 (over z).
Axes of the slice: x: 2, y: 2, z: 4, core: 2. Of those that a mesh axis runs over, the one named last changes fastest.
Arguments:
- velocity: float32 [64, 64, 128], P('slab', 'shot'), may hold values from 1.5 to 4.5
- aperture_start: int32 [8], P('shot'), may hold values from 0 to 4, as said below
- aperture_count: int32 [8], P('shot'), may hold values from 1 to 4
- wave_prev: float32 [8, 64, 32, 128], P('shot', 'slab'), may hold values from -6 to 6
- wave_now: float32 [8, 64, 32, 128], P('shot', 'slab'), may hold values from -6 to 6
- adjoint_prev: float32 [8, 64, 32, 128], P('shot', 'slab'), may hold values from -6 to 6
- adjoint_now: float32 [8, 64, 32, 128], P('shot', 'slab'), may hold values from -6 to 6
- source_cells: int32 [8, 4, 3], P('shot'), may hold values from 0 to 127, as said below
- wavelet: float32 [8, 4, 4], P('shot'), may hold values from -6 to 6
- receiver_cells: int32 [8, 16, 3], P('shot'), may hold values from 0 to 127, as said below
- trace: float32 [8, 4, 16], P('shot'), may hold values from -6 to 6
Outputs:
- wave_final: float32 [8, 64, 32, 128], P('shot', 'slab')
- adjoint_final: float32 [8, 64, 32, 128], P('shot', 'slab')
- gradient: float32 [64, 64, 128], P('slab', 'shot')
Inputs may be any that keep to these rules, and one draw needn't show every extreme that they name: aperture_start[g] lies between g - 3 and g, and at most 4. `source_cells`: x below 64, window y below 8, z below 128. `receiver_cells`: x below 64, window y below 8, z below 128.
All inputs are finite; a program needn't handle non-finite values.
Results may differ from a plain program's by a relative error of at most 0.0003.
Values sent between devices are 32-bit elements; how exact they have to be, the bound alone decides.
No kernel may reach another device: no remote copies, remote signals or barrier semaphores. Data moves between devices by JAX's collectives and lax.ppermute only.
A program may use at most 64 MiB of HBM per device.

v0:
```python
import jax
import jax.numpy as jnp
from jax import lax
from jax.sharding import PartitionSpec as P

STEPS = 4


stencil_weights = (-205.0 / 72.0, 8.0 / 5.0, -1.0 / 5.0, 8.0 / 315.0, -1.0 / 560.0)
time_step = 0.09


def passed_along(block, axis, distance):
    devices = range(lax.axis_size(axis))
    route = [(i - distance, i) for i in devices if i - distance in devices]
    return lax.ppermute(block, axis, route)


def padded_2(cells, sides, width):
    for axis, dim in sides:
        count = lax.axis_size(axis)
        ends = count - 1
        head = lax.slice_in_dim(cells, 0, width, axis=dim)
        tail = lax.slice_in_dim(cells, cells.shape[dim] - width, cells.shape[dim], axis=dim)
        cells = jnp.concatenate(
            [
                lax.ppermute(tail, axis, [(i, (i + 1) % count) for i in range(ends)]),
                cells,
                lax.ppermute(head, axis, [((i + 1) % count, i) for i in range(ends)]),
            ],
            axis=dim,
        )
    return cells


def stencil(padded):
    size_x = padded.shape[-3] - 8
    size_y = padded.shape[-2] - 8
    size_z = padded.shape[-1] - 8
    center = padded[..., 4 : 4 + size_x, 4 : 4 + size_y, 4 : 4 + size_z]
    total = 3.0 * stencil_weights[0] * center
    for k in range(1, 5):
        near = padded[..., 4 + k : 4 + k + size_x, 4 : 4 + size_y, 4 : 4 + size_z]
        near = near + padded[..., 4 - k : 4 - k + size_x, 4 : 4 + size_y, 4 : 4 + size_z]
        near = near + padded[..., 4 : 4 + size_x, 4 + k : 4 + k + size_y, 4 : 4 + size_z]
        near = near + padded[..., 4 : 4 + size_x, 4 - k : 4 - k + size_y, 4 : 4 + size_z]
        near = near + padded[..., 4 : 4 + size_x, 4 : 4 + size_y, 4 + k : 4 + k + size_z]
        near = near + padded[..., 4 : 4 + size_x, 4 : 4 + size_y, 4 - k : 4 - k + size_z]
        total = total + stencil_weights[k] * near
    return total


def inject(cells, amps, x_cells, rows, depth):
    along_x = (x_cells[:, None] == cells[None, :, 0]).astype(jnp.float32) * amps[None, :]
    along_y = (jnp.arange(rows)[:, None] == cells[None, :, 1]).astype(jnp.float32)
    along_z = (jnp.arange(depth)[:, None] == cells[None, :, 2]).astype(jnp.float32)
    return jnp.einsum("xs,ys,zs->xyz", along_x, along_y, along_z, precision=lax.Precision.HIGHEST)


def per_device(
    velocity,
    aperture_start,
    aperture_count,
    wave_prev,
    wave_now,
    adjoint_prev,
    adjoint_now,
    source_cells,
    wavelet,
    receiver_cells,
    trace,
):
    slab_cells, block_rows, depth_cells = velocity.shape
    window_rows = wave_now.shape[2]
    aperture = window_rows // block_rows
    spread_blocks = aperture - 1
    group_index = lax.axis_index("shot")
    start_block = aperture_start[0]
    live_count = aperture_count[0]
    pieces = []
    for offset in range(-spread_blocks, spread_blocks + 1):
        if offset == 0:
            pieces.append(velocity)
        else:
            pieces.append(passed_along(velocity, "shot", -offset))
    nearby = jnp.concatenate(pieces, axis=1)
    window = lax.dynamic_slice_in_dim(
        nearby, (start_block - group_index + spread_blocks) * block_rows, window_rows, 1
    )
    x_cells = lax.axis_index("slab") * slab_cells + jnp.arange(slab_cells)
    live = (jnp.arange(window_rows) < live_count * block_rows).astype(jnp.float32)[None, :, None]
    courant = window * window * (time_step * time_step)
    imaging = 2.0 * time_step * time_step * window
    w_prev = wave_prev[0] * live
    w_now = wave_now[0] * live
    j_prev = adjoint_prev[0] * live
    j_now = adjoint_now[0] * live
    grad = jnp.zeros((slab_cells, window_rows, depth_cells), jnp.float32)
    for step in range(STEPS):
        stacked = jnp.stack([w_now, j_now])
        haloed = padded_2(stacked, (("slab", 1),), 4)
        padded = jnp.pad(haloed, ((0, 0), (0, 0), (4, 4), (4, 4)))
        lapl = stencil(padded)
        grad = grad + imaging * j_now * lapl[0]
        w_next = (
            2.0 * w_now
            - w_prev
            + courant * lapl[0]
            + inject(source_cells[0], wavelet[0, step], x_cells, window_rows, depth_cells)
        ) * live
        j_next = (
            2.0 * j_now
            - j_prev
            + courant * lapl[1]
            + inject(receiver_cells[0], trace[0, step], x_cells, window_rows, depth_cells)
        ) * live
        w_prev, w_now = (w_now, w_next)
        j_prev, j_now = (j_now, j_next)
    buffer = jnp.zeros((slab_cells, (2 * spread_blocks + 1) * block_rows, depth_cells), jnp.float32)
    buffer = lax.dynamic_update_slice_in_dim(
        buffer, grad, (start_block - group_index + spread_blocks) * block_rows, 1
    )
    gradient = buffer[:, spread_blocks * block_rows : (spread_blocks + 1) * block_rows, :]
    for offset in range(-spread_blocks, spread_blocks + 1):
        if offset != 0:
            piece = buffer[
                :,
                (spread_blocks + offset) * block_rows : (spread_blocks + offset + 1) * block_rows,
                :,
            ]
            gradient = gradient + passed_along(piece, "shot", offset)
    return (w_now[None], j_now[None], gradient)


def solution(mesh):
    return jax.shard_map(
        per_device,
        mesh=mesh,
        in_specs=(
            P("slab", "shot", None),
            P("shot"),
            P("shot"),
            P("shot", "slab", None, None),
            P("shot", "slab", None, None),
            P("shot", "slab", None, None),
            P("shot", "slab", None, None),
            P("shot", None, None),
            P("shot", None, None),
            P("shot", None, None),
            P("shot", None, None),
        ),
        out_specs=(
            P("shot", "slab", None, None),
            P("shot", "slab", None, None),
            P("slab", "shot", None),
        ),
        check_vma=False,
    )
```

profile of v0, /device:TPU:27, one launch (start us, length us, event | category | flops | bytes accessed | tf_op | source)
XLA Modules:
  0.0 124.4 jit_solution(583033862533313273)
XLA Ops:
  0.6 0.9 copy.33
  1.6 3.7 %collective-permute-start = (f32[16,8,128]{2,0,1:T(8,128)S(1)}, f32[16,8,128]{2,0,1:T(8,128)S(1)}, u32[]{:S(2)}, u32[]{:S(2)}) collective-permute-start(f32[16,8,128]{2,0,1:T(8,128)S(1)} %copy.33), channel_id=1, source_target_pairs={{0,12},{4,16},{8,20},{12,24},{16,28},{1,13},{5,17},{9,21},{13,25},... | collective-permute-start | bytes 196616 | tf_op jit(solution)/shard_map/ppermute | solution.py:16
  5.3 1.9 %collective-permute-start.1 = (f32[16,8,128]{2,0,1:T(8,128)S(1)}, f32[16,8,128]{2,0,1:T(8,128)S(1)}, u32[]{:S(2)}, u32[]{:S(2)}) collective-permute-start(f32[16,8,128]{2,0,1:T(8,128)S(1)} %copy.33), channel_id=1, source_target_pairs={{0,8},{4,12},{8,16},{12,20},{16,24},{20,28},{1,9},{5,13},{9,17},{1... | collective-permute-start | bytes 196616 | tf_op jit(solution)/shard_map/ppermute | solution.py:16
  7.2 2.8 %collective-permute-start.2 = (f32[16,8,128]{2,0,1:T(8,128)S(1)}, f32[16,8,128]{2,0,1:T(8,128)S(1)}, u32[]{:S(2)}, u32[]{:S(2)}) collective-permute-start(f32[16,8,128]{2,0,1:T(8,128)S(1)} %copy.33), channel_id=1, source_target_pairs={{0,4},{4,8},{8,12},{12,16},{16,20},{20,24},{24,28},{1,5},{5,9},{9,... | collective-permute-start | bytes 196616 | tf_op jit(solution)/shard_map/ppermute | solution.py:16
  10.0 2.3 %collective-permute-start.3 = (f32[16,8,128]{2,0,1:T(8,128)S(1)}, f32[16,8,128]{2,0,1:T(8,128)S(1)}, u32[]{:S(2)}, u32[]{:S(2)}) collective-permute-start(f32[16,8,128]{2,0,1:T(8,128)S(1)} %copy.33), channel_id=1, source_target_pairs={{4,0},{8,4},{12,8},{16,12},{20,16},{24,20},{28,24},{5,1},{9,5},{13... | collective-permute-start | bytes 196616 | tf_op jit(solution)/shard_map/ppermute | solution.py:16
  12.3 3.3 %collective-permute-start.4 = (f32[16,8,128]{2,0,1:T(8,128)S(1)}, f32[16,8,128]{2,0,1:T(8,128)S(1)}, u32[]{:S(2)}, u32[]{:S(2)}) collective-permute-start(f32[16,8,128]{2,0,1:T(8,128)S(1)} %copy.33), channel_id=1, source_target_pairs={{8,0},{12,4},{16,8},{20,12},{24,16},{28,20},{9,1},{13,5},{17,9},{2... | collective-permute-start | bytes 196616 | tf_op jit(solution)/shard_map/ppermute | solution.py:16
  16.3 0.8 slice_bitcast_fusion.8
  17.1 0.7 copy.65
  18.5 0.8 slice_bitcast_fusion.9
  19.3 0.8 copy.42
  20.1 0.2 slice_reduce_fusion
  20.3 1.3 %copy_multiply_fusion.1 = (f32[1,16,32,128]{3,1,2,0:T(8,128)S(1)}, f32[1,16,32,128]{3,1,2,0:T(8,128)S(1)}) fusion(f32[1,16,32,128]{3,2,1,0:T(8,128)} %param.15, f32[32]{0:T(128)S(1)} %compare_convert_fusion, f32[1,16,32,128]{3,2,1,0:T(8,128)} %param.17), kind=kLoop, calls=%fused_computation.224 | loop fusion | flops 131072 | bytes 1048704 | tf_op jit(solution)/shard_map/mul | solution.py:95
  21.7 0.1 fusion.116
  21.7 0.7 fusion.129
  22.5 1.9 %collective-permute-start.5 = (f32[16,8,128]{2,0,1:T(8,128)S(1)}, f32[16,8,128]{2,0,1:T(8,128)S(1)}, u32[]{:S(2)}, u32[]{:S(2)}) collective-permute-start(f32[16,8,128]{2,0,1:T(8,128)S(1)} %copy.33), channel_id=1, source_target_pairs={{12,0},{16,4},{20,8},{24,12},{28,16},{13,1},{17,5},{21,9},{25,13},... | collective-permute-start | bytes 196616 | tf_op jit(solution)/shard_map/ppermute | solution.py:16
  24.4 2.1 %collective-permute-start.6 = (f32[2,4,32,128]{3,1,2,0:T(4,128)S(1)}, f32[2,4,32,128]{3,1,2,0:T(4,128)S(1)}, u32[]{:S(2)}, u32[]{:S(2)}) collective-permute-start(f32[2,4,32,128]{3,1,2,0:T(4,128)S(1)} %get-tuple-element.27), channel_id=1, source_target_pairs={{1,0},{2,1},{3,2},{5,4},{6,5},{7,6},{9,8},{10,9},{11,10},{13,12},{... | collective-permute-start | bytes 393224 | tf_op jit(solution)/shard_map/ppermute | solution.py:29
  26.5 1.3 %collective-permute-start.7 = (f32[2,4,32,128]{3,1,2,0:T(4,128)S(1)}, f32[2,4,32,128]{3,1,2,0:T(4,128)S(1)}, u32[]{:S(2)}, u32[]{:S(2)}) collective-permute-start(f32[2,4,32,128]{3,1,2,0:T(4,128)S(1)} %get-tuple-element.26), channel_id=1, source_target_pairs={{0,1},{1,2},{2,3},{4,5},{5,6},{6,7},{8,9},{9,10},{10,11},{12,13},{... | collective-permute-start | bytes 393224 | tf_op jit(solution)/shard_map/ppermute | solution.py:27
  27.9 0.4 collective-permute-done.5
  28.4 1.2 collective-permute-done.6
  29.6 3.9 %collective-permute-done.7 = f32[2,4,32,128]{3,1,2,0:T(4,128)S(1)} collective-permute-done((f32[2,4,32,128]{3,1,2,0:T(4,128)S(1)}, f32[2,4,32,128]{3,1,2,0:T(4,128)S(1)}, u32[]{:S(2)}, u32[]{:S(2)}) %collective-permute-start.7) | collective-permute-done | bytes 131104 | tf_op jit(solution)/shard_map/ppermute | solution.py:27
  33.5 1.0 pad_maximum_fusion
  34.5 0.7 select_maximum_fusion.9
  35.3 5.2 %fusion.40 = f32[2,16,32,128]{3,1,2,0:T(8,128)} fusion(f32[1,16,32,128]{3,1,2,0:T(8,128)} %copy-done.4, f32[1,16,32,128]{3,1,2,0:T(8,128)S(1)} %get-tuple-element.53, f32[2,24,40,136]{3,1,2,0:T(8,128)S(1)} %select_maximum_fusion.9, f32[2,20,32,128]{3,1,2,0:T(8,128)} %get-tuple-element.25, f32[2,20,32,128]{3,1,2,0:T(8,128)S(1)} %get-tuple-element.24), kind=kLoop, calls=%fused_computation.92 | loop fusion | flops 3932160 | bytes 13631488 | tf_op jit(solution)/shard_map/add | solution.py:49
  40.4 1.7 %fusion.13 = f32[16,32,128]{2,0,1:T(8,128)S(1)} fusion(f32[2,16,32,128]{3,1,2,0:T(8,128)} %fusion.40, f32[1,16,32,128]{3,2,1,0:T(8,128)} %param.16, f32[1,16,32,128]{3,2,1,0:T(8,128)} %param.17, f32[16,16]{0,1:T(8,128)S(1)} %get-tuple-element.48, f32[16,32]{0,1:T(8,128)S(1)} %convert_bitcast_fusion, f32[32]{0:T(128)S(1)} %compare_convert_fusion, ...), kind=kOutput, calls=%fused_computation.37 | convolution fusion | flops 13248512 | bytes 1313988 | tf_op jit(solution)/shard_map/xs,ys,zs->xyz/dot_general | solution.py:57
  42.1 1.8 %fusion.7 = f32[16,32,128]{2,0,1:T(8,128)S(1)} fusion(f32[1,16,32,128]{3,2,1,0:T(8,128)} %param.14, f32[2,16,32,128]{3,1,2,0:T(8,128)} %fusion.40, f32[1,16,32,128]{3,2,1,0:T(8,128)} %param.15, f32[32]{0:T(128)S(1)} %compare_convert_fusion, f32[4,16]{1,0:T(4,128)} %get-tuple-element.52, f32[4,32]{0,1:T(8,128)S(1)} %convert_bitcast_fusion.1, ...), kind=kOutput, calls=%fused_computation.27 | convolution fusion | flops 3803648 | bytes 1311636 | tf_op jit(solution)/shard_map/xs,ys,zs->xyz/dot_general | solution.py:57
  44.0 2.1 %collective-permute-start.8 = (f32[2,4,32,128]{3,1,2,0:T(4,128)S(1)}, f32[2,4,32,128]{3,1,2,0:T(4,128)S(1)}, u32[]{:S(2)}, u32[]{:S(2)}) collective-permute-start(f32[2,4,32,128]{3,1,2,0:T(4,128)S(1)} %get-tuple-element.23), channel_id=1, source_target_pairs={{1,0},{2,1},{3,2},{5,4},{6,5},{7,6},{9,8},{10,9},{11,10},{13,12},{... | collective-permute-start | bytes 393224 | tf_op jit(solution)/shard_map/ppermute | solution.py:29
  46.1 1.3 %collective-permute-start.9 = (f32[2,4,32,128]{3,1,2,0:T(4,128)S(1)}, f32[2,4,32,128]{3,1,2,0:T(4,128)S(1)}, u32[]{:S(2)}, u32[]{:S(2)}) collective-permute-start(f32[2,4,32,128]{3,1,2,0:T(4,128)S(1)} %get-tuple-element.22), channel_id=1, source_target_pairs={{0,1},{1,2},{2,3},{4,5},{5,6},{6,7},{8,9},{9,10},{10,11},{12,13},{... | collective-permute-start | bytes 393224 | tf_op jit(solution)/shard_map/ppermute | solution.py:27
  47.4 0.6 collective-permute-done.8
  48.0 3.8 %collective-permute-done.9 = f32[2,4,32,128]{3,1,2,0:T(4,128)S(1)} collective-permute-done((f32[2,4,32,128]{3,1,2,0:T(4,128)S(1)}, f32[2,4,32,128]{3,1,2,0:T(4,128)S(1)}, u32[]{:S(2)}, u32[]{:S(2)}) %collective-permute-start.9) | collective-permute-done | bytes 131104 | tf_op jit(solution)/shard_map/ppermute | solution.py:27
  51.8 1.3 %pad_maximum_fusion.1 = (f32[2,20,32,128]{3,1,2,0:T(8,128)}, f32[2,20,32,128]{3,1,2,0:T(8,128)}) fusion(f32[2,4,32,128]{3,1,2,0:T(4,128)S(1)} %collective-permute-done.8, f32[1,16,32,128]{3,1,2,0:T(8,128)S(1)} %bitcast.236, f32[1,16,32,128]{3,1,2,0:T(8,128)S(1)} %bitcast.248, f32[2,4,32,128]{3,1,2,0:T(4,128)S(1)} %collective-permute-done.9), kind=kLoop, calls=%fused_computation.47 | loop fusion | flops 655360 | bytes 2097152 | tf_op jit(solution)/shard_map/concatenate | solution.py:25
  53.1 0.7 select_maximum_fusion.6
  53.9 5.9 %fusion.35 = f32[2,16,32,128]{3,1,2,0:T(8,128)} fusion(f32[1,16,32,128]{3,1,2,0:T(8,128)S(1)} %bitcast.238, f32[1,16,32,128]{3,1,2,0:T(8,128)S(1)} %bitcast.250, f32[2,24,40,136]{3,1,2,0:T(8,128)S(1)} %select_maximum_fusion.6, f32[2,20,32,128]{3,1,2,0:T(8,128)} %get-tuple-element.21, f32[2,20,32,128]{3,1,2,0:T(8,128)} %get-tuple-element.20), kind=kLoop, calls=%fused_computation.87 | loop fusion | flops 3932160 | bytes 13631488 | tf_op jit(solution)/shard_map/add | solution.py:49
  59.8 1.3 %fusion.15 = f32[16,32,128]{2,0,1:T(8,128)S(1)} fusion(f32[2,16,32,128]{3,1,2,0:T(8,128)} %fusion.35, f32[16,32,128]{2,0,1:T(8,128)S(1)} %fusion.13, f32[1,16,32,128]{3,2,1,0:T(8,128)S(1)} %copy-done.5, f32[16,16]{0,1:T(8,128)S(1)} %get-tuple-element.47, f32[16,32]{0,1:T(8,128)S(1)} %convert_bitcast_fusion, f32[32]{0:T(128)S(1)} %compare_convert_fusion, ...), kind=kOutput, calls=%fused_computation.39 | convolution fusion | flops 13182976 | bytes 1313988 | tf_op jit(solution)/shard_map/xs,ys,zs->xyz/dot_general | solution.py:57
  61.2 1.6 %fusion.8 = f32[16,32,128]{2,0,1:T(8,128)S(1)} fusion(f32[16,32,128]{2,0,1:T(8,128)S(1)} %fusion.7, f32[2,16,32,128]{3,1,2,0:T(8,128)} %fusion.35, f32[1,16,32,128]{3,2,1,0:T(8,128)} %param.15, f32[32]{0:T(128)S(1)} %compare_convert_fusion, f32[4,16]{1,0:T(4,128)S(1)} %copy-done.10, f32[4,32]{0,1:T(8,128)S(1)} %convert_bitcast_fusion.1, ...), kind=kOutput, calls=%fused_computation.28 | convolution fusion | flops 3738112 | bytes 1311636 | tf_op jit(solution)/shard_map/xs,ys,zs->xyz/dot_general | solution.py:57
  62.8 2.1 %collective-permute-start.10 = (f32[2,4,32,128]{3,1,2,0:T(4,128)S(1)}, f32[2,4,32,128]{3,1,2,0:T(4,128)S(1)}, u32[]{:S(2)}, u32[]{:S(2)}) collective-permute-start(f32[2,4,32,128]{3,1,2,0:T(4,128)S(1)} %get-tuple-element.19), channel_id=1, source_target_pairs={{1,0},{2,1},{3,2},{5,4},{6,5},{7,6},{9,8},{10,9},{11,10},{13,12},{... | collective-permute-start | bytes 393224 | tf_op jit(solution)/shard_map/ppermute | solution.py:29
  64.9 1.5 %collective-permute-start.11 = (f32[2,4,32,128]{3,1,2,0:T(4,128)S(1)}, f32[2,4,32,128]{3,1,2,0:T(4,128)S(1)}, u32[]{:S(2)}, u32[]{:S(2)}) collective-permute-start(f32[2,4,32,128]{3,1,2,0:T(4,128)S(1)} %get-tuple-element.18), channel_id=1, source_target_pairs={{0,1},{1,2},{2,3},{4,5},{5,6},{6,7},{8,9},{9,10},{10,11},{12,13},{... | collective-permute-start | bytes 393224 | tf_op jit(solution)/shard_map/ppermute | solution.py:27
  66.4 0.4 collective-permute-done.10
  66.9 3.8 %collective-permute-done.11 = f32[2,4,32,128]{3,1,2,0:T(4,128)S(1)} collective-permute-done((f32[2,4,32,128]{3,1,2,0:T(4,128)S(1)}, f32[2,4,32,128]{3,1,2,0:T(4,128)S(1)}, u32[]{:S(2)}, u32[]{:S(2)}) %collective-permute-start.11) | collective-permute-done | bytes 131104 | tf_op jit(solution)/shard_map/ppermute | solution.py:27
  70.6 1.3 %pad_maximum_fusion.2 = (f32[2,20,32,128]{3,1,2,0:T(8,128)}, f32[2,20,32,128]{3,1,2,0:T(8,128)}) fusion(f32[2,4,32,128]{3,1,2,0:T(4,128)S(1)} %collective-permute-done.10, f32[1,16,32,128]{3,1,2,0:T(8,128)S(1)} %bitcast.232, f32[1,16,32,128]{3,1,2,0:T(8,128)S(1)} %bitcast.244, f32[2,4,32,128]{3,1,2,0:T(4,128)S(1)} %collective-permute-done.11), kind=kLoop, calls=%fused_computation.49 | loop fusion | flops 655360 | bytes 2097152 | tf_op jit(solution)/shard_map/concatenate | solution.py:25
  72.0 0.7 select_maximum_fusion.3
  72.7 5.9 %fusion.30 = f32[2,16,32,128]{3,1,2,0:T(8,128)} fusion(f32[1,16,32,128]{3,1,2,0:T(8,128)S(1)} %bitcast.234, f32[1,16,32,128]{3,1,2,0:T(8,128)S(1)} %bitcast.246, f32[2,24,40,136]{3,1,2,0:T(8,128)S(1)} %select_maximum_fusion.3, f32[2,20,32,128]{3,1,2,0:T(8,128)} %get-tuple-element.17, f32[2,20,32,128]{3,1,2,0:T(8,128)} %get-tuple-element.16), kind=kLoop, calls=%fused_computation.82 | loop fusion | flops 3932160 | bytes 13631488 | tf_op jit(solution)/shard_map/add | solution.py:49
  78.7 1.3 %fusion.17 = f32[16,32,128]{2,0,1:T(8,128)S(1)} fusion(f32[2,16,32,128]{3,1,2,0:T(8,128)} %fusion.30, f32[16,32,128]{2,0,1:T(8,128)S(1)} %fusion.13, f32[16,32,128]{2,0,1:T(8,128)S(1)} %fusion.15, f32[16,16]{0,1:T(8,128)S(1)} %get-tuple-element.46, f32[16,32]{0,1:T(8,128)S(1)} %convert_bitcast_fusion, f32[32]{0:T(128)S(1)} %compare_convert_fusion, ...), kind=kOutput, calls=%fused_computation.41 | convolution fusion | flops 13117440 | bytes 1313988 | tf_op jit(solution)/shard_map/xs,ys,zs->xyz/dot_general | solution.py:57
  80.0 1.5 %fusion.9 = f32[16,32,128]{2,0,1:T(8,128)S(1)} fusion(f32[16,32,128]{2,0,1:T(8,128)S(1)} %fusion.7, f32[16,32,128]{2,0,1:T(8,128)S(1)} %fusion.8, f32[2,16,32,128]{3,1,2,0:T(8,128)} %fusion.30, f32[32]{0:T(128)S(1)} %compare_convert_fusion, f32[4,16]{1,0:T(4,128)S(1)} %copy-done.9, f32[4,32]{0,1:T(8,128)S(1)} %convert_bitcast_fusion.1, ...), kind=kOutput, calls=%fused_computation.29 | convolution fusion | flops 3672576 | bytes 1311636 | tf_op jit(solution)/shard_map/xs,ys,zs->xyz/dot_general | solution.py:57
  81.5 2.6 %collective-permute-start.12 = (f32[2,4,32,128]{3,1,2,0:T(4,128)S(1)}, f32[2,4,32,128]{3,1,2,0:T(4,128)S(1)}, u32[]{:S(2)}, u32[]{:S(2)}) collective-permute-start(f32[2,4,32,128]{3,1,2,0:T(4,128)S(1)} %get-tuple-element.15), channel_id=1, source_target_pairs={{1,0},{2,1},{3,2},{5,4},{6,5},{7,6},{9,8},{10,9},{11,10},{13,12},{... | collective-permute-start | bytes 393224 | tf_op jit(solution)/shard_map/ppermute | solution.py:29
  84.1 1.3 %collective-permute-start.13 = (f32[2,4,32,128]{3,1,2,0:T(4,128)S(1)}, f32[2,4,32,128]{3,1,2,0:T(4,128)S(1)}, u32[]{:S(2)}, u32[]{:S(2)}) collective-permute-start(f32[2,4,32,128]{3,1,2,0:T(4,128)S(1)} %get-tuple-element.14), channel_id=1, source_target_pairs={{0,1},{1,2},{2,3},{4,5},{5,6},{6,7},{8,9},{9,10},{10,11},{12,13},{... | collective-permute-start | bytes 393224 | tf_op jit(solution)/shard_map/ppermute | solution.py:27
  85.4 0.6 collective-permute-done.12
  86.0 3.8 %collective-permute-done.13 = f32[2,4,32,128]{3,1,2,0:T(4,128)S(1)} collective-permute-done((f32[2,4,32,128]{3,1,2,0:T(4,128)S(1)}, f32[2,4,32,128]{3,1,2,0:T(4,128)S(1)}, u32[]{:S(2)}, u32[]{:S(2)}) %collective-permute-start.13) | collective-permute-done | bytes 131104 | tf_op jit(solution)/shard_map/ppermute | solution.py:27
  89.8 1.3 %pad_maximum_fusion.3 = (f32[2,20,32,128]{3,1,2,0:T(8,128)}, f32[2,20,32,128]{3,1,2,0:T(8,128)}) fusion(f32[2,4,32,128]{3,1,2,0:T(4,128)S(1)} %collective-permute-done.12, f32[1,16,32,128]{3,1,2,0:T(8,128)S(1)} %bitcast.240, f32[1,16,32,128]{3,1,2,0:T(8,128)S(1)} %bitcast.252, f32[2,4,32,128]{3,1,2,0:T(4,128)S(1)} %collective-permute-done.13), kind=kLoop, calls=%fused_computation.51 | loop fusion | flops 655360 | bytes 2097152 | tf_op jit(solution)/shard_map/concatenate | solution.py:25
  91.1 0.7 select_maximum_fusion
  91.9 6.0 %fusion.25 = f32[2,16,32,128]{3,1,2,0:T(8,128)} fusion(f32[1,16,32,128]{3,1,2,0:T(8,128)S(1)} %bitcast.242, f32[1,16,32,128]{3,1,2,0:T(8,128)} %bitcast.254, f32[2,24,40,136]{3,1,2,0:T(8,128)S(1)} %select_maximum_fusion, f32[2,20,32,128]{3,1,2,0:T(8,128)} %get-tuple-element.13, f32[2,20,32,128]{3,1,2,0:T(8,128)} %get-tuple-element.12), kind=kLoop, calls=%fused_computation.77 | loop fusion | flops 3932160 | bytes 13631488 | tf_op jit(solution)/shard_map/add | solution.py:49
  97.9 1.6 %multiply_add_fusion = f32[16,32,128]{2,0,1:T(8,128)S(1)} fusion(f32[16,32,128]{2,0,1:T(8,128)S(1)} %fusion.17, f32[16,32,128]{2,0,1:T(8,128)S(1)} %fusion.15, f32[16,32,128]{2,0,1:T(8,128)S(1)} %fusion.13, f32[2,16,32,128]{3,1,2,0:T(8,128)} %fusion.40, f32[2,16,32,128]{3,1,2,0:T(8,128)} %fusion.35, f32[2,16,32,128]{3,1,2,0:T(8,128)} %fusion.30, ...), kind=kLoop, calls=%fused_computation.217 | loop fusion | flops 851968 | bytes 2621572 | tf_op jit(solution)/shard_map/add | solution.py:104
  99.6 0.1 copy_dynamic-update-slice_fusion
  99.7 4.4 %collective-permute-start.14 = (f32[16,8,128]{2,1,0:T(8,128)S(1)}, f32[16,8,128]{2,1,0:T(8,128)S(1)}, u32[]{:S(2)}, u32[]{:S(2)}) collective-permute-start(f32[16,8,128]{2,1,0:T(8,128)S(1)} %get-tuple-element.28), channel_id=1, source_target_pairs={{12,0},{16,4},{20,8},{24,12},{28,16},{13,1},{17,5},{21,9},{25,13},... | collective-permute-start | bytes 196616 | tf_op jit(solution)/shard_map/ppermute | solution.py:16
  104.1 1.9 %collective-permute-start.15 = (f32[16,8,128]{2,1,0:T(8,128)S(1)}, f32[16,8,128]{2,1,0:T(8,128)S(1)}, u32[]{:S(2)}, u32[]{:S(2)}) collective-permute-start(f32[16,8,128]{2,1,0:T(8,128)S(1)} %get-tuple-element.33), channel_id=1, source_target_pairs={{8,0},{12,4},{16,8},{20,12},{24,16},{28,20},{9,1},{13,5},{17,9},{2... | collective-permute-start | bytes 196616 | tf_op jit(solution)/shard_map/ppermute | solution.py:16
  106.1 3.1 %collective-permute-start.16 = (f32[16,8,128]{2,1,0:T(8,128)S(1)}, f32[16,8,128]{2,1,0:T(8,128)S(1)}, u32[]{:S(2)}, u32[]{:S(2)}) collective-permute-start(f32[16,8,128]{2,1,0:T(8,128)S(1)} %get-tuple-element.32), channel_id=1, source_target_pairs={{4,0},{8,4},{12,8},{16,12},{20,16},{24,20},{28,24},{5,1},{9,5},{13... | collective-permute-start | bytes 196616 | tf_op jit(solution)/shard_map/ppermute | solution.py:16
  109.1 4.9 %collective-permute-start.17 = (f32[16,8,128]{2,1,0:T(8,128)S(1)}, f32[16,8,128]{2,1,0:T(8,128)S(1)}, u32[]{:S(2)}, u32[]{:S(2)}) collective-permute-start(f32[16,8,128]{2,1,0:T(8,128)S(1)} %get-tuple-element.31), channel_id=1, source_target_pairs={{0,4},{4,8},{8,12},{12,16},{16,20},{20,24},{24,28},{1,5},{5,9},{9,... | collective-permute-start | bytes 196616 | tf_op jit(solution)/shard_map/ppermute | solution.py:16
  114.1 3.6 %collective-permute-start.18 = (f32[16,8,128]{2,1,0:T(8,128)S(1)}, f32[16,8,128]{2,1,0:T(8,128)S(1)}, u32[]{:S(2)}, u32[]{:S(2)}) collective-permute-start(f32[16,8,128]{2,1,0:T(8,128)S(1)} %get-tuple-element.30), channel_id=1, source_target_pairs={{0,8},{4,12},{8,16},{12,20},{16,24},{20,28},{1,9},{5,13},{9,17},{1... | collective-permute-start | bytes 196616 | tf_op jit(solution)/shard_map/ppermute | solution.py:16
  117.8 0.3 fusion.20
  118.1 1.9 %collective-permute-start.19 = (f32[16,8,128]{2,1,0:T(8,128)S(1)}, f32[16,8,128]{2,1,0:T(8,128)S(1)}, u32[]{:S(2)}, u32[]{:S(2)}) collective-permute-start(f32[16,8,128]{2,1,0:T(8,128)S(1)} %get-tuple-element.29), channel_id=1, source_target_pairs={{0,12},{4,16},{8,20},{12,24},{16,28},{1,13},{5,17},{9,21},{13,25},... | collective-permute-start | bytes 196616 | tf_op jit(solution)/shard_map/ppermute | solution.py:16
  120.1 0.5 fusion.11
  120.6 0.8 copy.47
  121.3 0.8 copy.46
  122.2 1.5 %collective-permute-done.19 = f32[16,8,128]{2,1,0:T(8,128)S(1)} collective-permute-done((f32[16,8,128]{2,1,0:T(8,128)S(1)}, f32[16,8,128]{2,1,0:T(8,128)S(1)}, u32[]{:S(2)}, u32[]{:S(2)}) %collective-permute-start.19) | collective-permute-done | bytes 65568 | tf_op jit(solution)/shard_map/ppermute | solution.py:16
  123.7 0.7 fusion.96
  (50 shorter events, 0.4 us)
Async XLA Ops:
  0.6 27.2 %copy-start.8 = (f32[16,8,128]{2,1,0:T(8,128)S(1)}, f32[16,8,128]{2,1,0:T(8,128)}, u32[]{:S(2)}) copy-start(f32[16,8,128]{2,1,0:T(8,128)} %param.11) | copy-start | bytes 196612
  1.6 20.9 %collective-permute-start = (f32[16,8,128]{2,0,1:T(8,128)S(1)}, f32[16,8,128]{2,0,1:T(8,128)S(1)}, u32[]{:S(2)}, u32[]{:S(2)}) collective-permute-start(f32[16,8,128]{2,0,1:T(8,128)S(1)} %copy.33), channel_id=1, source_target_pairs={{0,12},{4,16},{8,20},{12,24},{16,28},{1,13},{5,17},{9,21},{13,25},... | collective-permute-start | bytes 196616 | tf_op jit(solution)/shard_map/ppermute | solution.py:16
  5.3 19.1 %collective-permute-start.1 = (f32[16,8,128]{2,0,1:T(8,128)S(1)}, f32[16,8,128]{2,0,1:T(8,128)S(1)}, u32[]{:S(2)}, u32[]{:S(2)}) collective-permute-start(f32[16,8,128]{2,0,1:T(8,128)S(1)} %copy.33), channel_id=1, source_target_pairs={{0,8},{4,12},{8,16},{12,20},{16,24},{20,28},{1,9},{5,13},{9,17},{1... | collective-permute-start | bytes 196616 | tf_op jit(solution)/shard_map/ppermute | solution.py:16
  7.2 19.3 %collective-permute-start.2 = (f32[16,8,128]{2,0,1:T(8,128)S(1)}, f32[16,8,128]{2,0,1:T(8,128)S(1)}, u32[]{:S(2)}, u32[]{:S(2)}) collective-permute-start(f32[16,8,128]{2,0,1:T(8,128)S(1)} %copy.33), channel_id=1, source_target_pairs={{0,4},{4,8},{8,12},{12,16},{16,20},{20,24},{24,28},{1,5},{5,9},{9,... | collective-permute-start | bytes 196616 | tf_op jit(solution)/shard_map/ppermute | solution.py:16
  10.0 17.9 %collective-permute-start.3 = (f32[16,8,128]{2,0,1:T(8,128)S(1)}, f32[16,8,128]{2,0,1:T(8,128)S(1)}, u32[]{:S(2)}, u32[]{:S(2)}) collective-permute-start(f32[16,8,128]{2,0,1:T(8,128)S(1)} %copy.33), channel_id=1, source_target_pairs={{4,0},{8,4},{12,8},{16,12},{20,16},{24,20},{28,24},{5,1},{9,5},{13... | collective-permute-start | bytes 196616 | tf_op jit(solution)/shard_map/ppermute | solution.py:16
  12.3 15.6 %collective-permute-start.4 = (f32[16,8,128]{2,0,1:T(8,128)S(1)}, f32[16,8,128]{2,0,1:T(8,128)S(1)}, u32[]{:S(2)}, u32[]{:S(2)}) collective-permute-start(f32[16,8,128]{2,0,1:T(8,128)S(1)} %copy.33), channel_id=1, source_target_pairs={{8,0},{12,4},{16,8},{20,12},{24,16},{28,20},{9,1},{13,5},{17,9},{2... | collective-permute-start | bytes 196616 | tf_op jit(solution)/shard_map/ppermute | solution.py:16
  21.6 12.9 %copy-start.4 = (f32[1,16,32,128]{3,1,2,0:T(8,128)}, f32[1,16,32,128]{3,1,2,0:T(8,128)S(1)}, u32[]{:S(2)}) copy-start(f32[1,16,32,128]{3,1,2,0:T(8,128)S(1)} %get-tuple-element.54) | copy-start | bytes 786436
  22.5 5.9 %collective-permute-start.5 = (f32[16,8,128]{2,0,1:T(8,128)S(1)}, f32[16,8,128]{2,0,1:T(8,128)S(1)}, u32[]{:S(2)}, u32[]{:S(2)}) collective-permute-start(f32[16,8,128]{2,0,1:T(8,128)S(1)} %copy.33), channel_id=1, source_target_pairs={{12,0},{16,4},{20,8},{24,12},{28,16},{13,1},{17,5},{21,9},{25,13},... | collective-permute-start | bytes 196616 | tf_op jit(solution)/shard_map/ppermute | solution.py:16
  24.4 5.2 %collective-permute-start.6 = (f32[2,4,32,128]{3,1,2,0:T(4,128)S(1)}, f32[2,4,32,128]{3,1,2,0:T(4,128)S(1)}, u32[]{:S(2)}, u32[]{:S(2)}) collective-permute-start(f32[2,4,32,128]{3,1,2,0:T(4,128)S(1)} %get-tuple-element.27), channel_id=1, source_target_pairs={{1,0},{2,1},{3,2},{5,4},{6,5},{7,6},{9,8},{10,9},{11,10},{13,12},{... | collective-permute-start | bytes 393224 | tf_op jit(solution)/shard_map/ppermute | solution.py:29
  26.5 7.0 %collective-permute-start.7 = (f32[2,4,32,128]{3,1,2,0:T(4,128)S(1)}, f32[2,4,32,128]{3,1,2,0:T(4,128)S(1)}, u32[]{:S(2)}, u32[]{:S(2)}) collective-permute-start(f32[2,4,32,128]{3,1,2,0:T(4,128)S(1)} %get-tuple-element.26), channel_id=1, source_target_pairs={{0,1},{1,2},{2,3},{4,5},{5,6},{6,7},{8,9},{9,10},{10,11},{12,13},{... | collective-permute-start | bytes 393224 | tf_op jit(solution)/shard_map/ppermute | solution.py:27
  28.4 51.6 %copy-start = (f32[16,56,128]{2,0,1:T(8,128)}, f32[16,56,128]{2,0,1:T(8,128)S(1)}, u32[]{:S(2)}) copy-start(f32[16,56,128]{2,0,1:T(8,128)S(1)} %constant_dynamic-update-slice_fusion) | copy-start | bytes 1376260
  44.0 4.0 %collective-permute-start.8 = (f32[2,4,32,128]{3,1,2,0:T(4,128)S(1)}, f32[2,4,32,128]{3,1,2,0:T(4,128)S(1)}, u32[]{:S(2)}, u32[]{:S(2)}) collective-permute-start(f32[2,4,32,128]{3,1,2,0:T(4,128)S(1)} %get-tuple-element.23), channel_id=1, source_target_pairs={{1,0},{2,1},{3,2},{5,4},{6,5},{7,6},{9,8},{10,9},{11,10},{13,12},{... | collective-permute-start | bytes 393224 | tf_op jit(solution)/shard_map/ppermute | solution.py:29
  46.1 5.7 %collective-permute-start.9 = (f32[2,4,32,128]{3,1,2,0:T(4,128)S(1)}, f32[2,4,32,128]{3,1,2,0:T(4,128)S(1)}, u32[]{:S(2)}, u32[]{:S(2)}) collective-permute-start(f32[2,4,32,128]{3,1,2,0:T(4,128)S(1)} %get-tuple-element.22), channel_id=1, source_target_pairs={{0,1},{1,2},{2,3},{4,5},{5,6},{6,7},{8,9},{9,10},{10,11},{12,13},{... | collective-permute-start | bytes 393224 | tf_op jit(solution)/shard_map/ppermute | solution.py:27
  53.9 6.0 %copy-start.5 = (f32[1,16,32,128]{3,2,1,0:T(8,128)S(1)}, f32[1,16,32,128]{3,2,1,0:T(8,128)}, u32[]{:S(2)}) copy-start(f32[1,16,32,128]{3,2,1,0:T(8,128)} %param.17) | copy-start | bytes 786436
  53.9 7.3 %copy-start.10 = (f32[4,16]{1,0:T(4,128)S(1)}, f32[4,16]{1,0:T(4,128)}, u32[]{:S(2)}) copy-start(f32[4,16]{1,0:T(4,128)} %get-tuple-element.51) | copy-start | bytes 772
  62.8 4.0 %collective-permute-start.10 = (f32[2,4,32,128]{3,1,2,0:T(4,128)S(1)}, f32[2,4,32,128]{3,1,2,0:T(4,128)S(1)}, u32[]{:S(2)}, u32[]{:S(2)}) collective-permute-start(f32[2,4,32,128]{3,1,2,0:T(4,128)S(1)} %get-tuple-element.19), channel_id=1, source_target_pairs={{1,0},{2,1},{3,2},{5,4},{6,5},{7,6},{9,8},{10,9},{11,10},{13,12},{... | collective-permute-start | bytes 393224 | tf_op jit(solution)/shard_map/ppermute | solution.py:29
  64.9 5.7 %collective-permute-start.11 = (f32[2,4,32,128]{3,1,2,0:T(4,128)S(1)}, f32[2,4,32,128]{3,1,2,0:T(4,128)S(1)}, u32[]{:S(2)}, u32[]{:S(2)}) collective-permute-start(f32[2,4,32,128]{3,1,2,0:T(4,128)S(1)} %get-tuple-element.18), channel_id=1, source_target_pairs={{0,1},{1,2},{2,3},{4,5},{5,6},{6,7},{8,9},{9,10},{10,11},{12,13},{... | collective-permute-start | bytes 393224 | tf_op jit(solution)/shard_map/ppermute | solution.py:27
  72.7 7.2 %copy-start.9 = (f32[4,16]{1,0:T(4,128)S(1)}, f32[4,16]{1,0:T(4,128)}, u32[]{:S(2)}) copy-start(f32[4,16]{1,0:T(4,128)} %get-tuple-element.50) | copy-start | bytes 772
  81.4 10.4 %copy-start.2 = (f32[16,32,128]{2,0,1:T(8,128)}, f32[16,32,128]{2,0,1:T(8,128)S(1)}, u32[]{:S(2)}) copy-start(f32[16,32,128]{2,0,1:T(8,128)S(1)} %fusion.9) | copy-start | bytes 786436
  81.5 4.5 %collective-permute-start.12 = (f32[2,4,32,128]{3,1,2,0:T(4,128)S(1)}, f32[2,4,32,128]{3,1,2,0:T(4,128)S(1)}, u32[]{:S(2)}, u32[]{:S(2)}) collective-permute-start(f32[2,4,32,128]{3,1,2,0:T(4,128)S(1)} %get-tuple-element.15), channel_id=1, source_target_pairs={{1,0},{2,1},{3,2},{5,4},{6,5},{7,6},{9,8},{10,9},{11,10},{13,12},{... | collective-permute-start | bytes 393224 | tf_op jit(solution)/shard_map/ppermute | solution.py:29
  84.1 5.7 %collective-permute-start.13 = (f32[2,4,32,128]{3,1,2,0:T(4,128)S(1)}, f32[2,4,32,128]{3,1,2,0:T(4,128)S(1)}, u32[]{:S(2)}, u32[]{:S(2)}) collective-permute-start(f32[2,4,32,128]{3,1,2,0:T(4,128)S(1)} %get-tuple-element.14), channel_id=1, source_target_pairs={{0,1},{1,2},{2,3},{4,5},{5,6},{6,7},{8,9},{9,10},{10,11},{12,13},{... | collective-permute-start | bytes 393224 | tf_op jit(solution)/shard_map/ppermute | solution.py:27
  91.9 6.0 %copy-start.6 = (f32[1,16,32,128]{3,2,1,0:T(8,128)S(1)}, f32[1,16,32,128]{3,2,1,0:T(8,128)}, u32[]{:S(2)}) copy-start(f32[1,16,32,128]{3,2,1,0:T(8,128)} %param.17) | copy-start | bytes 786436
  97.9 19.9 %copy-start.1 = (f32[16,56,128]{2,0,1:T(8,128)S(1)}, f32[16,56,128]{2,0,1:T(8,128)}, u32[]{:S(2)}) copy-start(f32[16,56,128]{2,0,1:T(8,128)} %copy-done) | copy-start | bytes 1376260
  97.9 19.9 %copy-start.7 = (f32[2,16,32,128]{3,1,2,0:T(8,128)S(1)}, f32[2,16,32,128]{3,1,2,0:T(8,128)}, u32[]{:S(2)}) copy-start(f32[2,16,32,128]{3,1,2,0:T(8,128)} %fusion.25) | copy-start | bytes 1572868
  99.5 20.5 %copy-start.3 = (f32[16,32,128]{2,0,1:T(8,128)S(1)}, f32[16,32,128]{2,0,1:T(8,128)}, u32[]{:S(2)}) copy-start(f32[16,32,128]{2,0,1:T(8,128)} %copy-done.2) | copy-start | bytes 786436
  99.7 18.4 %collective-permute-start.14 = (f32[16,8,128]{2,1,0:T(8,128)S(1)}, f32[16,8,128]{2,1,0:T(8,128)S(1)}, u32[]{:S(2)}, u32[]{:S(2)}) collective-permute-start(f32[16,8,128]{2,1,0:T(8,128)S(1)} %get-tuple-element.28), channel_id=1, source_target_pairs={{12,0},{16,4},{20,8},{24,12},{28,16},{13,1},{17,5},{21,9},{25,13},... | collective-permute-start | bytes 196616 | tf_op jit(solution)/shard_map/ppermute | solution.py:16
  104.1 18.0 %collective-permute-start.15 = (f32[16,8,128]{2,1,0:T(8,128)S(1)}, f32[16,8,128]{2,1,0:T(8,128)S(1)}, u32[]{:S(2)}, u32[]{:S(2)}) collective-permute-start(f32[16,8,128]{2,1,0:T(8,128)S(1)} %get-tuple-element.33), channel_id=1, source_target_pairs={{8,0},{12,4},{16,8},{20,12},{24,16},{28,20},{9,1},{13,5},{17,9},{2... | collective-permute-start | bytes 196616 | tf_op jit(solution)/shard_map/ppermute | solution.py:16
  106.1 16.1 %collective-permute-start.16 = (f32[16,8,128]{2,1,0:T(8,128)S(1)}, f32[16,8,128]{2,1,0:T(8,128)S(1)}, u32[]{:S(2)}, u32[]{:S(2)}) collective-permute-start(f32[16,8,128]{2,1,0:T(8,128)S(1)} %get-tuple-element.32), channel_id=1, source_target_pairs={{4,0},{8,4},{12,8},{16,12},{20,16},{24,20},{28,24},{5,1},{9,5},{13... | collective-permute-start | bytes 196616 | tf_op jit(solution)/shard_map/ppermute | solution.py:16
  109.1 13.0 %collective-permute-start.17 = (f32[16,8,128]{2,1,0:T(8,128)S(1)}, f32[16,8,128]{2,1,0:T(8,128)S(1)}, u32[]{:S(2)}, u32[]{:S(2)}) collective-permute-start(f32[16,8,128]{2,1,0:T(8,128)S(1)} %get-tuple-element.31), channel_id=1, source_target_pairs={{0,4},{4,8},{8,12},{12,16},{16,20},{20,24},{24,28},{1,5},{5,9},{9,... | collective-permute-start | bytes 196616 | tf_op jit(solution)/shard_map/ppermute | solution.py:16
  114.1 8.0 %collective-permute-start.18 = (f32[16,8,128]{2,1,0:T(8,128)S(1)}, f32[16,8,128]{2,1,0:T(8,128)S(1)}, u32[]{:S(2)}, u32[]{:S(2)}) collective-permute-start(f32[16,8,128]{2,1,0:T(8,128)S(1)} %get-tuple-element.30), channel_id=1, source_target_pairs={{0,8},{4,12},{8,16},{12,20},{16,24},{20,28},{1,9},{5,13},{9,17},{1... | collective-permute-start | bytes 196616 | tf_op jit(solution)/shard_map/ppermute | solution.py:16
  118.1 5.6 %collective-permute-start.19 = (f32[16,8,128]{2,1,0:T(8,128)S(1)}, f32[16,8,128]{2,1,0:T(8,128)S(1)}, u32[]{:S(2)}, u32[]{:S(2)}) collective-permute-start(f32[16,8,128]{2,1,0:T(8,128)S(1)} %get-tuple-element.29), channel_id=1, source_target_pairs={{0,12},{4,16},{8,20},{12,24},{16,28},{1,13},{5,17},{9,21},{13,25},... | collective-permute-start | bytes 196616 | tf_op jit(solution)/shard_map/ppermute | solution.py:16
where the time goes:
time: 125 us; the launch traced here: 124 us
  starting transfers between devices  50 us (40%)
  other arithmetic  35.6 us (28%)
  waiting for transfers between devices  20.2 us (16%)
  matrix products  9.95 us (8%)
  local copies, waits for them, and re-layouts  6.1 us (5%)
  between operations  2.52 us (2%)
    ppermute x12, starting transfers between devices, passed_along(): return lax.ppermute(block, axis, route)  35.9 us
    add x4, other arithmetic, stencil(): total = total + stencil_weights[k] * near  23 us
    ppermute x4, waiting for transfers between devices, padded_2(): lax.ppermute(tail, axis, [(i, (i + 1) % count) for i in range(ends)])  15.3 us
    dot_general x8, matrix products, inject(): jnp.einsum('xs,ys,zs->xyz', along_x, along_y, along_z, precision=lax.Prec...  9.95 us
    ppermute x4, starting transfers between devices, padded_2(): lax.ppermute(head, axis, [((i + 1) % count, i) for i in range(ends)])  8.82 us
    concatenate x8, other arithmetic, padded_2(): jnp.concatenate([lax.ppermute(tail, axis, [(i, (i + 1) % count) for i in...  7.96 us
    ppermute x4, starting transfers between devices, padded_2(): lax.ppermute(tail, axis, [(i, (i + 1) % count) for i in range(ends)])  5.35 us
    unnamed x33, local copies, waits for them, and re-layouts  4.04 us
  transfers between devices with their start and end apart: 20, of which 10 were waited for; matrix products, arithmetic and copies ran while one was open for 6% of the time, Pallas kernels for 0%

commit v1 on v0

v1 whole, which is shorter than its diff:
```python
import jax
import jax.numpy as jnp
import numpy as np
from jax import lax
from jax.experimental import pallas as pl
from jax.experimental.pallas import tpu as pltpu
from jax.sharding import PartitionSpec as P


SCALE = 5040.0
scaled_weights = (-14350.0, 8064.0, -1008.0, 128.0, -9.0)
time_step = 0.09
REACH = 4
TILE = 8


def swap_pairs(block, axis, first):
    count = lax.axis_size(axis)
    route = []
    for i in range(first, count - 1, 2):
        route += [(i, i + 1), (i + 1, i)]
    return lax.ppermute(block, axis, route)


def any_space():
    return pl.BlockSpec(memory_space=pl.ANY)


def in_hbm(array):
    return pltpu.with_memory_space_constraint(array, pltpu.HBM)


def packing_kernel(now_w, now_j, prev_w, prev_j, to_a, to_b, sems):
    cells = now_w.shape[1]
    deep_now = (to_a.shape[0] // 2 + REACH) // 2
    deep_prev = deep_now - REACH
    odd = lax.axis_index("slab") % 2
    copies = []
    for out, side in ((to_a, 1 - odd), (to_b, odd)):
        at = 0
        for field, deep in ((now_w, deep_now), (now_j, deep_now), (prev_w, deep_prev), (prev_j, deep_prev)):
            source = field.at[0, pl.ds(side * (cells - deep), deep)]
            copies.append(pltpu.make_async_copy(source, out.at[pl.ds(at, deep)], sems.at[len(copies)]))
            at += deep
    for copy in copies:
        copy.start()
    for copy in copies:
        copy.wait()


def pack(now_w, now_j, prev_w, prev_j, deep):
    rows, depth = now_w.shape[2:]
    out = pltpu.VMEM((4 * deep - 2 * REACH, rows, depth), jnp.float32)
    return pl.pallas_call(
        packing_kernel,
        out_shape=(out, out),
        in_specs=[pl.BlockSpec(memory_space=pltpu.HBM)] * 4,
        out_specs=(any_space(), any_space()),
        scratch_shapes=[pltpu.SemaphoreType.DMA((8,))],
        compiler_params=pltpu.CompilerParams(vmem_limit_bytes=1 << 20),
        cost_estimate=pl.CostEstimate(flops=0, bytes_accessed=4 << 20, transcendentals=0),
    )(*map(in_hbm, (now_w, now_j, prev_w, prev_j)))


def window_kernel(start, cells_w, cells_j, amps_w, amps_j, speeds, to_a, to_b, drops, sems):
    cells = speeds.shape[1]
    tiles, deep_prev = to_a.shape[:2]
    wide, depth = drops.shape[2], drops.shape[4]
    deep = deep_prev + REACH
    slab = lax.axis_index("slab")
    odd = slab % 2
    steps = amps_w.shape[1]
    start_block = start[0]
    copies = []
    for out, side in ((to_a, 1 - odd), (to_b, odd)):
        for tile in range(tiles):
            source = speeds.at[start_block + tile, pl.ds(side * (cells - deep_prev), deep_prev)]
            copies.append(pltpu.make_async_copy(source, out.at[tile], sems.at[len(copies)]))
    for copy in copies:
        copy.start()

    def clear(x, carry):
        for step in range(steps):
            for field in range(2):
                drops[step, field, x] = jnp.zeros((TILE, depth), jnp.float32)
        return carry

    lax.fori_loop(0, wide, clear, 0)
    row = lax.broadcasted_iota(jnp.int32, (TILE, depth), 0)
    col = lax.broadcasted_iota(jnp.int32, (TILE, depth), 1)

    def inject(field, places, amps):
        def one_cell(s, carry):
            x = places[0, 0, s] - (slab * cells - deep)

            @pl.when((x >= 0) & (x < wide))
            def _():
                here = (row == places[1, 0, s]) & (col == places[2, 0, s])
                for step in range(steps):
                    drops[step, field, x] = drops[step, field, x] + jnp.where(here, amps[0, step, s], 0.0)

            return carry

        lax.fori_loop(0, places.shape[2], one_cell, 0)

    inject(0, cells_w, amps_w)
    inject(1, cells_j, amps_j)
    for copy in copies:
        copy.wait()


def cut_window(start, cells_w, cells_j, amps_w, amps_j, speeds, tiles):
    cells, depth = speeds.shape[1], speeds.shape[3]
    steps = amps_w.shape[1]
    deep = steps * REACH
    out = pltpu.VMEM((tiles, deep - REACH, TILE, depth), jnp.float32)
    smem = pl.BlockSpec(memory_space=pltpu.SMEM)
    return pl.pallas_call(
        window_kernel,
        out_shape=(out, out, pltpu.VMEM((steps, 2, cells + 2 * deep, TILE, depth), jnp.float32)),
        in_specs=[smem] * 5 + [any_space()],
        out_specs=(any_space(), any_space(), pl.BlockSpec(memory_space=pltpu.VMEM)),
        scratch_shapes=[pltpu.SemaphoreType.DMA((2 * tiles,))],
        compiler_params=pltpu.CompilerParams(vmem_limit_bytes=8 << 20),
        cost_estimate=pl.CostEstimate(flops=1 << 20, bytes_accessed=2 << 20, transcendentals=0),
    )(start, cells_w, cells_j, amps_w, amps_j, in_hbm(speeds))


def steps_kernel(
    steps,
    start,
    count,
    now_w,
    now_j,
    prev_w,
    prev_j,
    from_a,
    from_b,
    speeds,
    speed_a,
    speed_b,
    drops,
    band,
    final_w,
    final_j,
    parts,
    one,
    two,
    model,
    grad,
    sems,
):
    cells, rows, depth = now_w.shape[1:]
    deep = steps * REACH
    deep_prev = deep - REACH
    wide = cells + 2 * deep
    tiles = rows // TILE
    odd = lax.axis_index("slab") % 2
    start_block = start[0]
    live = count[0]

    left_of_a = odd
    copies = []

    def bring(source, target):
        copy = pltpu.make_async_copy(source, target, sems.at[len(copies)])
        copy.start()
        copies.append(copy)

    inner = pl.ds(TILE, rows)
    for field, (now, prev) in enumerate(((now_w, prev_w), (now_j, prev_j))):
        bring(now.at[0], one.at[field, pl.ds(deep, cells), inner])
        bring(prev.at[0], two.at[field, pl.ds(deep, cells), inner])
        for buffer, on_left in ((from_a, left_of_a), (from_b, 1 - left_of_a)):
            at = (1 - on_left) * (deep + cells)
            bring(buffer.at[pl.ds(field * deep, deep)], one.at[field, pl.ds(at, deep), inner])
            at = on_left * REACH + (1 - on_left) * (deep + cells)
            bring(
                buffer.at[pl.ds(2 * deep + field * deep_prev, deep_prev)],
                two.at[field, pl.ds(at, deep_prev), inner],
            )
    for tile in range(tiles):
        bring(speeds.at[start_block + tile], model.at[tile, pl.ds(deep, cells)])
        for buffer, on_left in ((speed_a, left_of_a), (speed_b, 1 - left_of_a)):
            at = on_left * REACH + (1 - on_left) * (deep + cells)
            bring(buffer.at[tile], model.at[tile, pl.ds(at, deep_prev)])

    zero_tile = jnp.zeros((TILE, depth), jnp.float32)

    def clear_edges(x, carry):
        for buffer in (one, two):
            for field in range(2):
                buffer[field, x, pl.ds(0, TILE), :] = zero_tile
                buffer[field, x, pl.ds(TILE + rows, TILE), :] = zero_tile
        return carry

    lax.fori_loop(0, wide, clear_edges, 0)

    def clear_parts(b, carry):
        parts[b] = jnp.zeros(parts.shape[1:], jnp.float32)
        return carry

    lax.fori_loop(0, parts.shape[0], clear_parts, 0)

    for copy in copies:
        copy.wait()

    for tile in range(1, tiles):

        @pl.when(tile >= live)
        def _():
            def clear(x, carry):
                for buffer in (one, two):
                    for field in range(2):
                        buffer[field, x, pl.ds(TILE + tile * TILE, TILE), :] = zero_tile
                model[tile, x] = zero_tile
                return carry

            lax.fori_loop(0, wide, clear, 0)

    group = REACH

    def along_z(now, x):
        fields = [now[field, pl.ds(x, group), inner, :].reshape(group * rows, depth) for field in range(2)]
        cells_in = jnp.concatenate(fields, axis=0)
        high = cells_in.astype(jnp.bfloat16)
        low = (cells_in - high.astype(jnp.float32)).astype(jnp.bfloat16)
        return jnp.dot(
            jnp.concatenate([high, low], axis=1), band[...], preferred_element_type=jnp.float32
        )

    def advance(now, other, step, x_first, imaged):
        spread = along_z(now, x_first)
        for i in range(group):
            x = x_first + i
            speed = jnp.concatenate([model[tile, x] for tile in range(tiles)], axis=0)
            courant = speed * speed * (time_step * time_step / SCALE)
            pair = []
            for field in range(2):
                center = now[field, x, inner, :]
                lap = (3.0 * scaled_weights[0]) * center
                for k in range(1, REACH + 1):
                    near = now[field, x + k, inner, :] + now[field, x - k, inner, :]
                    near = near + now[field, x, pl.ds(TILE + k, rows), :]
                    near = near + now[field, x, pl.ds(TILE - k, rows), :]
                    lap = lap + scaled_weights[k] * near
                at = (field * group + i) * rows
                lap = lap + spread[at : at + rows]
                pair.append((center, lap))
                ahead = 2.0 * center - other[field, x, inner, :] + courant * lap
                other[field, x, pl.ds(TILE, TILE), :] = ahead[:TILE] + drops[step, field, x]
                other[field, x, pl.ds(2 * TILE, rows - TILE), :] = ahead[TILE:]
            if imaged:
                term = pair[1][0] * pair[0][1]
                if step == 0:
                    grad[x - deep] = term
                else:
                    grad[x - deep] = grad[x - deep] + term

    now, other = one, two
    for step in range(steps):
        margin = REACH * (step + 1)
        half = (deep - margin) // group

        def outside(i, carry):
            advance(now, other, step, margin + i * group + jnp.where(i >= half, cells, 0), False)
            return carry

        def inside(i, carry):
            advance(now, other, step, deep + i * group, True)
            return carry

        if half:
            lax.fori_loop(0, 2 * half, outside, 0)
        lax.fori_loop(0, cells // group, inside, 0)
        now, other = other, now

    out = []
    for field, final in ((0, final_w), (1, final_j)):
        out.append(pltpu.make_async_copy(now.at[field, pl.ds(deep, cells), inner], final.at[0], sems.at[field]))
        out[-1].start()

    def place(x, carry):
        for tile in range(tiles):
            speed = model[tile, deep + x]
            piece = grad[x, pl.ds(tile * TILE, TILE), :]
            parts[start_block + tile, x] = (2.0 * time_step * time_step / SCALE) * speed * piece
        return carry

    lax.fori_loop(0, cells, place, 0)
    for copy in out:
        copy.wait()


def run_steps(steps, start, count, fields, from_a, from_b, speeds, speed_a, speed_b, drops, groups):
    now = fields[0]
    cells, rows, depth = now.shape[1:]
    deep = steps * REACH
    wide = cells + 2 * deep
    tiles = rows // TILE
    copies = 12 + 3 * tiles
    final = jax.ShapeDtypeStruct(now.shape, jnp.float32)
    away = np.abs(np.subtract.outer(np.arange(depth), np.arange(depth)))
    band = np.zeros((depth, depth), np.float32)
    for k in range(1, REACH + 1):
        band[away == k] = scaled_weights[k]
    band = jnp.asarray(np.concatenate([band, band], axis=0), jnp.bfloat16)

    def kernel(*refs):
        steps_kernel(steps, *refs)

    field_buffer = pltpu.VMEM((2, wide, rows + 2 * TILE, depth), jnp.float32)
    hbm = pl.BlockSpec(memory_space=pltpu.HBM)
    vmem = pl.BlockSpec(memory_space=pltpu.VMEM)
    return pl.pallas_call(
        kernel,
        out_shape=(final, final, jax.ShapeDtypeStruct((groups, cells, TILE, depth), jnp.float32)),
        in_specs=[pl.BlockSpec(memory_space=pltpu.SMEM)] * 2 + [hbm] * 4 + [any_space()] * 5 + [vmem, vmem],
        out_specs=(any_space(), any_space(), vmem),
        scratch_shapes=[
            field_buffer,
            field_buffer,
            pltpu.VMEM((tiles, wide, TILE, depth), jnp.float32),
            pltpu.VMEM((cells, rows, depth), jnp.float32),
            pltpu.SemaphoreType.DMA((copies,)),
        ],
        compiler_params=pltpu.CompilerParams(vmem_limit_bytes=24 << 20),
        cost_estimate=pl.CostEstimate(flops=40 << 20, bytes_accessed=6 << 20, transcendentals=0),
    )(start, count, *map(in_hbm, fields), from_a, from_b, in_hbm(speeds), speed_a, speed_b, drops, band)


def per_device(
    velocity,
    aperture_start,
    aperture_count,
    wave_prev,
    wave_now,
    adjoint_prev,
    adjoint_now,
    source_cells,
    wavelet,
    receiver_cells,
    trace,
):
    steps = wavelet.shape[1]
    deep = steps * REACH
    tiles = wave_now.shape[2] // TILE

    to_a, to_b = pack(wave_now, adjoint_now, wave_prev, adjoint_prev, deep)
    from_a = swap_pairs(to_a, "slab", 0)
    from_b = swap_pairs(to_b, "slab", 1)
    speeds = lax.all_gather(velocity, "shot")

    cells_w, cells_j = (jnp.transpose(places, (2, 0, 1)) for places in (source_cells, receiver_cells))
    to_a, to_b, drops = cut_window(aperture_start, cells_w, cells_j, wavelet, trace, speeds, tiles)
    speed_a = swap_pairs(to_a, "slab", 0)
    speed_b = swap_pairs(to_b, "slab", 1)
    fields = (wave_now, adjoint_now, wave_prev, adjoint_prev)
    groups = lax.axis_size("shot")
    final_w, final_j, parts = run_steps(
        steps, aperture_start, aperture_count, fields, from_a, from_b, speeds, speed_a, speed_b, drops, groups
    )
    shares = lax.all_to_all(parts, "shot", 0, 0, tiled=True)
    return final_w, final_j, jnp.sum(shares, axis=0)


def solution(mesh):
    return jax.shard_map(
        per_device,
        mesh=mesh,
        in_specs=(
            P("slab", "shot", None),
            P("shot"),
            P("shot"),
            P("shot", "slab", None, None),
            P("shot", "slab", None, None),
            P("shot", "slab", None, None),
            P("shot", "slab", None, None),
            P("shot", None, None),
            P("shot", None, None),
            P("shot", None, None),
            P("shot", None, None),
        ),
        out_specs=(
            P("shot", "slab", None, None),
            P("shot", "slab", None, None),
            P("slab", "shot", None),
        ),
        check_vma=False,
    )
```

time: 125 us -> 55.7 us (0.45)
  the two profiles are of different devices: /device:TPU:27 before, /device:TPU:8 now
where the time goes in v1:
time: 55.7 us; the launch traced here: 55 us
  blocking collectives  25.6 us (46%)
  Pallas kernels  12.1 us (22%)
  waiting for transfers between devices  7.49 us (13%)
  starting transfers between devices  7.11 us (13%)
  between operations  2.03 us (4%)
  other arithmetic  0.66 us (1%)
    all_to_all x1, blocking collectives, per_device(): shares = lax.all_to_all(parts, 'shot', 0, 0, tiled=True)  13.9 us
    all_gather x1, blocking collectives, per_device(): speeds = lax.all_gather(velocity, 'shot')  11.8 us
    pallas_call x1, Pallas kernels, run_steps(): pl.pallas_call(kernel, out_shape=(final, final, jax.ShapeDtypeStruct((gro...  8.89 us
    ppermute x4, waiting for transfers between devices, swap_pairs(): return lax.ppermute(block, axis, route)  7.49 us
    ppermute x4, starting transfers between devices, swap_pairs(): return lax.ppermute(block, axis, route)  7.11 us
    pallas_call x1, Pallas kernels, cut_window(): pl.pallas_call(window_kernel, out_shape=(out, out, pltpu.VMEM((steps, 2,...  1.69 us
    pallas_call x1, Pallas kernels, pack(): pl.pallas_call(packing_kernel, out_shape=(out, out), in_specs=[pl.BlockSp...  1.54 us
  transfers between devices with their start and end apart: 4, of which 2 were waited for; matrix products, arithmetic and copies ran while one was open for 0% of the time, Pallas kernels for 3%

profile of v1, /device:TPU:8, one launch (start us, length us, event | category | flops | bytes accessed | tf_op | source)
XLA Modules:
  0.0 55.0 jit_solution(13124850625286440679)
XLA Ops:
  0.6 0.0 copy-start
  0.6 0.0 copy-start.2
  0.7 0.0 copy-start.4
  0.7 0.0 copy-start.1
  0.7 0.0 copy-start.3
  0.7 1.5 %shard_map.139 = (f32[56,32,128]{2,1,0:T(8,128)S(1)}, f32[56,32,128]{2,1,0:T(8,128)S(1)}) custom-call(f32[1,16,32,128]{3,2,1,0:T(8,128)} %refs_2_.1, f32[1,16,32,128]{3,2,1,0:T(8,128)} %refs_3_.1, f32[1,16,32,128]{3,2,1,0:T(8,128)} %refs_4_.1, f32[1,16,32,128]{3,2,1,0:T(8,128)} %refs_5_.1), custom_call_target="tpu_custom_call" | custom-call | bytes 4194304 | tf_op jit(solution)/shard_map/pallas_call | solution.py:54
  2.2 0.1 collective-permute-start
  2.3 5.0 %collective-permute-start.1 = (f32[56,32,128]{2,1,0:T(8,128)S(1)}, f32[56,32,128]{2,1,0:T(8,128)S(1)}, u32[]{:S(2)}, u32[]{:S(2)}) collective-permute-start(f32[56,32,128]{2,1,0:T(8,128)S(1)} %get-tuple-element.12), channel_id=1, source_target_pairs={{1,2},{2,1},{5,6},{6,5},{9,10},{10,9},{13,14},{14,13},{17,18},{18,... | collective-permute-start | bytes 2752520 | tf_op jit(solution)/shard_map/ppermute | solution.py:22
  8.0 11.8 %all-gather = f32[128,8,128]{2,1,0:T(8,128)} all-gather(f32[16,8,128]{2,1,0:T(8,128)} %param.12), channel_id=2, replica_groups=mesh['shot'=8,'slab'=4] {'shot'}, dimensions={0}, use_global_device_ids=true | all-gather | bytes 589824 | tf_op jit(solution)/shard_map/all_gather | solution.py:352
  19.8 0.0 copy-done.2
  19.8 0.0 copy-done.4
  19.8 0.0 copy-done.1
  19.8 0.0 copy-done.3
  19.8 1.7 %shard_map.140 = (f32[4,12,8,128]{3,2,1,0:T(8,128)S(1)}, f32[4,12,8,128]{3,2,1,0:T(8,128)S(1)}, f32[4,2,48,8,128]{4,3,2,1,0:T(8,128)S(1)}) custom-call(s32[1]{0:T(128)S(6)} %copy.15.start.refs_0_, s32[3,1,4]{2,1,0:T(1,128)S(1)} %bitcast.3, s32[3,1,16]{2,1,0:T(1,128)S(1)} %bitcast.4, f32[1,4,4]{2,1,0:T(4,128)S(1)} %copy-done.1, f32[1,4,16]{2,1,0:T(4,128)S(1)} %copy-done.2, ...), custom_call_target="tpu_custom_call" | custom-call | flops 1048576 | bytes 2097152 | tf_op jit(solution)/shard_map/pallas_call | solution.py:118
  21.5 0.1 collective-permute-start.2
  21.6 1.9 %collective-permute-start.3 = (f32[4,12,8,128]{3,2,1,0:T(8,128)S(1)}, f32[4,12,8,128]{3,2,1,0:T(8,128)S(1)}, u32[]{:S(2)}, u32[]{:S(2)}) collective-permute-start(f32[4,12,8,128]{3,2,1,0:T(8,128)S(1)} %get-tuple-element.14), channel_id=1, source_target_pairs={{1,2},{2,1},{5,6},{6,5},{9,10},{10,9},{13,14},{14,13},{17,18},{18,... | collective-permute-start | bytes 589832 | tf_op jit(solution)/shard_map/ppermute | solution.py:22
  24.1 4.6 %collective-permute-done.2.refs_9_ = f32[4,12,8,128]{3,2,1,0:T(8,128)S(1)} collective-permute-done((f32[4,12,8,128]{3,2,1,0:T(8,128)S(1)}, f32[4,12,8,128]{3,2,1,0:T(8,128)S(1)}, u32[]{:S(2)}, u32[]{:S(2)}) %collective-permute-start.2) | collective-permute-done | bytes 196640 | tf_op jit(solution)/shard_map/ppermute | solution.py:22
  28.7 2.9 %collective-permute-done.3.refs_10_ = f32[4,12,8,128]{3,2,1,0:T(8,128)S(1)} collective-permute-done((f32[4,12,8,128]{3,2,1,0:T(8,128)S(1)}, f32[4,12,8,128]{3,2,1,0:T(8,128)S(1)}, u32[]{:S(2)}, u32[]{:S(2)}) %collective-permute-start.3) | collective-permute-done | bytes 196640 | tf_op jit(solution)/shard_map/ppermute | solution.py:22
  31.6 0.0 collective-permute-done.refs_6_
  31.6 0.0 collective-permute-done.1.refs_7_
  31.6 0.0 copy-done
  31.6 8.9 %shard_map.141 = (f32[1,16,32,128]{3,2,1,0:T(8,128)}, f32[1,16,32,128]{3,2,1,0:T(8,128)}, f32[8,16,8,128]{3,2,1,0:T(8,128)S(1)}) custom-call(s32[1]{0:T(128)S(6)} %copy.15.start.refs_0_, s32[1]{0:T(128)S(6)} %copy.16.refs_1_, f32[1,16,32,128]{3,2,1,0:T(8,128)} %refs_2_.1, f32[1,16,32,128]{3,2,1,0:T(8,128)} %refs_3_.1, f32[1,16,32,128]{3,2,1,0:T(8,128)} %refs_4_.1, ...), custom_call_target="tpu_custom_call" | custom-call | flops 41943040 | bytes 6291456 | tf_op jit(solution)/shard_map/pallas_call | solution.py:315
  40.5 13.9 %all_to_all.5 = f32[8,16,8,128]{3,2,1,0:T(8,128)S(1)} all-to-all(f32[8,16,8,128]{3,2,1,0:T(8,128)S(1)} %get-tuple-element.18), channel_id=1, replica_groups=mesh['shot'=8,'slab'=4] {'shot'}, dimensions={0} | all-to-all | bytes 1048576 | tf_op jit(solution)/shard_map/all_to_all | solution.py:363
  54.4 0.7 %reduce_sum.9 = f32[16,8,128]{2,1,0:T(8,128)} reduce(f32[8,16,8,128]{3,2,1,0:T(8,128)S(1)} %all_to_all.5, f32[]{:T(128)} %constant.1.clone.1), dimensions={0}, to_apply=%region_0.0 | reduce | flops 114688 | bytes 589828 | tf_op jit(solution)/shard_map/reduce_sum | solution.py:364
Async XLA Ops:
  0.6 31.0 %copy-start = (bf16[256,128]{1,0:T(8,128)(2,1)S(1)}, bf16[256,128]{1,0:T(8,128)(2,1)}, u32[]{:S(2)}) copy-start(bf16[256,128]{1,0:T(8,128)(2,1)} %constant.4.clone.refs_12_) | copy-start | bytes 196612
  0.6 19.1 %copy-start.2 = (f32[1,4,16]{2,1,0:T(4,128)S(1)}, f32[1,4,16]{2,1,0:T(4,128)}, u32[]{:S(2)}) copy-start(f32[1,4,16]{2,1,0:T(4,128)} %amps_j.1) | copy-start | bytes 772
  0.7 19.1 %copy-start.4 = (s32[1,16,3]{1,0,2:T(1,128)S(1)}, s32[1,16,3]{1,0,2:T(1,128)}, u32[]{:S(2)}) copy-start(s32[1,16,3]{1,0,2:T(1,128)} %param.21) | copy-start | bytes 580
  0.7 19.1 %copy-start.1 = (f32[1,4,4]{2,1,0:T(4,128)S(1)}, f32[1,4,4]{2,1,0:T(4,128)}, u32[]{:S(2)}) copy-start(f32[1,4,4]{2,1,0:T(4,128)} %amps_w.1) | copy-start | bytes 196
  0.7 19.1 %copy-start.3 = (s32[1,4,3]{1,0,2:T(1,128)S(1)}, s32[1,4,3]{1,0,2:T(1,128)}, u32[]{:S(2)}) copy-start(s32[1,4,3]{1,0,2:T(1,128)} %param.19) | copy-start | bytes 148
  2.2 29.4 %collective-permute-start = (f32[56,32,128]{2,1,0:T(8,128)S(1)}, f32[56,32,128]{2,1,0:T(8,128)S(1)}, u32[]{:S(2)}, u32[]{:S(2)}) collective-permute-start(f32[56,32,128]{2,1,0:T(8,128)S(1)} %get-tuple-element.11), channel_id=1, source_target_pairs={{0,1},{1,0},{2,3},{3,2},{4,5},{5,4},{6,7},{7,6},{8,9},{9,8},{10,11... | collective-permute-start | bytes 2752520 | tf_op jit(solution)/shard_map/ppermute | solution.py:22
  2.3 29.3 %collective-permute-start.1 = (f32[56,32,128]{2,1,0:T(8,128)S(1)}, f32[56,32,128]{2,1,0:T(8,128)S(1)}, u32[]{:S(2)}, u32[]{:S(2)}) collective-permute-start(f32[56,32,128]{2,1,0:T(8,128)S(1)} %get-tuple-element.12), channel_id=1, source_target_pairs={{1,2},{2,1},{5,6},{6,5},{9,10},{10,9},{13,14},{14,13},{17,18},{18,... | collective-permute-start | bytes 2752520 | tf_op jit(solution)/shard_map/ppermute | solution.py:22
  21.5 7.2 %collective-permute-start.2 = (f32[4,12,8,128]{3,2,1,0:T(8,128)S(1)}, f32[4,12,8,128]{3,2,1,0:T(8,128)S(1)}, u32[]{:S(2)}, u32[]{:S(2)}) collective-permute-start(f32[4,12,8,128]{3,2,1,0:T(8,128)S(1)} %get-tuple-element.13), channel_id=1, source_target_pairs={{0,1},{1,0},{2,3},{3,2},{4,5},{5,4},{6,7},{7,6},{8,9},{9,8},{10,11... | collective-permute-start | bytes 589832 | tf_op jit(solution)/shard_map/ppermute | solution.py:22
  21.6 10.1 %collective-permute-start.3 = (f32[4,12,8,128]{3,2,1,0:T(8,128)S(1)}, f32[4,12,8,128]{3,2,1,0:T(8,128)S(1)}, u32[]{:S(2)}, u32[]{:S(2)}) collective-permute-start(f32[4,12,8,128]{3,2,1,0:T(8,128)S(1)} %get-tuple-element.14), channel_id=1, source_target_pairs={{1,2},{2,1},{5,6},{6,5},{9,10},{10,9},{13,14},{14,13},{17,18},{18,... | collective-permute-start | bytes 589832 | tf_op jit(solution)/shard_map/ppermute | solution.py:22

commit v2 on v1

--- a/solution.py
+++ b/solution.py
@@ -126,7 +126,54 @@
     )(start, cells_w, cells_j, amps_w, amps_j, in_hbm(speeds))
 
 
-def steps_kernel(
+def along_z(now, band, x):
+    rows, depth = now.shape[2] - 2 * TILE, now.shape[3]
+    inner = pl.ds(TILE, rows)
+    fields = [now[field, pl.ds(x, REACH), inner, :].reshape(REACH * rows, depth) for field in range(2)]
+    cells = jnp.concatenate(fields, axis=0)
+    high = cells.astype(jnp.bfloat16)
+    low = (cells - high.astype(jnp.float32)).astype(jnp.bfloat16)
+    return jnp.dot(jnp.concatenate([high, low], axis=1), band[...], preferred_element_type=jnp.float32)
+
+
+def laplacian(now, spread, field, i, x):
+    rows = now.shape[2] - 2 * TILE
+    inner = pl.ds(TILE, rows)
+    center = now[field, x, inner, :]
+    lap = (3.0 * scaled_weights[0]) * center
+    for k in range(1, REACH + 1):
+        near = now[field, x + k, inner, :] + now[field, x - k, inner, :]
+        near = near + now[field, x, pl.ds(TILE + k, rows), :]
+        near = near + now[field, x, pl.ds(TILE - k, rows), :]
+        lap = lap + scaled_weights[k] * near
+    at = (field * REACH + i) * rows
+    return center, lap + spread[at : at + rows]
+
+
+def store_layer(buffer, field, x, values, drop):
+    rows = values.shape[0]
+    buffer[field, x, pl.ds(TILE, TILE), :] = values[:TILE] + drop
+    buffer[field, x, pl.ds(2 * TILE, rows - TILE), :] = values[TILE:]
+
+
+def advance(now, other, courant, drops, band, step, x_first, grad, fresh, deep):
+    rows = now.shape[2] - 2 * TILE
+    inner = pl.ds(TILE, rows)
+    spread = along_z(now, band, x_first)
+    for i in range(REACH):
+        x = x_first + i
+        pair = []
+        for field in range(2):
+            center, lap = laplacian(now, spread, field, i, x)
+            pair.append((center, lap))
+            ahead = 2.0 * center - other[field, x, inner, :] + courant[x] * lap
+            store_layer(other, field, x, ahead, drops[step, field, x])
+        if grad is not None:
+            term = pair[1][0] * pair[0][1]
+            grad[x - deep] = term if fresh else grad[x - deep] + term
+
+
+def early_kernel(
     steps,
     start,
     count,
@@ -137,17 +184,15 @@
     from_a,
     from_b,
     speeds,
-    speed_a,
-    speed_b,
     drops,
     band,
-    final_w,
-    final_j,
-    parts,
     one,
     two,
+    courant,
+    image,
+    grad,
+    waiting,
     model,
-    grad,
     sems,
 ):
     cells, rows, depth = now_w.shape[1:]
@@ -180,10 +225,7 @@
                 two.at[field, pl.ds(at, deep_prev), inner],
             )
     for tile in range(tiles):
-        bring(speeds.at[start_block + tile], model.at[tile, pl.ds(deep, cells)])
-        for buffer, on_left in ((speed_a, left_of_a), (speed_b, 1 - left_of_a)):
-            at = on_left * REACH + (1 - on_left) * (deep + cells)
-            bring(buffer.at[tile], model.at[tile, pl.ds(at, deep_prev)])
+        bring(speeds.at[start_block + tile], model.at[tile])
 
     zero_tile = jnp.zeros((TILE, depth), jnp.float32)
 
@@ -195,15 +237,19 @@
         return carry
 
     lax.fori_loop(0, wide, clear_edges, 0)
-
-    def clear_parts(b, carry):
-        parts[b] = jnp.zeros(parts.shape[1:], jnp.float32)
-        return carry
-
-    lax.fori_loop(0, parts.shape[0], clear_parts, 0)
-
     for copy in copies:
         copy.wait()
+
+    def factors(x, carry):
+        for tile in range(tiles):
+            alive = jnp.where(tile < live, time_step * time_step / SCALE, 0.0)
+            speed = model[tile, x]
+            at = pl.ds(tile * TILE, TILE)
+            courant[deep + x, at, :] = alive * (speed * speed)
+            image[x, at, :] = (2.0 * time_step * time_step / SCALE) * speed
+        return carry
+
+    lax.fori_loop(0, cells, factors, 0)
 
     for tile in range(1, tiles):
 
@@ -213,66 +259,105 @@
                 for buffer in (one, two):
                     for field in range(2):
                         buffer[field, x, pl.ds(TILE + tile * TILE, TILE), :] = zero_tile
-                model[tile, x] = zero_tile
                 return carry
 
             lax.fori_loop(0, wide, clear, 0)
 
-    group = REACH
-
-    def along_z(now, x):
-        fields = [now[field, pl.ds(x, group), inner, :].reshape(group * rows, depth) for field in range(2)]
-        cells_in = jnp.concatenate(fields, axis=0)
-        high = cells_in.astype(jnp.bfloat16)
-        low = (cells_in - high.astype(jnp.float32)).astype(jnp.bfloat16)
-        return jnp.dot(
-            jnp.concatenate([high, low], axis=1), band[...], preferred_element_type=jnp.float32
-        )
-
-    def advance(now, other, step, x_first, imaged):
-        spread = along_z(now, x_first)
-        for i in range(group):
+    half = deep_prev // REACH
+
+    def outside(c, carry):
+        x_first = REACH + c * REACH + jnp.where(c >= half, cells, 0)
+        spread = along_z(one, band, x_first)
+        for i in range(REACH):
             x = x_first + i
-            speed = jnp.concatenate([model[tile, x] for tile in range(tiles)], axis=0)
-            courant = speed * speed * (time_step * time_step / SCALE)
-            pair = []
             for field in range(2):
-                center = now[field, x, inner, :]
-                lap = (3.0 * scaled_weights[0]) * center
-                for k in range(1, REACH + 1):
-                    near = now[field, x + k, inner, :] + now[field, x - k, inner, :]
-                    near = near + now[field, x, pl.ds(TILE + k, rows), :]
-                    near = near + now[field, x, pl.ds(TILE - k, rows), :]
-                    lap = lap + scaled_weights[k] * near
-                at = (field * group + i) * rows
-                lap = lap + spread[at : at + rows]
-                pair.append((center, lap))
-                ahead = 2.0 * center - other[field, x, inner, :] + courant * lap
-                other[field, x, pl.ds(TILE, TILE), :] = ahead[:TILE] + drops[step, field, x]
-                other[field, x, pl.ds(2 * TILE, rows - TILE), :] = ahead[TILE:]
-            if imaged:
-                term = pair[1][0] * pair[0][1]
-                if step == 0:
-                    grad[x - deep] = term
-                else:
-                    grad[x - deep] = grad[x - deep] + term
-
-    now, other = one, two
-    for step in range(steps):
+                center, lap = laplacian(one, spread, field, i, x)
+                waiting[field, c * REACH + i] = lap
+                store_layer(two, field, x, 2.0 * center - two[field, x, inner, :], drops[0, field, x])
+        return carry
+
+    def inside(c, carry):
+        advance(one, two, courant, drops, band, 0, deep + c * REACH, grad, True, deep)
+        return carry
+
+    def core(c, carry):
+        advance(two, one, courant, drops, band, 1, deep + REACH + c * REACH, grad, False, deep)
+        return carry
+
+    lax.fori_loop(0, cells // REACH, inside, 0)
+    lax.fori_loop(0, cells // REACH - 2, core, 0)
+    lax.fori_loop(0, 2 * half, outside, 0)
+
+
+def late_kernel(
+    steps,
+    start,
+    count,
+    speed_a,
+    speed_b,
+    drops,
+    band,
+    image,
+    waiting,
+    one_in,
+    two_in,
+    courant_in,
+    grad_in,
+    final_w,
+    final_j,
+    parts,
+    one,
+    two,
+    courant,
+    grad,
+    sems,
+):
+    cells, rows, depth = image.shape
+    deep = steps * REACH
+    deep_prev = deep - REACH
+    tiles = rows // TILE
+    odd = lax.axis_index("slab") % 2
+    start_block = start[0]
+    live = count[0]
+    inner = pl.ds(TILE, rows)
+
+    def finish(h, carry):
+        right = h >= deep_prev
+        layer = jnp.where(right, h - deep_prev, h)
+        x = jnp.where(right, deep + cells, REACH) + layer
+        use_a = jnp.where(right, 1 - odd, odd) == 1
+        for tile in range(tiles):
+            alive = jnp.where(tile < live, time_step * time_step / SCALE, 0.0)
+            speed = jnp.where(use_a, speed_a[tile, layer], speed_b[tile, layer])
+            factor = alive * (speed * speed)
+            courant[x, pl.ds(tile * TILE, TILE), :] = factor
+            for field in range(2):
+                at = pl.ds(TILE + tile * TILE, TILE)
+                change = factor * waiting[field, h, pl.ds(tile * TILE, TILE), :]
+                two[field, x, at, :] = two[field, x, at, :] + change
+        return carry
+
+    lax.fori_loop(0, 2 * deep_prev, finish, 0)
+
+    now, other = two, one
+    for step in range(1, steps):
         margin = REACH * (step + 1)
-        half = (deep - margin) // group
-
-        def outside(i, carry):
-            advance(now, other, step, margin + i * group + jnp.where(i >= half, cells, 0), False)
+        half = (deep - margin) // REACH
+
+        def outside(c, carry):
+            x = margin + c * REACH + jnp.where(c >= half, cells, 0)
+            advance(now, other, courant, drops, band, step, x, None, False, deep)
             return carry
 
-        def inside(i, carry):
-            advance(now, other, step, deep + i * group, True)
+        stride = cells - REACH if step == 1 else REACH
+
+        def inside(c, carry):
+            advance(now, other, courant, drops, band, step, deep + c * stride, grad, False, deep)
             return carry
 
         if half:
             lax.fori_loop(0, 2 * half, outside, 0)
-        lax.fori_loop(0, cells // group, inside, 0)
+        lax.fori_loop(0, 2 if step == 1 else cells // REACH, inside, 0)
         now, other = other, now
 
     out = []
@@ -280,11 +365,16 @@
         out.append(pltpu.make_async_copy(now.at[field, pl.ds(deep, cells), inner], final.at[0], sems.at[field]))
         out[-1].start()
 
+    def clear_parts(b, carry):
+        parts[b] = jnp.zeros(parts.shape[1:], jnp.float32)
+        return carry
+
+    lax.fori_loop(0, parts.shape[0], clear_parts, 0)
+
     def place(x, carry):
         for tile in range(tiles):
-            speed = model[tile, deep + x]
-            piece = grad[x, pl.ds(tile * TILE, TILE), :]
-            parts[start_block + tile, x] = (2.0 * time_step * time_step / SCALE) * speed * piece
+            at = pl.ds(tile * TILE, TILE)
+            parts[start_block + tile, x] = image[x, at, :] * grad[x, at, :]
         return carry
 
     lax.fori_loop(0, cells, place, 0)
@@ -296,37 +386,55 @@
     now = fields[0]
     cells, rows, depth = now.shape[1:]
     deep = steps * REACH
+    deep_prev = deep - REACH
     wide = cells + 2 * deep
     tiles = rows // TILE
-    copies = 12 + 3 * tiles
-    final = jax.ShapeDtypeStruct(now.shape, jnp.float32)
+    copies = 12 + tiles
     away = np.abs(np.subtract.outer(np.arange(depth), np.arange(depth)))
     band = np.zeros((depth, depth), np.float32)
     for k in range(1, REACH + 1):
         band[away == k] = scaled_weights[k]
     band = jnp.asarray(np.concatenate([band, band], axis=0), jnp.bfloat16)
 
-    def kernel(*refs):
-        steps_kernel(steps, *refs)
-
-    field_buffer = pltpu.VMEM((2, wide, rows + 2 * TILE, depth), jnp.float32)
+    smem = pl.BlockSpec(memory_space=pltpu.SMEM)
     hbm = pl.BlockSpec(memory_space=pltpu.HBM)
     vmem = pl.BlockSpec(memory_space=pltpu.VMEM)
-    return pl.pallas_call(
-        kernel,
-        out_shape=(final, final, jax.ShapeDtypeStruct((groups, cells, TILE, depth), jnp.float32)),
-        in_specs=[pl.BlockSpec(memory_space=pltpu.SMEM)] * 2 + [hbm] * 4 + [any_space()] * 5 + [vmem, vmem],
-        out_specs=(any_space(), any_space(), vmem),
+    buffer = pltpu.VMEM((2, wide, rows + 2 * TILE, depth), jnp.float32)
+    factors = pltpu.VMEM((wide, rows, depth), jnp.float32)
+    layers = pltpu.VMEM((cells, rows, depth), jnp.float32)
+    waiting = pltpu.VMEM((2, 2 * deep_prev, rows, depth), jnp.float32)
+
+    def early(*refs):
+        early_kernel(steps, *refs)
+
+    def late(*refs):
+        late_kernel(steps, *refs)
+
+    one, two, courant, image, grad, waiting = pl.pallas_call(
+        early,
+        out_shape=(buffer, buffer, factors, layers, layers, waiting),
+        in_specs=[smem] * 2 + [hbm] * 4 + [any_space()] * 3 + [vmem, vmem],
+        out_specs=(vmem,) * 6,
         scratch_shapes=[
-            field_buffer,
-            field_buffer,
-            pltpu.VMEM((tiles, wide, TILE, depth), jnp.float32),
-            pltpu.VMEM((cells, rows, depth), jnp.float32),
+            pltpu.VMEM((tiles, cells, TILE, depth), jnp.float32),
             pltpu.SemaphoreType.DMA((copies,)),
         ],
-        compiler_params=pltpu.CompilerParams(vmem_limit_bytes=24 << 20),
+        compiler_params=pltpu.CompilerParams(vmem_limit_bytes=8 << 20),
         cost_estimate=pl.CostEstimate(flops=40 << 20, bytes_accessed=6 << 20, transcendentals=0),
-    )(start, count, *map(in_hbm, fields), from_a, from_b, in_hbm(speeds), speed_a, speed_b, drops, band)
+    )(start, count, *map(in_hbm, fields), from_a, from_b, in_hbm(speeds), drops, band)
+    final = jax.ShapeDtypeStruct(now.shape, jnp.float32)
+    parts = pltpu.VMEM((groups, cells, TILE, depth), jnp.float32)
+    results = pl.pallas_call(
+        late,
+        out_shape=(final, final, parts, buffer, buffer, factors, layers),
+        in_specs=[smem] * 2 + [vmem] * 10,
+        out_specs=(any_space(), any_space()) + (vmem,) * 5,
+        input_output_aliases={8: 3, 9: 4, 10: 5, 11: 6},
+        scratch_shapes=[pltpu.SemaphoreType.DMA((2,))],
+        compiler_params=pltpu.CompilerParams(vmem_limit_bytes=8 << 20),
+        cost_estimate=pl.CostEstimate(flops=40 << 20, bytes_accessed=6 << 20, transcendentals=0),
+    )(start, count, speed_a, speed_b, drops, band, image, waiting, one, two, courant, grad)
+    return results[:3]
 
 
 def per_device(
@@ -347,14 +455,14 @@
     tiles = wave_now.shape[2] // TILE
 
     to_a, to_b = pack(wave_now, adjoint_now, wave_prev, adjoint_prev, deep)
+    from_b = swap_pairs(to_b, "slab", 1)
     from_a = swap_pairs(to_a, "slab", 0)
-    from_b = swap_pairs(to_b, "slab", 1)
     speeds = lax.all_gather(velocity, "shot")
 
     cells_w, cells_j = (jnp.transpose(places, (2, 0, 1)) for places in (source_cells, receiver_cells))
     to_a, to_b, drops = cut_window(aperture_start, cells_w, cells_j, wavelet, trace, speeds, tiles)
+    speed_b = swap_pairs(to_b, "slab", 1)
     speed_a = swap_pairs(to_a, "slab", 0)
-    speed_b = swap_pairs(to_b, "slab", 1)
     fields = (wave_now, adjoint_now, wave_prev, adjoint_prev)
     groups = lax.axis_size("shot")
     final_w, final_j, parts = run_steps(

time: 55.7 us -> 52.3 us (0.939)
  the two profiles are of different devices: /device:TPU:8 before, /device:TPU:16 now
where the time goes in v2:
time: 52.3 us; the launch traced here: 52 us
  blocking collectives  26.2 us (50%)
  Pallas kernels  11.8 us (23%)
  starting transfers between devices  7.53 us (14%)
  local copies, waits for them, and re-layouts  3.56 us (7%)
  between operations  2.01 us (4%)
  other arithmetic  0.66 us (1%)
    all_to_all x1, blocking collectives, per_device(): shares = lax.all_to_all(parts, 'shot', 0, 0, tiled=True)  14.4 us
    all_gather x1, blocking collectives, per_device(): speeds = lax.all_gather(velocity, 'shot')  11.8 us
    ppermute x4, starting transfers between devices, swap_pairs(): return lax.ppermute(block, axis, route)  7.53 us
    pallas_call x1, Pallas kernels, run_steps(): pl.pallas_call(late, out_shape=(final, final, parts, buffer, buffer, fact...  4.55 us
    pallas_call x1, Pallas kernels, run_steps(): pl.pallas_call(early, out_shape=(buffer, buffer, factors, layers, layers,...  4.01 us
    unnamed x10, local copies, waits for them, and re-layouts  3.56 us
    pallas_call x1, Pallas kernels, cut_window(): pl.pallas_call(window_kernel, out_shape=(out, out, pltpu.VMEM((steps, 2,...  1.69 us
    pallas_call x1, Pallas kernels, pack(): pl.pallas_call(packing_kernel, out_shape=(out, out), in_specs=[pl.BlockSp...  1.51 us
  transfers between devices with their start and end apart: 4, of which 1 were waited for; matrix products, arithmetic and copies ran while one was open for 0% of the time, Pallas kernels for 11%

profile of v2, /device:TPU:16, one launch (start us, length us, event | category | flops | bytes accessed | tf_op | source)
XLA Modules:
  0.0 52.0 jit_solution(5322948058264759750)
XLA Ops:
  0.6 1.5 %shard_map.140 = (f32[56,32,128]{2,1,0:T(8,128)S(1)}, f32[56,32,128]{2,1,0:T(8,128)S(1)}) custom-call(f32[1,16,32,128]{3,2,1,0:T(8,128)} %refs_2_.1, f32[1,16,32,128]{3,2,1,0:T(8,128)} %refs_3_.1, f32[1,16,32,128]{3,2,1,0:T(8,128)} %refs_4_.1, f32[1,16,32,128]{3,2,1,0:T(8,128)} %refs_5_.2), custom_call_target="tpu_custom_call" | custom-call | bytes 4194304 | tf_op jit(solution)/shard_map/pallas_call | solution.py:54
  2.1 1.6 %collective-permute-start.2 = (f32[56,32,128]{2,1,0:T(8,128)S(1)}, f32[56,32,128]{2,1,0:T(8,128)S(1)}, u32[]{:S(2)}, u32[]{:S(2)}) collective-permute-start(f32[56,32,128]{2,1,0:T(8,128)S(1)} %get-tuple-element.20), channel_id=1, source_target_pairs={{0,1},{1,0},{2,3},{3,2},{4,5},{5,4},{6,7},{7,6},{8,9},{9,8},{10,11... | collective-permute-start | bytes 2752520 | tf_op jit(solution)/shard_map/ppermute | solution.py:22
  3.8 1.9 %collective-permute-start.3 = (f32[56,32,128]{2,1,0:T(8,128)S(1)}, f32[56,32,128]{2,1,0:T(8,128)S(1)}, u32[]{:S(2)}, u32[]{:S(2)}) collective-permute-start(f32[56,32,128]{2,1,0:T(8,128)S(1)} %get-tuple-element.21), channel_id=1, source_target_pairs={{1,2},{2,1},{5,6},{6,5},{9,10},{10,9},{13,14},{14,13},{17,18},{18,... | collective-permute-start | bytes 2752520 | tf_op jit(solution)/shard_map/ppermute | solution.py:22
  6.3 11.8 %all-gather = f32[128,8,128]{2,1,0:T(8,128)} all-gather(f32[16,8,128]{2,1,0:T(8,128)} %param.12), channel_id=2, replica_groups=mesh['shot'=8,'slab'=4] {'shot'}, dimensions={0}, use_global_device_ids=true | all-gather | bytes 589824 | tf_op jit(solution)/shard_map/all_gather | solution.py:460
  18.1 0.0 copy-start.1
  18.1 0.7 %copy-done.1 = f32[1,4,4]{2,1,0:T(4,128)S(1)} copy-done((f32[1,4,4]{2,1,0:T(4,128)S(1)}, f32[1,4,4]{2,1,0:T(4,128)}, u32[]{:S(2)}) %copy-start.1) | copy-done | bytes 88
  18.8 0.0 copy-start.2
  18.8 0.7 %copy-done.2 = f32[1,4,16]{2,1,0:T(4,128)S(1)} copy-done((f32[1,4,16]{2,1,0:T(4,128)S(1)}, f32[1,4,16]{2,1,0:T(4,128)}, u32[]{:S(2)}) %copy-start.2) | copy-done | bytes 280
  19.5 0.0 copy-start.3
  19.5 0.7 %copy-done.3 = s32[1,4,3]{1,0,2:T(1,128)S(1)} copy-done((s32[1,4,3]{1,0,2:T(1,128)S(1)}, s32[1,4,3]{1,0,2:T(1,128)}, u32[]{:S(2)}) %copy-start.3) | copy-done | bytes 72
  20.2 0.0 copy-start.4
  20.2 0.7 %copy-done.4 = s32[1,16,3]{1,0,2:T(1,128)S(1)} copy-done((s32[1,16,3]{1,0,2:T(1,128)S(1)}, s32[1,16,3]{1,0,2:T(1,128)}, u32[]{:S(2)}) %copy-start.4) | copy-done | bytes 216
  20.8 1.7 %shard_map.139 = (f32[4,12,8,128]{3,2,1,0:T(8,128)S(1)}, f32[4,12,8,128]{3,2,1,0:T(8,128)S(1)}, f32[4,2,48,8,128]{4,3,2,1,0:T(8,128)S(1)}) custom-call(s32[1]{0:T(128)S(6)} %copy.23.start.refs_0_, s32[3,1,4]{2,1,0:T(1,128)S(1)} %bitcast.3, s32[3,1,16]{2,1,0:T(1,128)S(1)} %bitcast.4, f32[1,4,4]{2,1,0:T(4,128)S(1)} %copy-done.1, f32[1,4,16]{2,1,0:T(4,128)S(1)} %copy-done.2, ...), custom_call_target="tpu_custom_call" | custom-call | flops 1048576 | bytes 2097152 | tf_op jit(solution)/shard_map/pallas_call | solution.py:118
  22.5 0.1 collective-permute-start
  22.6 3.9 %collective-permute-start.1 = (f32[4,12,8,128]{3,2,1,0:T(8,128)S(1)}, f32[4,12,8,128]{3,2,1,0:T(8,128)S(1)}, u32[]{:S(2)}, u32[]{:S(2)}) collective-permute-start(f32[4,12,8,128]{3,2,1,0:T(8,128)S(1)} %get-tuple-element.18), channel_id=1, source_target_pairs={{1,2},{2,1},{5,6},{6,5},{9,10},{10,9},{13,14},{14,13},{17,18},{18,... | collective-permute-start | bytes 589832 | tf_op jit(solution)/shard_map/ppermute | solution.py:22
  27.2 0.0 collective-permute-done.2.refs_6_
  27.2 0.3 collective-permute-done.3.refs_7_
  27.5 0.0 copy-start
  27.5 0.8 %copy-done = bf16[256,128]{1,0:T(8,128)(2,1)S(1)} copy-done((bf16[256,128]{1,0:T(8,128)(2,1)S(1)}, bf16[256,128]{1,0:T(8,128)(2,1)}, u32[]{:S(2)}) %copy-start) | copy-done | bytes 65560
  28.3 4.0 %shard_map.141 = (f32[2,48,48,128]{3,2,1,0:T(8,128)S(1)}, f32[2,48,48,128]{3,2,1,0:T(8,128)S(1)}, f32[48,32,128]{2,1,0:T(8,128)S(1)}, f32[16,32,128]{2,1,0:T(8,1...) custom-call(s32[1]{0:T(128)S(6)} %copy.23.start.refs_0_, s32[1]{0:T(128)S(6)} %copy.24.refs_1_, ...), custom_call_target="tpu_custom_call" | custom-call | flops 41943040 | bytes 6291456 | tf_op jit(solution)/shard_map/pallas_call | solution.py:413
  32.3 0.0 collective-permute-done.refs_2_
  32.3 0.0 collective-permute-done.1.refs_3_
  32.4 4.5 %shard_map.142 = (f32[1,16,32,128]{3,2,1,0:T(8,128)}, f32[1,16,32,128]{3,2,1,0:T(8,128)}, f32[8,16,8,128]{3,2,1,0:T(8,128)S(1)}, f32[2,48,48,128]{3,2,1,0:T(8,12...) custom-call(s32[1]{0:T(128)S(6)} %copy.23.start.refs_0_, ...), custom_call_target="tpu_custom_call", output_to_operand_aliasing={{3}: (8, {}), {4}: (9, {}), {5}: (10, {}), {6}: (11, {})} | custom-call | flops 41943040 | bytes 6291456 | tf_op jit(solution)/shard_map/pallas_call | solution.py:427
  36.9 14.4 %all_to_all.5 = f32[8,16,8,128]{3,2,1,0:T(8,128)S(1)} all-to-all(f32[8,16,8,128]{3,2,1,0:T(8,128)S(1)} %get-tuple-element.30), channel_id=1, replica_groups=mesh['shot'=8,'slab'=4] {'shot'}, dimensions={0} | all-to-all | bytes 1048576 | tf_op jit(solution)/shard_map/all_to_all | solution.py:471
  51.3 0.7 %reduce_sum.9 = f32[16,8,128]{2,1,0:T(8,128)} reduce(f32[8,16,8,128]{3,2,1,0:T(8,128)S(1)} %all_to_all.5, f32[]{:T(128)} %constant.1.clone.1), dimensions={0}, to_apply=%region_0.0 | reduce | flops 114688 | bytes 589828 | tf_op jit(solution)/shard_map/reduce_sum | solution.py:472
Async XLA Ops:
  2.1 25.0 %collective-permute-start.2 = (f32[56,32,128]{2,1,0:T(8,128)S(1)}, f32[56,32,128]{2,1,0:T(8,128)S(1)}, u32[]{:S(2)}, u32[]{:S(2)}) collective-permute-start(f32[56,32,128]{2,1,0:T(8,128)S(1)} %get-tuple-element.20), channel_id=1, source_target_pairs={{0,1},{1,0},{2,3},{3,2},{4,5},{5,4},{6,7},{7,6},{8,9},{9,8},{10,11... | collective-permute-start | bytes 2752520 | tf_op jit(solution)/shard_map/ppermute | solution.py:22
  3.8 23.7 %collective-permute-start.3 = (f32[56,32,128]{2,1,0:T(8,128)S(1)}, f32[56,32,128]{2,1,0:T(8,128)S(1)}, u32[]{:S(2)}, u32[]{:S(2)}) collective-permute-start(f32[56,32,128]{2,1,0:T(8,128)S(1)} %get-tuple-element.21), channel_id=1, source_target_pairs={{1,2},{2,1},{5,6},{6,5},{9,10},{10,9},{13,14},{14,13},{17,18},{18,... | collective-permute-start | bytes 2752520 | tf_op jit(solution)/shard_map/ppermute | solution.py:22
  18.1 0.7 %copy-start.1 = (f32[1,4,4]{2,1,0:T(4,128)S(1)}, f32[1,4,4]{2,1,0:T(4,128)}, u32[]{:S(2)}) copy-start(f32[1,4,4]{2,1,0:T(4,128)} %amps_w.1) | copy-start | bytes 196
  18.8 0.7 %copy-start.2 = (f32[1,4,16]{2,1,0:T(4,128)S(1)}, f32[1,4,16]{2,1,0:T(4,128)}, u32[]{:S(2)}) copy-start(f32[1,4,16]{2,1,0:T(4,128)} %amps_j.1) | copy-start | bytes 772
  19.5 0.7 %copy-start.3 = (s32[1,4,3]{1,0,2:T(1,128)S(1)}, s32[1,4,3]{1,0,2:T(1,128)}, u32[]{:S(2)}) copy-start(s32[1,4,3]{1,0,2:T(1,128)} %param.19) | copy-start | bytes 148
  20.2 0.7 %copy-start.4 = (s32[1,16,3]{1,0,2:T(1,128)S(1)}, s32[1,16,3]{1,0,2:T(1,128)}, u32[]{:S(2)}) copy-start(s32[1,16,3]{1,0,2:T(1,128)} %param.21) | copy-start | bytes 580
  22.5 9.8 %collective-permute-start = (f32[4,12,8,128]{3,2,1,0:T(8,128)S(1)}, f32[4,12,8,128]{3,2,1,0:T(8,128)S(1)}, u32[]{:S(2)}, u32[]{:S(2)}) collective-permute-start(f32[4,12,8,128]{3,2,1,0:T(8,128)S(1)} %get-tuple-element.17), channel_id=1, source_target_pairs={{0,1},{1,0},{2,3},{3,2},{4,5},{5,4},{6,7},{7,6},{8,9},{9,8},{10,11... | collective-permute-start | bytes 589832 | tf_op jit(solution)/shard_map/ppermute | solution.py:22
  22.6 9.7 %collective-permute-start.1 = (f32[4,12,8,128]{3,2,1,0:T(8,128)S(1)}, f32[4,12,8,128]{3,2,1,0:T(8,128)S(1)}, u32[]{:S(2)}, u32[]{:S(2)}) collective-permute-start(f32[4,12,8,128]{3,2,1,0:T(8,128)S(1)} %get-tuple-element.18), channel_id=1, source_target_pairs={{1,2},{2,1},{5,6},{6,5},{9,10},{10,9},{13,14},{14,13},{17,18},{18,... | collective-permute-start | bytes 589832 | tf_op jit(solution)/shard_map/ppermute | solution.py:22
  27.5 0.8 %copy-start = (bf16[256,128]{1,0:T(8,128)(2,1)S(1)}, bf16[256,128]{1,0:T(8,128)(2,1)}, u32[]{:S(2)}) copy-start(bf16[256,128]{1,0:T(8,128)(2,1)} %constant.4.clone.refs_10_.refs_5_) | copy-start | bytes 196612

commit v3 on v2

v3 whole, which is shorter than its diff:
```python
import jax
import jax.numpy as jnp
from jax import lax
from jax.experimental import pallas as pl
from jax.experimental.pallas import tpu as pltpu
from jax.sharding import PartitionSpec as P


SCALE = 5040.0
scaled_weights = (-14350.0, 8064.0, -1008.0, 128.0, -9.0)
time_step = 0.09
REACH = 4
TILE = 8


def swap_pairs(block, axis, first):
    count = lax.axis_size(axis)
    route = []
    for i in range(first, count - 1, 2):
        route += [(i, i + 1), (i + 1, i)]
    return lax.ppermute(block, axis, route)


def any_space():
    return pl.BlockSpec(memory_space=pl.ANY)


def in_hbm(array):
    return pltpu.with_memory_space_constraint(array, pltpu.HBM)


def packing_kernel(now_w, now_j, prev_w, prev_j, to_a, to_b, sems):
    cells = now_w.shape[1]
    deep_now = (to_a.shape[0] // 2 + REACH) // 2
    deep_prev = deep_now - REACH
    odd = lax.axis_index("slab") % 2
    copies, bring = bringing(sems)
    for out, side in ((to_a, 1 - odd), (to_b, odd)):
        at = 0
        for field, deep in ((now_w, deep_now), (now_j, deep_now), (prev_w, deep_prev), (prev_j, deep_prev)):
            bring(field.at[0, pl.ds(side * (cells - deep), deep)], out.at[pl.ds(at, deep)])
            at += deep
    for copy in copies:
        copy.wait()


def pack(fields, deep):
    rows, depth = fields[0].shape[2:]
    out = pltpu.VMEM((4 * deep - 2 * REACH, rows, depth), jnp.float32)
    return pl.pallas_call(
        packing_kernel,
        out_shape=(out, out),
        in_specs=[pl.BlockSpec(memory_space=pltpu.HBM)] * 4,
        out_specs=(any_space(), any_space()),
        scratch_shapes=[pltpu.SemaphoreType.DMA((8,))],
        compiler_params=pltpu.CompilerParams(vmem_limit_bytes=1 << 20),
        cost_estimate=pl.CostEstimate(flops=0, bytes_accessed=4 << 20, transcendentals=0),
    )(*map(in_hbm, fields))


def bringing(sems):
    copies = []

    def bring(source, target):
        copy = pltpu.make_async_copy(source, target, sems.at[len(copies)])
        copy.start()
        copies.append(copy)

    return copies, bring


def opening_kernel(
    start,
    count,
    cells_w_in,
    cells_j_in,
    amps_w_in,
    amps_j_in,
    now_w,
    now_j,
    prev_w,
    prev_j,
    speeds,
    to_a,
    to_b,
    drops,
    band,
    one,
    two,
    courant,
    image,
    grad,
    cells_w,
    cells_j,
    amps_w,
    amps_j,
    model,
    sems,
):
    cells, rows, depth = image.shape
    tiles, deep_prev = to_a.shape[:2]
    wide = drops.shape[2]
    steps = drops.shape[0]
    deep = deep_prev + REACH
    slab = lax.axis_index("slab")
    odd = slab % 2
    start_block = start[0]
    live = count[0]
    copies, bring = bringing(sems)
    for out, side in ((to_a, 1 - odd), (to_b, odd)):
        for tile in range(tiles):
            bring(speeds.at[start_block + tile, pl.ds(side * (cells - deep_prev), deep_prev)], out.at[tile])
    for source, target in ((cells_w_in, cells_w), (cells_j_in, cells_j), (amps_w_in, amps_w), (amps_j_in, amps_j)):
        bring(source, target)
    for tile in range(tiles):
        bring(speeds.at[start_block + tile], model.at[tile])
    inner = pl.ds(TILE, rows)
    for field, (now, prev) in enumerate(((now_w, prev_w), (now_j, prev_j))):
        bring(now.at[0], one.at[field, pl.ds(deep, cells), inner])
        bring(prev.at[0], two.at[field, pl.ds(deep, cells), inner])

    zero_tile = jnp.zeros((TILE, depth), jnp.float32)

    def clear(x, carry):
        for step in range(steps):
            for field in range(2):
                drops[step, field, x] = zero_tile
        for buffer in (one, two):
            for field in range(2):
                buffer[field, x, pl.ds(0, TILE), :] = zero_tile
                buffer[field, x, pl.ds(TILE + rows, TILE), :] = zero_tile
        return carry

    lax.fori_loop(0, wide, clear, 0)
    away = lax.broadcasted_iota(jnp.int32, (depth, depth), 0) - lax.broadcasted_iota(jnp.int32, (depth, depth), 1)
    matrix = jnp.zeros((depth, depth), jnp.float32)
    for k in range(1, REACH + 1):
        matrix = jnp.where((away == k) | (away == -k), scaled_weights[k], matrix)
    band[pl.ds(0, depth), :] = matrix.astype(jnp.bfloat16)
    band[pl.ds(depth, depth), :] = matrix.astype(jnp.bfloat16)
    for copy in copies:
        copy.wait()

    row = lax.broadcasted_iota(jnp.int32, (TILE, depth), 0)
    col = lax.broadcasted_iota(jnp.int32, (TILE, depth), 1)

    def inject(field, places, amps):
        def one_cell(s, carry):
            x = places[0, 0, s] - (slab * cells - deep)

            @pl.when((x >= 0) & (x < wide))
            def _():
                here = (row == places[1, 0, s]) & (col == places[2, 0, s])
                for step in range(steps):
                    drops[step, field, x] = drops[step, field, x] + jnp.where(here, amps[0, step, s], 0.0)

            return carry

        lax.fori_loop(0, places.shape[2], one_cell, 0)

    inject(0, cells_w, amps_w)
    inject(1, cells_j, amps_j)

    def factors(x, carry):
        for tile in range(tiles):
            alive = jnp.where(tile < live, time_step * time_step / SCALE, 0.0)
            speed = model[tile, x]
            at = pl.ds(tile * TILE, TILE)
            courant[deep + x, at, :] = alive * (speed * speed)
            image[x, at, :] = (2.0 * time_step * time_step / SCALE) * speed
        return carry

    lax.fori_loop(0, cells, factors, 0)
    clear_dead(one, two, live, deep, deep + cells)

    def core(c, carry):
        advance(one, two, courant, drops, band, 0, deep + REACH + c * REACH, grad, True, deep)
        return carry

    lax.fori_loop(0, cells // REACH - 2, core, 0, unroll=2)


def clear_dead(one, two, live, first, last):
    tiles = one.shape[2] // TILE - 2
    for tile in range(1, tiles):

        @pl.when(tile >= live)
        def _():
            def clear(x, carry):
                for buffer in (one, two):
                    for field in range(2):
                        buffer[field, x, pl.ds(TILE + tile * TILE, TILE), :] = jnp.zeros(
                            (TILE, one.shape[3]), jnp.float32
                        )
                return carry

            lax.fori_loop(first, last, clear, 0)


def opening(start, count, small, fields, speeds, steps):
    groups, cells, _, depth = speeds.shape
    rows = fields[0].shape[2]
    tiles = rows // TILE
    deep = steps * REACH
    wide = cells + 2 * deep
    halo = pltpu.VMEM((tiles, deep - REACH, TILE, depth), jnp.float32)
    drops = pltpu.VMEM((steps, 2, wide, TILE, depth), jnp.float32)
    band = pltpu.VMEM((2 * depth, depth), jnp.bfloat16)
    buffer = pltpu.VMEM((2, wide, rows + 2 * TILE, depth), jnp.float32)
    courant = pltpu.VMEM((wide, rows, depth), jnp.float32)
    layers = pltpu.VMEM((cells, rows, depth), jnp.float32)
    vmem = pl.BlockSpec(memory_space=pltpu.VMEM)
    return pl.pallas_call(
        opening_kernel,
        out_shape=(halo, halo, drops, band, buffer, buffer, courant, layers, layers),
        in_specs=[pl.BlockSpec(memory_space=pltpu.SMEM)] * 2 + [pl.BlockSpec(memory_space=pltpu.HBM)] * 9,
        out_specs=(vmem,) * 9,
        scratch_shapes=[pltpu.SMEM(array.shape, array.dtype) for array in small]
        + [
            pltpu.VMEM((tiles, cells, TILE, depth), jnp.float32),
            pltpu.SemaphoreType.DMA((3 * tiles + 8,)),
        ],
        compiler_params=pltpu.CompilerParams(vmem_limit_bytes=8 << 20),
        cost_estimate=pl.CostEstimate(flops=4 << 20, bytes_accessed=4 << 20, transcendentals=0),
    )(start, count, *map(in_hbm, small), *map(in_hbm, fields), in_hbm(speeds))


def along_z(now, band, x):
    rows, depth = now.shape[2] - 2 * TILE, now.shape[3]
    inner = pl.ds(TILE, rows)
    fields = [now[field, pl.ds(x, REACH), inner, :].reshape(REACH * rows, depth) for field in range(2)]
    cells = jnp.concatenate(fields, axis=0)
    high = cells.astype(jnp.bfloat16)
    low = (cells - high.astype(jnp.float32)).astype(jnp.bfloat16)
    return jnp.dot(jnp.concatenate([high, low], axis=1), band[...], preferred_element_type=jnp.float32)


def laplacian(now, spread, field, i, x):
    rows = now.shape[2] - 2 * TILE
    inner = pl.ds(TILE, rows)
    center = now[field, x, inner, :]
    lap = (3.0 * scaled_weights[0]) * center
    for k in range(1, REACH + 1):
        near = now[field, x + k, inner, :] + now[field, x - k, inner, :]
        near = near + now[field, x, pl.ds(TILE + k, rows), :]
        near = near + now[field, x, pl.ds(TILE - k, rows), :]
        lap = lap + scaled_weights[k] * near
    at = (field * REACH + i) * rows
    return center, lap + spread[at : at + rows]


def store_layer(buffer, field, x, values, drop):
    rows = values.shape[0]
    buffer[field, x, pl.ds(TILE, TILE), :] = values[:TILE] + drop
    buffer[field, x, pl.ds(2 * TILE, rows - TILE), :] = values[TILE:]


def advance(now, other, courant, drops, band, step, x_first, grad, fresh, deep):
    rows = now.shape[2] - 2 * TILE
    inner = pl.ds(TILE, rows)
    spread = along_z(now, band, x_first)
    for i in range(REACH):
        x = x_first + i
        pair = []
        for field in range(2):
            center, lap = laplacian(now, spread, field, i, x)
            pair.append((center, lap))
            ahead = 2.0 * center - other[field, x, inner, :] + courant[x] * lap
            store_layer(other, field, x, ahead, drops[step, field, x])
        if grad is not None:
            term = pair[1][0] * pair[0][1]
            grad[x - deep] = term if fresh else grad[x - deep] + term


def early_kernel(steps, count, from_a, from_b, courant, drops, band, one_in, two_in, grad_in, one, two, grad, waiting, sems):
    cells, rows, depth = grad.shape
    deep = steps * REACH
    deep_prev = deep - REACH
    wide = cells + 2 * deep
    odd = lax.axis_index("slab") % 2

    left_of_a = odd
    copies, bring = bringing(sems)
    inner = pl.ds(TILE, rows)
    for field in range(2):
        for buffer, on_left in ((from_a, left_of_a), (from_b, 1 - left_of_a)):
            at = (1 - on_left) * (deep + cells)
            bring(buffer.at[pl.ds(field * deep, deep)], one.at[field, pl.ds(at, deep), inner])
            at = on_left * REACH + (1 - on_left) * (deep + cells)
            bring(
                buffer.at[pl.ds(2 * deep + field * deep_prev, deep_prev)],
                two.at[field, pl.ds(at, deep_prev), inner],
            )
    for copy in copies:
        copy.wait()
    clear_dead(one, two, count[0], 0, deep)
    clear_dead(one, two, count[0], deep + cells, wide)

    half = deep_prev // REACH

    def outside(c, carry):
        x_first = REACH + c * REACH + jnp.where(c >= half, cells, 0)
        spread = along_z(one, band, x_first)
        for i in range(REACH):
            x = x_first + i
            for field in range(2):
                center, lap = laplacian(one, spread, field, i, x)
                waiting[field, c * REACH + i] = lap
                store_layer(two, field, x, 2.0 * center - two[field, x, inner, :], drops[0, field, x])
        return carry

    def inside(c, carry):
        advance(one, two, courant, drops, band, 0, deep + c * (cells - REACH), grad, True, deep)
        return carry

    def core(c, carry):
        advance(two, one, courant, drops, band, 1, deep + REACH + c * REACH, grad, False, deep)
        return carry

    lax.fori_loop(0, 2, inside, 0, unroll=2)
    lax.fori_loop(0, 2 * half, outside, 0, unroll=2)
    lax.fori_loop(0, cells // REACH - 2, core, 0, unroll=2)


def late_kernel(
    steps,
    start,
    count,
    speed_a,
    speed_b,
    drops,
    band,
    image,
    waiting,
    one_in,
    two_in,
    courant_in,
    grad_in,
    final_w,
    final_j,
    parts,
    one,
    two,
    courant,
    grad,
    sems,
):
    cells, rows, depth = image.shape
    deep = steps * REACH
    deep_prev = deep - REACH
    tiles = rows // TILE
    odd = lax.axis_index("slab") % 2
    start_block = start[0]
    live = count[0]
    inner = pl.ds(TILE, rows)

    def finish(h, carry):
        right = h >= deep_prev
        layer = jnp.where(right, h - deep_prev, h)
        x = jnp.where(right, deep + cells, REACH) + layer
        use_a = jnp.where(right, 1 - odd, odd) == 1
        for tile in range(tiles):
            alive = jnp.where(tile < live, time_step * time_step / SCALE, 0.0)
            speed = jnp.where(use_a, speed_a[tile, layer], speed_b[tile, layer])
            factor = alive * (speed * speed)
            courant[x, pl.ds(tile * TILE, TILE), :] = factor
            for field in range(2):
                at = pl.ds(TILE + tile * TILE, TILE)
                change = factor * waiting[field, h, pl.ds(tile * TILE, TILE), :]
                two[field, x, at, :] = two[field, x, at, :] + change
        return carry

    lax.fori_loop(0, 2 * deep_prev, finish, 0)

    now, other = two, one
    for step in range(1, steps):
        margin = REACH * (step + 1)
        half = (deep - margin) // REACH

        def outside(c, carry):
            x = margin + c * REACH + jnp.where(c >= half, cells, 0)
            advance(now, other, courant, drops, band, step, x, None, False, deep)
            return carry

        stride = cells - REACH if step == 1 else REACH

        def inside(c, carry):
            advance(now, other, courant, drops, band, step, deep + c * stride, grad, False, deep)
            return carry

        if half:
            lax.fori_loop(0, 2 * half, outside, 0, unroll=2)
        lax.fori_loop(0, 2 if step == 1 else cells // REACH, inside, 0, unroll=2)
        now, other = other, now

    out = []
    for field, final in ((0, final_w), (1, final_j)):
        out.append(pltpu.make_async_copy(now.at[field, pl.ds(deep, cells), inner], final.at[0], sems.at[field]))
        out[-1].start()

    def clear_parts(b, carry):
        parts[b] = jnp.zeros(parts.shape[1:], jnp.float32)
        return carry

    lax.fori_loop(0, parts.shape[0], clear_parts, 0)

    def place(x, carry):
        for tile in range(tiles):
            at = pl.ds(tile * TILE, TILE)
            parts[start_block + tile, x] = image[x, at, :] * grad[x, at, :]
        return carry

    lax.fori_loop(0, cells, place, 0)
    for copy in out:
        copy.wait()


def early_steps(steps, count, from_a, from_b, courant, drops, band, one, two, grad):
    rows, depth = grad.shape[1:]
    deep_prev = (steps - 1) * REACH
    smem = pl.BlockSpec(memory_space=pltpu.SMEM)
    vmem = pl.BlockSpec(memory_space=pltpu.VMEM)
    same = [pltpu.VMEM(array.shape, array.dtype) for array in (one, two, grad)]

    def kernel(*refs):
        early_kernel(steps, *refs)

    return pl.pallas_call(
        kernel,
        out_shape=(*same, pltpu.VMEM((2, 2 * deep_prev, rows, depth), jnp.float32)),
        in_specs=[smem, any_space(), any_space()] + [vmem] * 6,
        out_specs=(vmem,) * 4,
        input_output_aliases={6: 0, 7: 1, 8: 2},
        scratch_shapes=[pltpu.SemaphoreType.DMA((8,))],
        compiler_params=pltpu.CompilerParams(vmem_limit_bytes=8 << 20),
        cost_estimate=pl.CostEstimate(flops=20 << 20, bytes_accessed=4 << 20, transcendentals=0),
    )(count, from_a, from_b, courant, drops, band, one, two, grad)


def late_steps(steps, start, count, speed_a, speed_b, drops, band, image, waiting, one, two, courant, grad, groups):
    cells, rows, depth = image.shape
    smem = pl.BlockSpec(memory_space=pltpu.SMEM)
    vmem = pl.BlockSpec(memory_space=pltpu.VMEM)
    final = jax.ShapeDtypeStruct((1, cells, rows, depth), jnp.float32)
    parts = pltpu.VMEM((groups, cells, TILE, depth), jnp.float32)
    same = [pltpu.VMEM(array.shape, array.dtype) for array in (one, two, courant, grad)]

    def kernel(*refs):
        late_kernel(steps, *refs)

    return pl.pallas_call(
        kernel,
        out_shape=(final, final, parts, *same),
        in_specs=[smem] * 2 + [vmem] * 10,
        out_specs=(any_space(), any_space()) + (vmem,) * 5,
        input_output_aliases={8: 3, 9: 4, 10: 5, 11: 6},
        scratch_shapes=[pltpu.SemaphoreType.DMA((2,))],
        compiler_params=pltpu.CompilerParams(vmem_limit_bytes=8 << 20),
        cost_estimate=pl.CostEstimate(flops=40 << 20, bytes_accessed=6 << 20, transcendentals=0),
    )(start, count, speed_a, speed_b, drops, band, image, waiting, one, two, courant, grad)[:3]


def per_device(
    velocity,
    aperture_start,
    aperture_count,
    wave_prev,
    wave_now,
    adjoint_prev,
    adjoint_now,
    source_cells,
    wavelet,
    receiver_cells,
    trace,
):
    steps = wavelet.shape[1]
    deep = steps * REACH
    fields = (wave_now, adjoint_now, wave_prev, adjoint_prev)

    to_a, to_b = pack(fields, deep)
    from_a = swap_pairs(to_a, "slab", 0)
    from_b = swap_pairs(to_b, "slab", 1)
    speeds = lax.all_gather(velocity, "shot")

    cells_w, cells_j = (jnp.transpose(places, (2, 0, 1)) for places in (source_cells, receiver_cells))
    small = (cells_w, cells_j, wavelet, trace)
    to_a, to_b, drops, band, one, two, courant, image, grad = opening(
        aperture_start, aperture_count, small, fields, speeds, steps
    )
    speed_a = swap_pairs(to_a, "slab", 0)
    speed_b = swap_pairs(to_b, "slab", 1)
    one, two, grad, waiting = early_steps(
        steps, aperture_count, from_a, from_b, courant, drops, band, one, two, grad
    )
    final_w, final_j, parts = late_steps(
        steps,
        aperture_start,
        aperture_count,
        speed_a,
        speed_b,
        drops,
        band,
        image,
        waiting,
        one,
        two,
        courant,
        grad,
        lax.axis_size("shot"),
    )
    shares = lax.all_to_all(parts, "shot", 0, 0, tiled=True)
    return final_w, final_j, jnp.sum(shares, axis=0)


def solution(mesh):
    return jax.shard_map(
        per_device,
        mesh=mesh,
        in_specs=(
            P("slab", "shot", None),
            P("shot"),
            P("shot"),
            P("shot", "slab", None, None),
            P("shot", "slab", None, None),
            P("shot", "slab", None, None),
            P("shot", "slab", None, None),
            P("shot", None, None),
            P("shot", None, None),
            P("shot", None, None),
            P("shot", None, None),
        ),
        out_specs=(
            P("shot", "slab", None, None),
            P("shot", "slab", None, None),
            P("slab", "shot", None),
        ),
        check_vma=False,
    )
```

time: 52.3 us -> 50.1 us (0.958)
  the two profiles are of different devices: /device:TPU:16 before, /device:TPU:8 now
where the time goes in v3:
time: 50.1 us; the launch traced here: 49.6 us
  blocking collectives  24.2 us (48%)
  Pallas kernels  10.5 us (21%)
  starting transfers between devices  7.1 us (14%)
  waiting for transfers between devices  5.18 us (10%)
  between operations  2 us (4%)
  other arithmetic  0.66 us (1%)
    all_to_all x1, blocking collectives, per_device(): shares = lax.all_to_all(parts, 'shot', 0, 0, tiled=True)  12.5 us
    all_gather x1, blocking collectives, per_device(): speeds = lax.all_gather(velocity, 'shot')  11.7 us
    ppermute x4, starting transfers between devices, swap_pairs(): return lax.ppermute(block, axis, route)  7.1 us
    ppermute x4, waiting for transfers between devices, swap_pairs(): return lax.ppermute(block, axis, route)  5.18 us
    pallas_call x1, Pallas kernels, late_steps(): pl.pallas_call(kernel, out_shape=(final, final, parts, *same), in_specs=[...  4.14 us
    pallas_call x1, Pallas kernels, opening(): pl.pallas_call(opening_kernel, out_shape=(halo, halo, drops, band, buffer...  2.62 us
    pallas_call x1, Pallas kernels, early_steps(): pl.pallas_call(kernel, out_shape=(*same, pltpu.VMEM((2, 2 * deep_prev, ro...  2.19 us
    pallas_call x1, Pallas kernels, pack(): pl.pallas_call(packing_kernel, out_shape=(out, out), in_specs=[pl.BlockSp...  1.5 us
  transfers between devices with their start and end apart: 4, of which 3 were waited for; matrix products, arithmetic and copies ran while one was open for 0% of the time, Pallas kernels for 10%

profile of v3, /device:TPU:8, one launch (start us, length us, event | category | flops | bytes accessed | tf_op | source)
XLA Modules:
  0.0 49.6 jit_solution(14739437935732266975)
XLA Ops:
  0.6 1.5 %shard_map.131 = (f32[56,32,128]{2,1,0:T(8,128)S(1)}, f32[56,32,128]{2,1,0:T(8,128)S(1)}) custom-call(f32[1,16,32,128]{3,2,1,0:T(8,128)} %now_w.3, f32[1,16,32,128]{3,2,1,0:T(8,128)} %now_j.3, f32[1,16,32,128]{3,2,1,0:T(8,128)} %prev_w.3, f32[1,16,32,128]{3,2,1,0:T(8,128)} %prev_j.3), custom_call_target="tpu_custom_call" | custom-call | bytes 4194304 | tf_op jit(solution)/shard_map/pallas_call | solution.py:50
  2.1 0.1 collective-permute-start.2
  2.2 5.0 %collective-permute-start.3 = (f32[56,32,128]{2,1,0:T(8,128)S(1)}, f32[56,32,128]{2,1,0:T(8,128)S(1)}, u32[]{:S(2)}, u32[]{:S(2)}) collective-permute-start(f32[56,32,128]{2,1,0:T(8,128)S(1)} %get-tuple-element.27), channel_id=1, source_target_pairs={{1,2},{2,1},{5,6},{6,5},{9,10},{10,9},{13,14},{14,13},{17,18},{18,... | collective-permute-start | bytes 2752520 | tf_op jit(solution)/shard_map/ppermute | solution.py:21
  8.6 11.7 %all-gather = f32[128,8,128]{2,1,0:T(8,128)} all-gather(f32[16,8,128]{2,1,0:T(8,128)} %param.11), channel_id=2, replica_groups=mesh['shot'=8,'slab'=4] {'shot'}, dimensions={0}, use_global_device_ids=true | all-gather | bytes 589824 | tf_op jit(solution)/shard_map/all_gather | solution.py:483
  20.3 2.6 %shard_map.130 = (f32[4,12,8,128]{3,2,1,0:T(8,128)S(1)}, f32[4,12,8,128]{3,2,1,0:T(8,128)S(1)}, f32[4,2,48,8,128]{4,3,2,1,0:T(8,128)S(1)}, bf16[256,128]{1,0:T(8...) custom-call(s32[1]{0:T(128)S(6)} %copy.28.start.refs_0_, ...), custom_call_target="tpu_custom_call" | custom-call | flops 4194304 | bytes 4194304 | tf_op jit(solution)/shard_map/pallas_call | solution.py:213
  22.9 0.1 collective-permute-start
  23.0 1.9 %collective-permute-start.1 = (f32[4,12,8,128]{3,2,1,0:T(8,128)S(1)}, f32[4,12,8,128]{3,2,1,0:T(8,128)S(1)}, u32[]{:S(2)}, u32[]{:S(2)}) collective-permute-start(f32[4,12,8,128]{3,2,1,0:T(8,128)S(1)} %get-tuple-element.22), channel_id=1, source_target_pairs={{1,2},{2,1},{5,6},{6,5},{9,10},{10,9},{13,14},{14,13},{17,18},{18,... | collective-permute-start | bytes 589832 | tf_op jit(solution)/shard_map/ppermute | solution.py:21
  24.9 0.0 collective-permute-done.2.refs_1_
  25.0 2.4 %collective-permute-done.3.refs_2_ = f32[56,32,128]{2,1,0:T(8,128)S(1)} collective-permute-done((f32[56,32,128]{2,1,0:T(8,128)S(1)}, f32[56,32,128]{2,1,0:T(8,128)S(1)}, u32[]{:S(2)}, u32[]{:S(2)}) %collective-permute-start.3) | collective-permute-done | bytes 917536 | tf_op jit(solution)/shard_map/ppermute | solution.py:21
  27.3 2.2 %shard_map.132 = (f32[2,48,48,128]{3,2,1,0:T(8,128)S(1)}, f32[2,48,48,128]{3,2,1,0:T(8,128)S(1)}, f32[16,32,128]{2,1,0:T(8,128)S(1)}, f32[2,24,32,128]{3,2,1,0:T(8,128)S(1)}) custom-call(s32[1]{0:T(128)S(6)} %copy.29.count.refs_0_.refs_1_, ...), custom_call_target="tpu_custom_call", output_to_operand_aliasing={{0}: (6, {}), {1}: (7, {}), {2}: (8, {})} | custom-call | flops 20971520 | bytes 4194304 | tf_op jit(solution)/shard_map/pallas_call | solution.py:428
  29.5 0.9 %collective-permute-done.refs_2_ = f32[4,12,8,128]{3,2,1,0:T(8,128)S(1)} collective-permute-done((f32[4,12,8,128]{3,2,1,0:T(8,128)S(1)}, f32[4,12,8,128]{3,2,1,0:T(8,128)S(1)}, u32[]{:S(2)}, u32[]{:S(2)}) %collective-permute-start) | collective-permute-done | bytes 196640 | tf_op jit(solution)/shard_map/ppermute | solution.py:21
  30.4 1.9 %collective-permute-done.1.refs_3_ = f32[4,12,8,128]{3,2,1,0:T(8,128)S(1)} collective-permute-done((f32[4,12,8,128]{3,2,1,0:T(8,128)S(1)}, f32[4,12,8,128]{3,2,1,0:T(8,128)S(1)}, u32[]{:S(2)}, u32[]{:S(2)}) %collective-permute-start.1) | collective-permute-done | bytes 196640 | tf_op jit(solution)/shard_map/ppermute | solution.py:21
  32.3 4.1 %shard_map.133 = (f32[1,16,32,128]{3,2,1,0:T(8,128)}, f32[1,16,32,128]{3,2,1,0:T(8,128)}, f32[8,16,8,128]{3,2,1,0:T(8,128)S(1)}, f32[2,48,48,128]{3,2,1,0:T(8,12...) custom-call(s32[1]{0:T(128)S(6)} %copy.28.start.refs_0_, ...), custom_call_target="tpu_custom_call", output_to_operand_aliasing={{3}: (8, {}), {4}: (9, {}), {5}: (10, {}), {6}: (11, {})} | custom-call | flops 41943040 | bytes 6291456 | tf_op jit(solution)/shard_map/pallas_call | solution.py:451
  36.5 12.5 %all_to_all.5 = f32[8,16,8,128]{3,2,1,0:T(8,128)S(1)} all-to-all(f32[8,16,8,128]{3,2,1,0:T(8,128)S(1)} %get-tuple-element.38), channel_id=1, replica_groups=mesh['shot'=8,'slab'=4] {'shot'}, dimensions={0} | all-to-all | bytes 1048576 | tf_op jit(solution)/shard_map/all_to_all | solution.py:511
  48.9 0.7 %reduce_sum.9 = f32[16,8,128]{2,1,0:T(8,128)} reduce(f32[8,16,8,128]{3,2,1,0:T(8,128)S(1)} %all_to_all.5, f32[]{:T(128)} %constant.0.clone.1), dimensions={0}, to_apply=%region_0.0 | reduce | flops 114688 | bytes 589828 | tf_op jit(solution)/shard_map/reduce_sum | solution.py:512
Async XLA Ops:
  2.1 22.8 %collective-permute-start.2 = (f32[56,32,128]{2,1,0:T(8,128)S(1)}, f32[56,32,128]{2,1,0:T(8,128)S(1)}, u32[]{:S(2)}, u32[]{:S(2)}) collective-permute-start(f32[56,32,128]{2,1,0:T(8,128)S(1)} %get-tuple-element.26), channel_id=1, source_target_pairs={{0,1},{1,0},{2,3},{3,2},{4,5},{5,4},{6,7},{7,6},{8,9},{9,8},{10,11... | collective-permute-start | bytes 2752520 | tf_op jit(solution)/shard_map/ppermute | solution.py:21
  2.2 25.1 %collective-permute-start.3 = (f32[56,32,128]{2,1,0:T(8,128)S(1)}, f32[56,32,128]{2,1,0:T(8,128)S(1)}, u32[]{:S(2)}, u32[]{:S(2)}) collective-permute-start(f32[56,32,128]{2,1,0:T(8,128)S(1)} %get-tuple-element.27), channel_id=1, source_target_pairs={{1,2},{2,1},{5,6},{6,5},{9,10},{10,9},{13,14},{14,13},{17,18},{18,... | collective-permute-start | bytes 2752520 | tf_op jit(solution)/shard_map/ppermute | solution.py:21
  22.9 7.5 %collective-permute-start = (f32[4,12,8,128]{3,2,1,0:T(8,128)S(1)}, f32[4,12,8,128]{3,2,1,0:T(8,128)S(1)}, u32[]{:S(2)}, u32[]{:S(2)}) collective-permute-start(f32[4,12,8,128]{3,2,1,0:T(8,128)S(1)} %get-tuple-element.21), channel_id=1, source_target_pairs={{0,1},{1,0},{2,3},{3,2},{4,5},{5,4},{6,7},{7,6},{8,9},{9,8},{10,11... | collective-permute-start | bytes 589832 | tf_op jit(solution)/shard_map/ppermute | solution.py:21
  23.0 9.3 %collective-permute-start.1 = (f32[4,12,8,128]{3,2,1,0:T(8,128)S(1)}, f32[4,12,8,128]{3,2,1,0:T(8,128)S(1)}, u32[]{:S(2)}, u32[]{:S(2)}) collective-permute-start(f32[4,12,8,128]{3,2,1,0:T(8,128)S(1)} %get-tuple-element.22), channel_id=1, source_target_pairs={{1,2},{2,1},{5,6},{6,5},{9,10},{10,9},{13,14},{14,13},{17,18},{18,... | collective-permute-start | bytes 589832 | tf_op jit(solution)/shard_map/ppermute | solution.py:21

commit v4 on v3

--- a/solution.py
+++ b/solution.py
@@ -255,7 +255,7 @@
     buffer[field, x, pl.ds(2 * TILE, rows - TILE), :] = values[TILE:]
 
 
-def advance(now, other, courant, drops, band, step, x_first, grad, fresh, deep):
+def advance(now, other, courant, drops, band, step, x_first, grad, fresh, deep, finals=None):
     rows = now.shape[2] - 2 * TILE
     inner = pl.ds(TILE, rows)
     spread = along_z(now, band, x_first)
@@ -266,13 +266,17 @@
             center, lap = laplacian(now, spread, field, i, x)
             pair.append((center, lap))
             ahead = 2.0 * center - other[field, x, inner, :] + courant[x] * lap
-            store_layer(other, field, x, ahead, drops[step, field, x])
+            if finals is None:
+                store_layer(other, field, x, ahead, drops[step, field, x])
+            else:
+                finals[field, x - deep, pl.ds(0, TILE), :] = ahead[:TILE] + drops[step, field, x]
+                finals[field, x - deep, pl.ds(TILE, rows - TILE), :] = ahead[TILE:]
         if grad is not None:
             term = pair[1][0] * pair[0][1]
             grad[x - deep] = term if fresh else grad[x - deep] + term
 
 
-def early_kernel(steps, count, from_a, from_b, courant, drops, band, one_in, two_in, grad_in, one, two, grad, waiting, sems):
+def early_kernel(steps, count, from_a, from_b, courant, drops, band, one_in, two_in, grad_in, one, two, grad, waiting, parts, sems):
     cells, rows, depth = grad.shape
     deep = steps * REACH
     deep_prev = deep - REACH
@@ -291,6 +295,11 @@
                 buffer.at[pl.ds(2 * deep + field * deep_prev, deep_prev)],
                 two.at[field, pl.ds(at, deep_prev), inner],
             )
+    def clear_parts(b, carry):
+        parts[b] = jnp.zeros(parts.shape[1:], jnp.float32)
+        return carry
+
+    lax.fori_loop(0, parts.shape[0], clear_parts, 0)
     for copy in copies:
         copy.wait()
     clear_dead(one, two, count[0], 0, deep)
@@ -336,13 +345,15 @@
     two_in,
     courant_in,
     grad_in,
+    parts_in,
     final_w,
     final_j,
-    parts,
     one,
     two,
     courant,
     grad,
+    parts,
+    finals,
     sems,
 ):
     cells, rows, depth = image.shape
@@ -353,6 +364,8 @@
     start_block = start[0]
     live = count[0]
     inner = pl.ds(TILE, rows)
+
+    copies, bring = bringing(sems)
 
     def finish(h, carry):
         right = h >= deep_prev
@@ -370,7 +383,7 @@
                 two[field, x, at, :] = two[field, x, at, :] + change
         return carry
 
-    lax.fori_loop(0, 2 * deep_prev, finish, 0)
+    lax.fori_loop(0, 2 * deep_prev, finish, 0, unroll=4)
 
     now, other = two, one
     for step in range(1, steps):
@@ -385,24 +398,20 @@
         stride = cells - REACH if step == 1 else REACH
 
         def inside(c, carry):
-            advance(now, other, courant, drops, band, step, deep + c * stride, grad, False, deep)
+            last = finals if step == steps - 1 else None
+            advance(now, other, courant, drops, band, step, deep + c * stride, grad, False, deep, last)
             return carry
 
         if half:
             lax.fori_loop(0, 2 * half, outside, 0, unroll=2)
-        lax.fori_loop(0, 2 if step == 1 else cells // REACH, inside, 0, unroll=2)
+        groups = 2 if step == 1 else cells // REACH
+        for first in range(0, groups, 2):
+            lax.fori_loop(first, min(first + 2, groups), inside, 0, unroll=2)
+            if step == steps - 1:
+                done = pl.ds(first * REACH, min(2, groups - first) * REACH)
+                bring(finals.at[0, done], final_w.at[0, done])
+                bring(finals.at[1, done], final_j.at[0, done])
         now, other = other, now
-
-    out = []
-    for field, final in ((0, final_w), (1, final_j)):
-        out.append(pltpu.make_async_copy(now.at[field, pl.ds(deep, cells), inner], final.at[0], sems.at[field]))
-        out[-1].start()
-
-    def clear_parts(b, carry):
-        parts[b] = jnp.zeros(parts.shape[1:], jnp.float32)
-        return carry
-
-    lax.fori_loop(0, parts.shape[0], clear_parts, 0)
 
     def place(x, carry):
         for tile in range(tiles):
@@ -410,14 +419,16 @@
             parts[start_block + tile, x] = image[x, at, :] * grad[x, at, :]
         return carry
 
-    lax.fori_loop(0, cells, place, 0)
-    for copy in out:
+    lax.fori_loop(0, cells, place, 0, unroll=4)
+    for copy in copies:
         copy.wait()
 
 
-def early_steps(steps, count, from_a, from_b, courant, drops, band, one, two, grad):
-    rows, depth = grad.shape[1:]
+def early_steps(steps, count, from_a, from_b, courant, drops, band, one, two, grad, groups):
+    cells, rows, depth = grad.shape
     deep_prev = (steps - 1) * REACH
+    waiting = pltpu.VMEM((2, 2 * deep_prev, rows, depth), jnp.float32)
+    parts = pltpu.VMEM((groups, cells, TILE, depth), jnp.float32)
     smem = pl.BlockSpec(memory_space=pltpu.SMEM)
     vmem = pl.BlockSpec(memory_space=pltpu.VMEM)
     same = [pltpu.VMEM(array.shape, array.dtype) for array in (one, two, grad)]
@@ -427,9 +438,9 @@
 
     return pl.pallas_call(
         kernel,
-        out_shape=(*same, pltpu.VMEM((2, 2 * deep_prev, rows, depth), jnp.float32)),
+        out_shape=(*same, waiting, parts),
         in_specs=[smem, any_space(), any_space()] + [vmem] * 6,
-        out_specs=(vmem,) * 4,
+        out_specs=(vmem,) * 5,
         input_output_aliases={6: 0, 7: 1, 8: 2},
         scratch_shapes=[pltpu.SemaphoreType.DMA((8,))],
         compiler_params=pltpu.CompilerParams(vmem_limit_bytes=8 << 20),
@@ -437,27 +448,29 @@
     )(count, from_a, from_b, courant, drops, band, one, two, grad)
 
 
-def late_steps(steps, start, count, speed_a, speed_b, drops, band, image, waiting, one, two, courant, grad, groups):
-    cells, rows, depth = image.shape
+def late_steps(steps, start, count, speed_a, speed_b, drops, band, image, waiting, one, two, courant, grad, parts):
     smem = pl.BlockSpec(memory_space=pltpu.SMEM)
     vmem = pl.BlockSpec(memory_space=pltpu.VMEM)
-    final = jax.ShapeDtypeStruct((1, cells, rows, depth), jnp.float32)
-    parts = pltpu.VMEM((groups, cells, TILE, depth), jnp.float32)
-    same = [pltpu.VMEM(array.shape, array.dtype) for array in (one, two, courant, grad)]
+    final = jax.ShapeDtypeStruct((1, *image.shape), jnp.float32)
+    same = [pltpu.VMEM(array.shape, array.dtype) for array in (one, two, courant, grad, parts)]
 
     def kernel(*refs):
         late_kernel(steps, *refs)
 
-    return pl.pallas_call(
+    results = pl.pallas_call(
         kernel,
-        out_shape=(final, final, parts, *same),
-        in_specs=[smem] * 2 + [vmem] * 10,
+        out_shape=(final, final, *same),
+        in_specs=[smem] * 2 + [vmem] * 11,
         out_specs=(any_space(), any_space()) + (vmem,) * 5,
-        input_output_aliases={8: 3, 9: 4, 10: 5, 11: 6},
-        scratch_shapes=[pltpu.SemaphoreType.DMA((2,))],
+        input_output_aliases={8: 2, 9: 3, 10: 4, 11: 5, 12: 6},
+        scratch_shapes=[
+            pltpu.VMEM((2, *image.shape), jnp.float32),
+            pltpu.SemaphoreType.DMA((2 * image.shape[0] // REACH,)),
+        ],
         compiler_params=pltpu.CompilerParams(vmem_limit_bytes=8 << 20),
         cost_estimate=pl.CostEstimate(flops=40 << 20, bytes_accessed=6 << 20, transcendentals=0),
-    )(start, count, speed_a, speed_b, drops, band, image, waiting, one, two, courant, grad)[:3]
+    )(start, count, speed_a, speed_b, drops, band, image, waiting, one, two, courant, grad, parts)
+    return results[0], results[1], results[6]
 
 
 def per_device(
@@ -489,8 +502,8 @@
     )
     speed_a = swap_pairs(to_a, "slab", 0)
     speed_b = swap_pairs(to_b, "slab", 1)
-    one, two, grad, waiting = early_steps(
-        steps, aperture_count, from_a, from_b, courant, drops, band, one, two, grad
+    one, two, grad, waiting, parts = early_steps(
+        steps, aperture_count, from_a, from_b, courant, drops, band, one, two, grad, lax.axis_size("shot")
     )
     final_w, final_j, parts = late_steps(
         steps,
@@ -506,7 +519,7 @@
         two,
         courant,
         grad,
-        lax.axis_size("shot"),
+        parts,
     )
     shares = lax.all_to_all(parts, "shot", 0, 0, tiled=True)
     return final_w, final_j, jnp.sum(shares, axis=0)

time: 50.1 us -> 49.8 us (level)
  no operation moved by 1% of the time
where the time goes in v4:
time: 49.8 us; the launch traced here: 49.3 us
  blocking collectives  24.2 us (49%)
  Pallas kernels  10.2 us (20%)
  starting transfers between devices  7.13 us (14%)
  waiting for transfers between devices  5.16 us (10%)
  between operations  2 us (4%)
  other arithmetic  0.66 us (1%)
    all_to_all x1, blocking collectives, per_device(): shares = lax.all_to_all(parts, 'shot', 0, 0, tiled=True)  12.4 us
    all_gather x1, blocking collectives, per_device(): speeds = lax.all_gather(velocity, 'shot')  11.7 us
    ppermute x4, starting transfers between devices, swap_pairs(): return lax.ppermute(block, axis, route)  7.13 us
    ppermute x4, waiting for transfers between devices, swap_pairs(): return lax.ppermute(block, axis, route)  5.16 us
    pallas_call x1, Pallas kernels, late_steps(): pl.pallas_call(kernel, out_shape=(final, final, *same), in_specs=[smem] *...  3.85 us
    pallas_call x1, Pallas kernels, opening(): pl.pallas_call(opening_kernel, out_shape=(halo, halo, drops, band, buffer...  2.58 us
    pallas_call x1, Pallas kernels, early_steps(): pl.pallas_call(kernel, out_shape=(*same, waiting, parts), in_specs=[smem,...  2.23 us
    pallas_call x1, Pallas kernels, pack(): pl.pallas_call(packing_kernel, out_shape=(out, out), in_specs=[pl.BlockSp...  1.5 us
  transfers between devices with their start and end apart: 4, of which 3 were waited for; matrix products, arithmetic and copies ran while one was open for 0% of the time, Pallas kernels for 10%

profile of v4, /device:TPU:8, one launch (start us, length us, event | category | flops | bytes accessed | tf_op | source)
XLA Modules:
  0.0 49.3 jit_solution(3769590688998190839)
XLA Ops:
  0.6 1.5 %shard_map.131 = (f32[56,32,128]{2,1,0:T(8,128)S(1)}, f32[56,32,128]{2,1,0:T(8,128)S(1)}) custom-call(f32[1,16,32,128]{3,2,1,0:T(8,128)} %now_w.3, f32[1,16,32,128]{3,2,1,0:T(8,128)} %now_j.3, f32[1,16,32,128]{3,2,1,0:T(8,128)} %prev_w.3, f32[1,16,32,128]{3,2,1,0:T(8,128)} %prev_j.3), custom_call_target="tpu_custom_call" | custom-call | bytes 4194304 | tf_op jit(solution)/shard_map/pallas_call | solution.py:50
  2.1 0.1 collective-permute-start.2
  2.2 5.0 %collective-permute-start.3 = (f32[56,32,128]{2,1,0:T(8,128)S(1)}, f32[56,32,128]{2,1,0:T(8,128)S(1)}, u32[]{:S(2)}, u32[]{:S(2)}) collective-permute-start(f32[56,32,128]{2,1,0:T(8,128)S(1)} %get-tuple-element.28), channel_id=1, source_target_pairs={{1,2},{2,1},{5,6},{6,5},{9,10},{10,9},{13,14},{14,13},{17,18},{18,... | collective-permute-start | bytes 2752520 | tf_op jit(solution)/shard_map/ppermute | solution.py:21
  8.6 11.7 %all-gather = f32[128,8,128]{2,1,0:T(8,128)} all-gather(f32[16,8,128]{2,1,0:T(8,128)} %param.11), channel_id=2, replica_groups=mesh['shot'=8,'slab'=4] {'shot'}, dimensions={0}, use_global_device_ids=true | all-gather | bytes 589824 | tf_op jit(solution)/shard_map/all_gather | solution.py:496
  20.3 2.6 %shard_map.130 = (f32[4,12,8,128]{3,2,1,0:T(8,128)S(1)}, f32[4,12,8,128]{3,2,1,0:T(8,128)S(1)}, f32[4,2,48,8,128]{4,3,2,1,0:T(8,128)S(1)}, bf16[256,128]{1,0:T(8...) custom-call(s32[1]{0:T(128)S(6)} %copy.30.start.refs_0_, ...), custom_call_target="tpu_custom_call" | custom-call | flops 4194304 | bytes 4194304 | tf_op jit(solution)/shard_map/pallas_call | solution.py:213
  22.9 0.1 collective-permute-start
  23.0 2.0 %collective-permute-start.1 = (f32[4,12,8,128]{3,2,1,0:T(8,128)S(1)}, f32[4,12,8,128]{3,2,1,0:T(8,128)S(1)}, u32[]{:S(2)}, u32[]{:S(2)}) collective-permute-start(f32[4,12,8,128]{3,2,1,0:T(8,128)S(1)} %get-tuple-element.23), channel_id=1, source_target_pairs={{1,2},{2,1},{5,6},{6,5},{9,10},{10,9},{13,14},{14,13},{17,18},{18,... | collective-permute-start | bytes 589832 | tf_op jit(solution)/shard_map/ppermute | solution.py:21
  24.9 0.0 collective-permute-done.2.refs_1_
  25.0 2.4 %collective-permute-done.3.refs_2_ = f32[56,32,128]{2,1,0:T(8,128)S(1)} collective-permute-done((f32[56,32,128]{2,1,0:T(8,128)S(1)}, f32[56,32,128]{2,1,0:T(8,128)S(1)}, u32[]{:S(2)}, u32[]{:S(2)}) %collective-permute-start.3) | collective-permute-done | bytes 917536 | tf_op jit(solution)/shard_map/ppermute | solution.py:21
  27.3 2.2 %shard_map.132 = (f32[2,48,48,128]{3,2,1,0:T(8,128)S(1)}, f32[2,48,48,128]{3,2,1,0:T(8,128)S(1)}, f32[16,32,128]{2,1,0:T(8,128)S(1)}, f32[2,24,32,128]{3,2,1,0:T(8,128)S(1)}, f32[8,16,8,128]{3,2,1,0:T(8,128)S(1)}) custom-call(s32[1]{0:T(128)S(6)} %copy.31.count.refs_0_.refs_1_, ...), custom_call_target="tpu_custom_call", output_to_operand_aliasing={{0}: (6, {}), {1}: (7, {}), {2}: (8, {})} | custom-call | flops 20971520 | bytes 4194304 | tf_op jit(solution)/shard_map/pallas_call | solution.py:439
  29.6 0.9 %collective-permute-done.refs_2_ = f32[4,12,8,128]{3,2,1,0:T(8,128)S(1)} collective-permute-done((f32[4,12,8,128]{3,2,1,0:T(8,128)S(1)}, f32[4,12,8,128]{3,2,1,0:T(8,128)S(1)}, u32[]{:S(2)}, u32[]{:S(2)}) %collective-permute-start) | collective-permute-done | bytes 196640 | tf_op jit(solution)/shard_map/ppermute | solution.py:21
  30.4 1.9 %collective-permute-done.1.refs_3_ = f32[4,12,8,128]{3,2,1,0:T(8,128)S(1)} collective-permute-done((f32[4,12,8,128]{3,2,1,0:T(8,128)S(1)}, f32[4,12,8,128]{3,2,1,0:T(8,128)S(1)}, u32[]{:S(2)}, u32[]{:S(2)}) %collective-permute-start.1) | collective-permute-done | bytes 196640 | tf_op jit(solution)/shard_map/ppermute | solution.py:21
  32.4 3.9 %shard_map.133 = (f32[1,16,32,128]{3,2,1,0:T(8,128)}, f32[1,16,32,128]{3,2,1,0:T(8,128)}, f32[2,48,48,128]{3,2,1,0:T(8,128)S(1)}, f32[2,48,48,128]{3,2,1,0:T(8,1...) custom-call(s32[1]{0:T(128)S(6)} %copy.30.start.refs_0_, ...), custom_call_target="tpu_custom_call", output_to_operand_aliasing={{2}: (8, {}), {3}: (9, {}), {4}: (10, {}), {5}: (11, {}), {... | custom-call | flops 41943040 | bytes 6291456 | tf_op jit(solution)/shard_map/pallas_call | solution.py:460
  36.2 12.4 %all_to_all.5 = f32[8,16,8,128]{3,2,1,0:T(8,128)S(1)} all-to-all(f32[8,16,8,128]{3,2,1,0:T(8,128)S(1)} %get-tuple-element.40), channel_id=1, replica_groups=mesh['shot'=8,'slab'=4] {'shot'}, dimensions={0} | all-to-all | bytes 1048576 | tf_op jit(solution)/shard_map/all_to_all | solution.py:524
  48.7 0.7 %reduce_sum.9 = f32[16,8,128]{2,1,0:T(8,128)} reduce(f32[8,16,8,128]{3,2,1,0:T(8,128)S(1)} %all_to_all.5, f32[]{:T(128)} %constant.0.clone.1), dimensions={0}, to_apply=%region_0.0 | reduce | flops 114688 | bytes 589828 | tf_op jit(solution)/shard_map/reduce_sum | solution.py:525
Async XLA Ops:
  2.1 22.8 %collective-permute-start.2 = (f32[56,32,128]{2,1,0:T(8,128)S(1)}, f32[56,32,128]{2,1,0:T(8,128)S(1)}, u32[]{:S(2)}, u32[]{:S(2)}) collective-permute-start(f32[56,32,128]{2,1,0:T(8,128)S(1)} %get-tuple-element.27), channel_id=1, source_target_pairs={{0,1},{1,0},{2,3},{3,2},{4,5},{5,4},{6,7},{7,6},{8,9},{9,8},{10,11... | collective-permute-start | bytes 2752520 | tf_op jit(solution)/shard_map/ppermute | solution.py:21
  2.2 25.1 %collective-permute-start.3 = (f32[56,32,128]{2,1,0:T(8,128)S(1)}, f32[56,32,128]{2,1,0:T(8,128)S(1)}, u32[]{:S(2)}, u32[]{:S(2)}) collective-permute-start(f32[56,32,128]{2,1,0:T(8,128)S(1)} %get-tuple-element.28), channel_id=1, source_target_pairs={{1,2},{2,1},{5,6},{6,5},{9,10},{10,9},{13,14},{14,13},{17,18},{18,... | collective-permute-start | bytes 2752520 | tf_op jit(solution)/shard_map/ppermute | solution.py:21
  22.9 7.5 %collective-permute-start = (f32[4,12,8,128]{3,2,1,0:T(8,128)S(1)}, f32[4,12,8,128]{3,2,1,0:T(8,128)S(1)}, u32[]{:S(2)}, u32[]{:S(2)}) collective-permute-start(f32[4,12,8,128]{3,2,1,0:T(8,128)S(1)} %get-tuple-element.22), channel_id=1, source_target_pairs={{0,1},{1,0},{2,3},{3,2},{4,5},{5,4},{6,7},{7,6},{8,9},{9,8},{10,11... | collective-permute-start | bytes 589832 | tf_op jit(solution)/shard_map/ppermute | solution.py:21
  23.0 9.4 %collective-permute-start.1 = (f32[4,12,8,128]{3,2,1,0:T(8,128)S(1)}, f32[4,12,8,128]{3,2,1,0:T(8,128)S(1)}, u32[]{:S(2)}, u32[]{:S(2)}) collective-permute-start(f32[4,12,8,128]{3,2,1,0:T(8,128)S(1)} %get-tuple-element.23), channel_id=1, source_target_pairs={{1,2},{2,1},{5,6},{6,5},{9,10},{10,9},{13,14},{14,13},{17,18},{18,... | collective-permute-start | bytes 589832 | tf_op jit(solution)/shard_map/ppermute | solution.py:21

commit v5 on v4

--- a/solution.py
+++ b/solution.py
@@ -94,26 +94,21 @@
     cells_j,
     amps_w,
     amps_j,
-    model,
     sems,
 ):
     cells, rows, depth = image.shape
-    tiles, deep_prev = to_a.shape[:2]
+    tiles = rows // TILE
+    steps = drops.shape[0]
+    deep = steps * REACH
+    near = deep - 2 * REACH
     wide = drops.shape[2]
-    steps = drops.shape[0]
-    deep = deep_prev + REACH
     slab = lax.axis_index("slab")
     odd = slab % 2
     start_block = start[0]
     live = count[0]
     copies, bring = bringing(sems)
-    for out, side in ((to_a, 1 - odd), (to_b, odd)):
-        for tile in range(tiles):
-            bring(speeds.at[start_block + tile, pl.ds(side * (cells - deep_prev), deep_prev)], out.at[tile])
     for source, target in ((cells_w_in, cells_w), (cells_j_in, cells_j), (amps_w_in, amps_w), (amps_j_in, amps_j)):
         bring(source, target)
-    for tile in range(tiles):
-        bring(speeds.at[start_block + tile], model.at[tile])
     inner = pl.ds(TILE, rows)
     for field, (now, prev) in enumerate(((now_w, prev_w), (now_j, prev_j))):
         bring(now.at[0], one.at[field, pl.ds(deep, cells), inner])
@@ -138,7 +133,24 @@
         matrix = jnp.where((away == k) | (away == -k), scaled_weights[k], matrix)
     band[pl.ds(0, depth), :] = matrix.astype(jnp.bfloat16)
     band[pl.ds(depth, depth), :] = matrix.astype(jnp.bfloat16)
-    for copy in copies:
+
+    def factors(x, carry):
+        for tile in range(tiles):
+            alive = jnp.where(tile < live, time_step * time_step / SCALE, 0.0)
+            speed = speeds[start_block + tile, x]
+            at = pl.ds(tile * TILE, TILE)
+            courant[deep + x, at, :] = alive * (speed * speed)
+            image[x, at, :] = (2.0 * time_step * time_step / SCALE) * speed
+        return carry
+
+    lax.fori_loop(0, cells, factors, 0, unroll=4)
+
+    for out, side in ((to_a, 1 - odd), (to_b, odd)):
+        for layer in range(near):
+            for tile in range(tiles):
+                speed = speeds[start_block + tile, side * (cells - near) + layer]
+                out[layer, pl.ds(tile * TILE, TILE), :] = speed
+    for copy in copies[:4]:
         copy.wait()
 
     row = lax.broadcasted_iota(jnp.int32, (TILE, depth), 0)
@@ -161,16 +173,8 @@
     inject(0, cells_w, amps_w)
     inject(1, cells_j, amps_j)
 
-    def factors(x, carry):
-        for tile in range(tiles):
-            alive = jnp.where(tile < live, time_step * time_step / SCALE, 0.0)
-            speed = model[tile, x]
-            at = pl.ds(tile * TILE, TILE)
-            courant[deep + x, at, :] = alive * (speed * speed)
-            image[x, at, :] = (2.0 * time_step * time_step / SCALE) * speed
-        return carry
-
-    lax.fori_loop(0, cells, factors, 0)
+    for copy in copies[4:]:
+        copy.wait()
     clear_dead(one, two, live, deep, deep + cells)
 
     def core(c, carry):
@@ -178,6 +182,11 @@
         return carry
 
     lax.fori_loop(0, cells // REACH - 2, core, 0, unroll=2)
+    for out, side in ((to_a, 1 - odd), (to_b, odd)):
+        for field in range(2):
+            for i in range(REACH):
+                x = deep + REACH + (1 - side) * (cells - 3 * REACH) + i
+                out[near + field * REACH + i] = two[field, x, inner, :]
 
 
 def clear_dead(one, two, live, first, last):
@@ -198,12 +207,11 @@
 
 
 def opening(start, count, small, fields, speeds, steps):
-    groups, cells, _, depth = speeds.shape
+    cells, depth = speeds.shape[1], speeds.shape[3]
     rows = fields[0].shape[2]
-    tiles = rows // TILE
     deep = steps * REACH
     wide = cells + 2 * deep
-    halo = pltpu.VMEM((tiles, deep - REACH, TILE, depth), jnp.float32)
+    halo = pltpu.VMEM((deep, rows, depth), jnp.float32)
     drops = pltpu.VMEM((steps, 2, wide, TILE, depth), jnp.float32)
     band = pltpu.VMEM((2 * depth, depth), jnp.bfloat16)
     buffer = pltpu.VMEM((2, wide, rows + 2 * TILE, depth), jnp.float32)
@@ -213,16 +221,13 @@
     return pl.pallas_call(
         opening_kernel,
         out_shape=(halo, halo, drops, band, buffer, buffer, courant, layers, layers),
-        in_specs=[pl.BlockSpec(memory_space=pltpu.SMEM)] * 2 + [pl.BlockSpec(memory_space=pltpu.HBM)] * 9,
+        in_specs=[pl.BlockSpec(memory_space=pltpu.SMEM)] * 2 + [pl.BlockSpec(memory_space=pltpu.HBM)] * 8 + [vmem],
         out_specs=(vmem,) * 9,
         scratch_shapes=[pltpu.SMEM(array.shape, array.dtype) for array in small]
-        + [
-            pltpu.VMEM((tiles, cells, TILE, depth), jnp.float32),
-            pltpu.SemaphoreType.DMA((3 * tiles + 8,)),
-        ],
+        + [pltpu.SemaphoreType.DMA((8,))],
         compiler_params=pltpu.CompilerParams(vmem_limit_bytes=8 << 20),
         cost_estimate=pl.CostEstimate(flops=4 << 20, bytes_accessed=4 << 20, transcendentals=0),
-    )(start, count, *map(in_hbm, small), *map(in_hbm, fields), in_hbm(speeds))
+    )(start, count, *map(in_hbm, small), *map(in_hbm, fields), speeds)
 
 
 def along_z(now, band, x):
@@ -235,51 +240,54 @@
     return jnp.dot(jnp.concatenate([high, low], axis=1), band[...], preferred_element_type=jnp.float32)
 
 
-def laplacian(now, spread, field, i, x):
+def each_tile(now, band, x_first, visit):
     rows = now.shape[2] - 2 * TILE
-    inner = pl.ds(TILE, rows)
-    center = now[field, x, inner, :]
-    lap = (3.0 * scaled_weights[0]) * center
-    for k in range(1, REACH + 1):
-        near = now[field, x + k, inner, :] + now[field, x - k, inner, :]
-        near = near + now[field, x, pl.ds(TILE + k, rows), :]
-        near = near + now[field, x, pl.ds(TILE - k, rows), :]
-        lap = lap + scaled_weights[k] * near
-    at = (field * REACH + i) * rows
-    return center, lap + spread[at : at + rows]
-
-
-def store_layer(buffer, field, x, values, drop):
-    rows = values.shape[0]
-    buffer[field, x, pl.ds(TILE, TILE), :] = values[:TILE] + drop
-    buffer[field, x, pl.ds(2 * TILE, rows - TILE), :] = values[TILE:]
+    spread = along_z(now, band, x_first)
+    for tile in range(rows // TILE):
+        at = TILE + tile * TILE
+        pairs = []
+        for field in range(2):
+            line = [now[field, x_first + i, pl.ds(at, TILE), :] for i in range(-REACH, 2 * REACH)]
+            for i in range(REACH):
+                center = line[REACH + i]
+                lap = (3.0 * scaled_weights[0]) * center
+                for k in range(1, REACH + 1):
+                    near = line[REACH + i + k] + line[REACH + i - k]
+                    near = near + now[field, x_first + i, pl.ds(at + k, TILE), :]
+                    near = near + now[field, x_first + i, pl.ds(at - k, TILE), :]
+                    lap = lap + scaled_weights[k] * near
+                row = (field * REACH + i) * rows + tile * TILE
+                pairs.append((center, lap + spread[row : row + TILE]))
+        for i in range(REACH):
+            visit(tile, i, (pairs[i], pairs[REACH + i]))
 
 
 def advance(now, other, courant, drops, band, step, x_first, grad, fresh, deep, finals=None):
-    rows = now.shape[2] - 2 * TILE
-    inner = pl.ds(TILE, rows)
-    spread = along_z(now, band, x_first)
-    for i in range(REACH):
+    def visit(tile, i, pair):
         x = x_first + i
-        pair = []
-        for field in range(2):
-            center, lap = laplacian(now, spread, field, i, x)
-            pair.append((center, lap))
-            ahead = 2.0 * center - other[field, x, inner, :] + courant[x] * lap
+        own = pl.ds(tile * TILE, TILE)
+        padded = pl.ds(TILE + tile * TILE, TILE)
+        factor = courant[x, own, :]
+        for field, (center, lap) in enumerate(pair):
+            ahead = 2.0 * center - other[field, x, padded, :] + factor * lap
+            if tile == 0:
+                ahead = ahead + drops[step, field, x]
             if finals is None:
-                store_layer(other, field, x, ahead, drops[step, field, x])
+                other[field, x, padded, :] = ahead
             else:
-                finals[field, x - deep, pl.ds(0, TILE), :] = ahead[:TILE] + drops[step, field, x]
-                finals[field, x - deep, pl.ds(TILE, rows - TILE), :] = ahead[TILE:]
+                finals[field, x - deep, own, :] = ahead
         if grad is not None:
             term = pair[1][0] * pair[0][1]
-            grad[x - deep] = term if fresh else grad[x - deep] + term
+            grad[x - deep, own, :] = term if fresh else grad[x - deep, own, :] + term
+
+    each_tile(now, band, x_first, visit)
 
 
 def early_kernel(steps, count, from_a, from_b, courant, drops, band, one_in, two_in, grad_in, one, two, grad, waiting, parts, sems):
     cells, rows, depth = grad.shape
     deep = steps * REACH
-    deep_prev = deep - REACH
+    near = deep - 2 * REACH
+    held = near + REACH
     wide = cells + 2 * deep
     odd = lax.axis_index("slab") % 2
 
@@ -288,13 +296,10 @@
     inner = pl.ds(TILE, rows)
     for field in range(2):
         for buffer, on_left in ((from_a, left_of_a), (from_b, 1 - left_of_a)):
-            at = (1 - on_left) * (deep + cells)
-            bring(buffer.at[pl.ds(field * deep, deep)], one.at[field, pl.ds(at, deep), inner])
-            at = on_left * REACH + (1 - on_left) * (deep + cells)
-            bring(
-                buffer.at[pl.ds(2 * deep + field * deep_prev, deep_prev)],
-                two.at[field, pl.ds(at, deep_prev), inner],
-            )
+            at = on_left * (deep - held) + (1 - on_left) * (deep + cells)
+            bring(buffer.at[pl.ds(field * held, held)], one.at[field, pl.ds(at, held), inner])
+            at = on_left * (deep - near) + (1 - on_left) * (deep + cells)
+            bring(buffer.at[pl.ds(2 * held + field * near, near)], two.at[field, pl.ds(at, near), inner])
     def clear_parts(b, carry):
         parts[b] = jnp.zeros(parts.shape[1:], jnp.float32)
         return carry
@@ -305,17 +310,20 @@
     clear_dead(one, two, count[0], 0, deep)
     clear_dead(one, two, count[0], deep + cells, wide)
 
-    half = deep_prev // REACH
+    half = near // REACH
 
     def outside(c, carry):
-        x_first = REACH + c * REACH + jnp.where(c >= half, cells, 0)
-        spread = along_z(one, band, x_first)
-        for i in range(REACH):
+        x_first = deep - near + c * REACH + jnp.where(c >= half, cells, 0)
+
+        def visit(tile, i, pair):
             x = x_first + i
-            for field in range(2):
-                center, lap = laplacian(one, spread, field, i, x)
-                waiting[field, c * REACH + i] = lap
-                store_layer(two, field, x, 2.0 * center - two[field, x, inner, :], drops[0, field, x])
+            padded = pl.ds(TILE + tile * TILE, TILE)
+            for field, (center, lap) in enumerate(pair):
+                waiting[field, c * REACH + i, pl.ds(tile * TILE, TILE), :] = lap
+                ahead = 2.0 * center - two[field, x, padded, :]
+                two[field, x, padded, :] = ahead + drops[0, field, x] if tile == 0 else ahead
+
+        each_tile(one, band, x_first, visit)
         return carry
 
     def inside(c, carry):
@@ -335,8 +343,8 @@
     steps,
     start,
     count,
-    speed_a,
-    speed_b,
+    next_a,
+    next_b,
     drops,
     band,
     image,
@@ -358,32 +366,38 @@
 ):
     cells, rows, depth = image.shape
     deep = steps * REACH
-    deep_prev = deep - REACH
+    near = deep - 2 * REACH
     tiles = rows // TILE
     odd = lax.axis_index("slab") % 2
     start_block = start[0]
     live = count[0]
-    inner = pl.ds(TILE, rows)
 
     copies, bring = bringing(sems)
 
     def finish(h, carry):
-        right = h >= deep_prev
-        layer = jnp.where(right, h - deep_prev, h)
-        x = jnp.where(right, deep + cells, REACH) + layer
+        right = h >= near
+        layer = jnp.where(right, h - near, h)
+        x = jnp.where(right, deep + cells, deep - near) + layer
         use_a = jnp.where(right, 1 - odd, odd) == 1
         for tile in range(tiles):
             alive = jnp.where(tile < live, time_step * time_step / SCALE, 0.0)
-            speed = jnp.where(use_a, speed_a[tile, layer], speed_b[tile, layer])
+            own = pl.ds(tile * TILE, TILE)
+            speed = jnp.where(use_a, next_a[layer, own, :], next_b[layer, own, :])
             factor = alive * (speed * speed)
-            courant[x, pl.ds(tile * TILE, TILE), :] = factor
+            courant[x, own, :] = factor
             for field in range(2):
                 at = pl.ds(TILE + tile * TILE, TILE)
-                change = factor * waiting[field, h, pl.ds(tile * TILE, TILE), :]
+                change = factor * waiting[field, h, own, :]
                 two[field, x, at, :] = two[field, x, at, :] + change
         return carry
 
-    lax.fori_loop(0, 2 * deep_prev, finish, 0, unroll=4)
+    lax.fori_loop(0, 2 * near, finish, 0, unroll=4)
+    inner = pl.ds(TILE, rows)
+    for message, left in ((next_a, odd), (next_b, 1 - odd)):
+        for field in range(2):
+            for i in range(REACH):
+                x = left * (deep - near - REACH) + (1 - left) * (deep + cells + near) + i
+                two[field, x, inner, :] = message[near + field * REACH + i]
 
     now, other = two, one
     for step in range(1, steps):
@@ -426,8 +440,7 @@
 
 def early_steps(steps, count, from_a, from_b, courant, drops, band, one, two, grad, groups):
     cells, rows, depth = grad.shape
-    deep_prev = (steps - 1) * REACH
-    waiting = pltpu.VMEM((2, 2 * deep_prev, rows, depth), jnp.float32)
+    waiting = pltpu.VMEM((2, 2 * (steps - 2) * REACH, rows, depth), jnp.float32)
     parts = pltpu.VMEM((groups, cells, TILE, depth), jnp.float32)
     smem = pl.BlockSpec(memory_space=pltpu.SMEM)
     vmem = pl.BlockSpec(memory_space=pltpu.VMEM)
@@ -448,7 +461,7 @@
     )(count, from_a, from_b, courant, drops, band, one, two, grad)
 
 
-def late_steps(steps, start, count, speed_a, speed_b, drops, band, image, waiting, one, two, courant, grad, parts):
+def late_steps(steps, start, count, next_a, next_b, drops, band, image, waiting, one, two, courant, grad, parts):
     smem = pl.BlockSpec(memory_space=pltpu.SMEM)
     vmem = pl.BlockSpec(memory_space=pltpu.VMEM)
     final = jax.ShapeDtypeStruct((1, *image.shape), jnp.float32)
@@ -469,7 +482,7 @@
         ],
         compiler_params=pltpu.CompilerParams(vmem_limit_bytes=8 << 20),
         cost_estimate=pl.CostEstimate(flops=40 << 20, bytes_accessed=6 << 20, transcendentals=0),
-    )(start, count, speed_a, speed_b, drops, band, image, waiting, one, two, courant, grad, parts)
+    )(start, count, next_a, next_b, drops, band, image, waiting, one, two, courant, grad, parts)
     return results[0], results[1], results[6]
 
 
@@ -490,7 +503,7 @@
     deep = steps * REACH
     fields = (wave_now, adjoint_now, wave_prev, adjoint_prev)
 
-    to_a, to_b = pack(fields, deep)
+    to_a, to_b = pack(fields, deep - REACH)
     from_a = swap_pairs(to_a, "slab", 0)
     from_b = swap_pairs(to_b, "slab", 1)
     speeds = lax.all_gather(velocity, "shot")
@@ -500,8 +513,8 @@
     to_a, to_b, drops, band, one, two, courant, image, grad = opening(
         aperture_start, aperture_count, small, fields, speeds, steps
     )
-    speed_a = swap_pairs(to_a, "slab", 0)
-    speed_b = swap_pairs(to_b, "slab", 1)
+    next_a = swap_pairs(to_a, "slab", 0)
+    next_b = swap_pairs(to_b, "slab", 1)
     one, two, grad, waiting, parts = early_steps(
         steps, aperture_count, from_a, from_b, courant, drops, band, one, two, grad, lax.axis_size("shot")
     )
@@ -509,8 +522,8 @@
         steps,
         aperture_start,
         aperture_count,
-        speed_a,
-        speed_b,
+        next_a,
+        next_b,
         drops,
         band,
         image,

time: 49.8 us -> 48.1 us (0.966)
  blocking collectives: 24.2 us -> 22.4 us
  waiting for transfers between devices: 5.16 us -> 6.74 us
  Pallas kernels: 10.2 us -> 8.93 us
    all_gather x1, blocking collectives: 11.7 us -> 10.2 us  [per_device(): speeds = lax.all_gather(velocity, 'shot')]
    ppermute x4, waiting for transfers between devices: 5.16 us -> 6.74 us  [swap_pairs(): return lax.ppermute(block, axis, route)]
    pallas_call x1, Pallas kernels: 2.58 us -> 1.7 us  [opening(): pl.pallas_call(opening_kernel, out_shape=(halo, halo, drops, band, buffer...]
  transfers between devices with their start and end apart: 4 -> 4, of which waited for: 3 -> 2; matrix products, arithmetic and copies ran while one was open for 0% -> 0% of each run, Pallas kernels for 10% -> 8%
where the time goes in v5:
time: 48.1 us; the launch traced here: 47.8 us
  blocking collectives  22.4 us (47%)
  Pallas kernels  8.93 us (19%)
  starting transfers between devices  7.1 us (15%)
  waiting for transfers between devices  6.74 us (14%)
  between operations  2.01 us (4%)
  other arithmetic  0.66 us (1%)
    all_to_all x1, blocking collectives, per_device(): shares = lax.all_to_all(parts, 'shot', 0, 0, tiled=True)  12.2 us
    all_gather x1, blocking collectives, per_device(): speeds = lax.all_gather(velocity, 'shot')  10.2 us
    ppermute x4, starting transfers between devices, swap_pairs(): return lax.ppermute(block, axis, route)  7.1 us
    ppermute x4, waiting for transfers between devices, swap_pairs(): return lax.ppermute(block, axis, route)  6.74 us
    pallas_call x1, Pallas kernels, late_steps(): pl.pallas_call(kernel, out_shape=(final, final, *same), in_specs=[smem] *...  3.87 us
    pallas_call x1, Pallas kernels, early_steps(): pl.pallas_call(kernel, out_shape=(*same, waiting, parts), in_specs=[smem,...  1.92 us
    pallas_call x1, Pallas kernels, opening(): pl.pallas_call(opening_kernel, out_shape=(halo, halo, drops, band, buffer...  1.7 us
    pallas_call x1, Pallas kernels, pack(): pl.pallas_call(packing_kernel, out_shape=(out, out), in_specs=[pl.BlockSp...  1.45 us
  transfers between devices with their start and end apart: 4, of which 2 were waited for; matrix products, arithmetic and copies ran while one was open for 0% of the time, Pallas kernels for 8%

profile of v5, /device:TPU:8, one launch (start us, length us, event | category | flops | bytes accessed | tf_op | source)
XLA Modules:
  0.0 47.8 jit_solution(12741364702633024433)
XLA Ops:
  0.6 1.4 %shard_map.131 = (f32[40,32,128]{2,1,0:T(8,128)S(1)}, f32[40,32,128]{2,1,0:T(8,128)S(1)}) custom-call(f32[1,16,32,128]{3,2,1,0:T(8,128)} %now_w.3, f32[1,16,32,128]{3,2,1,0:T(8,128)} %now_j.3, f32[1,16,32,128]{3,2,1,0:T(8,128)} %prev_w.3, f32[1,16,32,128]{3,2,1,0:T(8,128)} %prev_j.3), custom_call_target="tpu_custom_call" | custom-call | bytes 4194304 | tf_op jit(solution)/shard_map/pallas_call | solution.py:50
  2.1 0.1 collective-permute-start.2
  2.2 5.0 %collective-permute-start.3 = (f32[40,32,128]{2,1,0:T(8,128)S(1)}, f32[40,32,128]{2,1,0:T(8,128)S(1)}, u32[]{:S(2)}, u32[]{:S(2)}) collective-permute-start(f32[40,32,128]{2,1,0:T(8,128)S(1)} %get-tuple-element.28), channel_id=1, source_target_pairs={{1,2},{2,1},{5,6},{6,5},{9,10},{10,9},{13,14},{14,13},{17,18},{18,... | collective-permute-start | bytes 1966088 | tf_op jit(solution)/shard_map/ppermute | solution.py:21
  8.5 10.2 %all-gather = f32[128,8,128]{2,1,0:T(8,128)S(1)} all-gather(f32[16,8,128]{2,1,0:T(8,128)} %param.11), channel_id=2, replica_groups=mesh['shot'=8,'slab'=4] {'shot'}, dimensions={0}, use_global_device_ids=true | all-gather | bytes 589824 | tf_op jit(solution)/shard_map/all_gather | solution.py:509
  18.7 1.7 %shard_map.130 = (f32[16,32,128]{2,1,0:T(8,128)S(1)}, f32[16,32,128]{2,1,0:T(8,128)S(1)}, f32[4,2,48,8,128]{4,3,2,1,0:T(8,128)S(1)}, bf16[256,128]{1,0:T(8,128)(...) custom-call(s32[1]{0:T(128)S(6)} %copy.30.start.refs_0_, ...), custom_call_target="tpu_custom_call" | custom-call | flops 4194304 | bytes 4194304 | tf_op jit(solution)/shard_map/pallas_call | solution.py:221
  20.4 0.1 collective-permute-start
  20.4 1.9 %collective-permute-start.1 = (f32[16,32,128]{2,1,0:T(8,128)S(1)}, f32[16,32,128]{2,1,0:T(8,128)S(1)}, u32[]{:S(2)}, u32[]{:S(2)}) collective-permute-start(f32[16,32,128]{2,1,0:T(8,128)S(1)} %get-tuple-element.23), channel_id=1, source_target_pairs={{1,2},{2,1},{5,6},{6,5},{9,10},{10,9},{13,14},{14,13},{17,18},{18,... | collective-permute-start | bytes 786440 | tf_op jit(solution)/shard_map/ppermute | solution.py:21
  22.4 0.0 collective-permute-done.2.refs_1_
  22.4 0.0 collective-permute-done.3.refs_2_
  22.4 1.9 %shard_map.132 = (f32[2,48,48,128]{3,2,1,0:T(8,128)S(1)}, f32[2,48,48,128]{3,2,1,0:T(8,128)S(1)}, f32[16,32,128]{2,1,0:T(8,128)S(1)}, f32[2,16,32,128]{3,2,1,0:T(8,128)S(1)}, f32[8,16,8,128]{3,2,1,0:T(8,128)S(1)}) custom-call(s32[1]{0:T(128)S(6)} %copy.31.count.refs_0_.refs_1_, ...), custom_call_target="tpu_custom_call", output_to_operand_aliasing={{0}: (6, {}), {1}: (7, {}), {2}: (8, {})} | custom-call | flops 20971520 | bytes 4194304 | tf_op jit(solution)/shard_map/pallas_call | solution.py:452
  24.3 4.8 %collective-permute-done.refs_2_ = f32[16,32,128]{2,1,0:T(8,128)S(1)} collective-permute-done((f32[16,32,128]{2,1,0:T(8,128)S(1)}, f32[16,32,128]{2,1,0:T(8,128)S(1)}, u32[]{:S(2)}, u32[]{:S(2)}) %collective-permute-start) | collective-permute-done | bytes 262176 | tf_op jit(solution)/shard_map/ppermute | solution.py:21
  29.1 1.9 %collective-permute-done.1.refs_3_ = f32[16,32,128]{2,1,0:T(8,128)S(1)} collective-permute-done((f32[16,32,128]{2,1,0:T(8,128)S(1)}, f32[16,32,128]{2,1,0:T(8,128)S(1)}, u32[]{:S(2)}, u32[]{:S(2)}) %collective-permute-start.1) | collective-permute-done | bytes 262176 | tf_op jit(solution)/shard_map/ppermute | solution.py:21
  31.1 3.9 %shard_map.133 = (f32[1,16,32,128]{3,2,1,0:T(8,128)}, f32[1,16,32,128]{3,2,1,0:T(8,128)}, f32[2,48,48,128]{3,2,1,0:T(8,128)S(1)}, f32[2,48,48,128]{3,2,1,0:T(8,1...) custom-call(s32[1]{0:T(128)S(6)} %copy.30.start.refs_0_, ...), custom_call_target="tpu_custom_call", output_to_operand_aliasing={{2}: (8, {}), {3}: (9, {}), {4}: (10, {}), {5}: (11, {}), {... | custom-call | flops 41943040 | bytes 6291456 | tf_op jit(solution)/shard_map/pallas_call | solution.py:473
  34.9 12.2 %all_to_all.5 = f32[8,16,8,128]{3,2,1,0:T(8,128)S(1)} all-to-all(f32[8,16,8,128]{3,2,1,0:T(8,128)S(1)} %get-tuple-element.40), channel_id=1, replica_groups=mesh['shot'=8,'slab'=4] {'shot'}, dimensions={0} | all-to-all | bytes 1048576 | tf_op jit(solution)/shard_map/all_to_all | solution.py:537
  47.1 0.7 %reduce_sum.9 = f32[16,8,128]{2,1,0:T(8,128)} reduce(f32[8,16,8,128]{3,2,1,0:T(8,128)S(1)} %all_to_all.5, f32[]{:T(128)} %constant.0.clone.1), dimensions={0}, to_apply=%region_0.0 | reduce | flops 114688 | bytes 589828 | tf_op jit(solution)/shard_map/reduce_sum | solution.py:538
Async XLA Ops:
  2.1 20.3 %collective-permute-start.2 = (f32[40,32,128]{2,1,0:T(8,128)S(1)}, f32[40,32,128]{2,1,0:T(8,128)S(1)}, u32[]{:S(2)}, u32[]{:S(2)}) collective-permute-start(f32[40,32,128]{2,1,0:T(8,128)S(1)} %get-tuple-element.27), channel_id=1, source_target_pairs={{0,1},{1,0},{2,3},{3,2},{4,5},{5,4},{6,7},{7,6},{8,9},{9,8},{10,11... | collective-permute-start | bytes 1966088 | tf_op jit(solution)/shard_map/ppermute | solution.py:21
  2.2 20.2 %collective-permute-start.3 = (f32[40,32,128]{2,1,0:T(8,128)S(1)}, f32[40,32,128]{2,1,0:T(8,128)S(1)}, u32[]{:S(2)}, u32[]{:S(2)}) collective-permute-start(f32[40,32,128]{2,1,0:T(8,128)S(1)} %get-tuple-element.28), channel_id=1, source_target_pairs={{1,2},{2,1},{5,6},{6,5},{9,10},{10,9},{13,14},{14,13},{17,18},{18,... | collective-permute-start | bytes 1966088 | tf_op jit(solution)/shard_map/ppermute | solution.py:21
  20.4 8.8 %collective-permute-start = (f32[16,32,128]{2,1,0:T(8,128)S(1)}, f32[16,32,128]{2,1,0:T(8,128)S(1)}, u32[]{:S(2)}, u32[]{:S(2)}) collective-permute-start(f32[16,32,128]{2,1,0:T(8,128)S(1)} %get-tuple-element.22), channel_id=1, source_target_pairs={{0,1},{1,0},{2,3},{3,2},{4,5},{5,4},{6,7},{7,6},{8,9},{9,8},{10,11... | collective-permute-start | bytes 786440 | tf_op jit(solution)/shard_map/ppermute | solution.py:21
  20.4 10.6 %collective-permute-start.1 = (f32[16,32,128]{2,1,0:T(8,128)S(1)}, f32[16,32,128]{2,1,0:T(8,128)S(1)}, u32[]{:S(2)}, u32[]{:S(2)}) collective-permute-start(f32[16,32,128]{2,1,0:T(8,128)S(1)} %get-tuple-element.23), channel_id=1, source_target_pairs={{1,2},{2,1},{5,6},{6,5},{9,10},{10,9},{13,14},{14,13},{17,18},{18,... | collective-permute-start | bytes 786440 | tf_op jit(solution)/shard_map/ppermute | solution.py:21

commit v6 on v5

--- a/solution.py
+++ b/solution.py
@@ -177,11 +177,8 @@
         copy.wait()
     clear_dead(one, two, live, deep, deep + cells)
 
-    def core(c, carry):
-        advance(one, two, courant, drops, band, 0, deep + REACH + c * REACH, grad, True, deep)
-        return carry
-
-    lax.fori_loop(0, cells // REACH - 2, core, 0, unroll=2)
+    for groups in paired(range(deep + REACH, deep + cells - REACH, REACH)):
+        advance(one, two, courant, drops, band, 0, groups, grad, True, deep)
     for out, side in ((to_a, 1 - odd), (to_b, odd)):
         for field in range(2):
             for i in range(REACH):
@@ -230,41 +227,40 @@
     )(start, count, *map(in_hbm, small), *map(in_hbm, fields), speeds)
 
 
-def along_z(now, band, x):
+def along_z(now, band, field, x):
     rows, depth = now.shape[2] - 2 * TILE, now.shape[3]
-    inner = pl.ds(TILE, rows)
-    fields = [now[field, pl.ds(x, REACH), inner, :].reshape(REACH * rows, depth) for field in range(2)]
-    cells = jnp.concatenate(fields, axis=0)
+    cells = now[field, pl.ds(x, REACH), pl.ds(TILE, rows), :].reshape(REACH * rows, depth)
     high = cells.astype(jnp.bfloat16)
     low = (cells - high.astype(jnp.float32)).astype(jnp.bfloat16)
     return jnp.dot(jnp.concatenate([high, low], axis=1), band[...], preferred_element_type=jnp.float32)
 
 
-def each_tile(now, band, x_first, visit):
+def each_tile(now, band, groups, visit):
     rows = now.shape[2] - 2 * TILE
-    spread = along_z(now, band, x_first)
-    for tile in range(rows // TILE):
-        at = TILE + tile * TILE
-        pairs = []
-        for field in range(2):
-            line = [now[field, x_first + i, pl.ds(at, TILE), :] for i in range(-REACH, 2 * REACH)]
+    spreads = [[along_z(now, band, field, x_first) for field in range(2)] for x_first in groups]
+    for g, x_first in enumerate(groups):
+        for tile in range(rows // TILE):
+            at = TILE + tile * TILE
+            pairs = []
+            for field in range(2):
+                line = [now[field, x_first + i, pl.ds(at, TILE), :] for i in range(-REACH, 2 * REACH)]
+                for i in range(REACH):
+                    center = line[REACH + i]
+                    lap = (3.0 * scaled_weights[0]) * center
+                    for k in range(1, REACH + 1):
+                        near = line[REACH + i + k] + line[REACH + i - k]
+                        near = near + now[field, x_first + i, pl.ds(at + k, TILE), :]
+                        near = near + now[field, x_first + i, pl.ds(at - k, TILE), :]
+                        lap = lap + scaled_weights[k] * near
+                    row = i * rows + tile * TILE
+                    pairs.append((center, lap + spreads[g][field][row : row + TILE]))
             for i in range(REACH):
-                center = line[REACH + i]
-                lap = (3.0 * scaled_weights[0]) * center
-                for k in range(1, REACH + 1):
-                    near = line[REACH + i + k] + line[REACH + i - k]
-                    near = near + now[field, x_first + i, pl.ds(at + k, TILE), :]
-                    near = near + now[field, x_first + i, pl.ds(at - k, TILE), :]
-                    lap = lap + scaled_weights[k] * near
-                row = (field * REACH + i) * rows + tile * TILE
-                pairs.append((center, lap + spread[row : row + TILE]))
-        for i in range(REACH):
-            visit(tile, i, (pairs[i], pairs[REACH + i]))
-
-
-def advance(now, other, courant, drops, band, step, x_first, grad, fresh, deep, finals=None):
-    def visit(tile, i, pair):
-        x = x_first + i
+                visit(g, tile, i, (pairs[i], pairs[REACH + i]))
+
+
+def advance(now, other, courant, drops, band, step, groups, grad, fresh, deep, finals=None):
+    def visit(g, tile, i, pair):
+        x = groups[g] + i
         own = pl.ds(tile * TILE, TILE)
         padded = pl.ds(TILE + tile * TILE, TILE)
         factor = courant[x, own, :]
@@ -280,7 +276,7 @@
             term = pair[1][0] * pair[0][1]
             grad[x - deep, own, :] = term if fresh else grad[x - deep, own, :] + term
 
-    each_tile(now, band, x_first, visit)
+    each_tile(now, band, groups, visit)
 
 
 def early_kernel(steps, count, from_a, from_b, courant, drops, band, one_in, two_in, grad_in, one, two, grad, waiting, parts, sems):
@@ -310,33 +306,29 @@
     clear_dead(one, two, count[0], 0, deep)
     clear_dead(one, two, count[0], deep + cells, wide)
 
-    half = near // REACH
-
     def outside(c, carry):
-        x_first = deep - near + c * REACH + jnp.where(c >= half, cells, 0)
-
-        def visit(tile, i, pair):
-            x = x_first + i
+        groups = [deep - near + c * (near + cells) + i for i in range(0, near, REACH)]
+
+        def visit(g, tile, i, pair):
+            x = groups[g] + i
             padded = pl.ds(TILE + tile * TILE, TILE)
             for field, (center, lap) in enumerate(pair):
-                waiting[field, c * REACH + i, pl.ds(tile * TILE, TILE), :] = lap
+                waiting[field, c * near + g * REACH + i, pl.ds(tile * TILE, TILE), :] = lap
                 ahead = 2.0 * center - two[field, x, padded, :]
                 two[field, x, padded, :] = ahead + drops[0, field, x] if tile == 0 else ahead
 
-        each_tile(one, band, x_first, visit)
+        each_tile(one, band, groups, visit)
         return carry
 
-    def inside(c, carry):
-        advance(one, two, courant, drops, band, 0, deep + c * (cells - REACH), grad, True, deep)
-        return carry
-
-    def core(c, carry):
-        advance(two, one, courant, drops, band, 1, deep + REACH + c * REACH, grad, False, deep)
-        return carry
-
-    lax.fori_loop(0, 2, inside, 0, unroll=2)
-    lax.fori_loop(0, 2 * half, outside, 0, unroll=2)
-    lax.fori_loop(0, cells // REACH - 2, core, 0, unroll=2)
+    advance(one, two, courant, drops, band, 0, [deep, deep + cells - REACH], grad, True, deep)
+    lax.fori_loop(0, 2, outside, 0)
+    for groups in paired(range(deep + REACH, deep + cells - REACH, REACH)):
+        advance(two, one, courant, drops, band, 1, groups, grad, False, deep)
+
+
+def paired(starts):
+    starts = list(starts)
+    return [starts[i : i + 2] for i in range(0, len(starts), 2)]
 
 
 def late_kernel(
@@ -401,28 +393,17 @@
 
     now, other = two, one
     for step in range(1, steps):
-        margin = REACH * (step + 1)
-        half = (deep - margin) // REACH
-
-        def outside(c, carry):
-            x = margin + c * REACH + jnp.where(c >= half, cells, 0)
-            advance(now, other, courant, drops, band, step, x, None, False, deep)
-            return carry
-
-        stride = cells - REACH if step == 1 else REACH
-
-        def inside(c, carry):
-            last = finals if step == steps - 1 else None
-            advance(now, other, courant, drops, band, step, deep + c * stride, grad, False, deep, last)
-            return carry
-
-        if half:
-            lax.fori_loop(0, 2 * half, outside, 0, unroll=2)
-        groups = 2 if step == 1 else cells // REACH
-        for first in range(0, groups, 2):
-            lax.fori_loop(first, min(first + 2, groups), inside, 0, unroll=2)
-            if step == steps - 1:
-                done = pl.ds(first * REACH, min(2, groups - first) * REACH)
+        edge = range(REACH * (step + 1), deep, REACH)
+        groups = list(edge) + [x + cells + deep - REACH * (step + 1) for x in edge]
+        for pair in paired(groups):
+            advance(now, other, courant, drops, band, step, pair, None, False, deep)
+        own = range(deep, deep + cells, REACH)
+        groups = [own[0], own[-1]] if step == 1 else own
+        last = finals if step == steps - 1 else None
+        for pair in paired(groups):
+            advance(now, other, courant, drops, band, step, pair, grad, False, deep, last)
+            if last is not None:
+                done = pl.ds(pair[0] - deep, len(pair) * REACH)
                 bring(finals.at[0, done], final_w.at[0, done])
                 bring(finals.at[1, done], final_j.at[0, done])
         now, other = other, now

time: 48.1 us -> 48.2 us (level)
  no operation moved by 1% of the time
where the time goes in v6:
time: 48.2 us; the launch traced here: 47.9 us
  blocking collectives  22.4 us (46%)
  Pallas kernels  8.97 us (19%)
  starting transfers between devices  7.1 us (15%)
  waiting for transfers between devices  6.81 us (14%)
  between operations  2.01 us (4%)
  other arithmetic  0.66 us (1%)
    all_to_all x1, blocking collectives, per_device(): shares = lax.all_to_all(parts, 'shot', 0, 0, tiled=True)  12.2 us
    all_gather x1, blocking collectives, per_device(): speeds = lax.all_gather(velocity, 'shot')  10.2 us
    ppermute x4, starting transfers between devices, swap_pairs(): return lax.ppermute(block, axis, route)  7.1 us
    ppermute x4, waiting for transfers between devices, swap_pairs(): return lax.ppermute(block, axis, route)  6.81 us
    pallas_call x1, Pallas kernels, late_steps(): pl.pallas_call(kernel, out_shape=(final, final, *same), in_specs=[smem] *...  3.9 us
    pallas_call x1, Pallas kernels, early_steps(): pl.pallas_call(kernel, out_shape=(*same, waiting, parts), in_specs=[smem,...  1.92 us
    pallas_call x1, Pallas kernels, opening(): pl.pallas_call(opening_kernel, out_shape=(halo, halo, drops, band, buffer...  1.7 us
    pallas_call x1, Pallas kernels, pack(): pl.pallas_call(packing_kernel, out_shape=(out, out), in_specs=[pl.BlockSp...  1.45 us
  transfers between devices with their start and end apart: 4, of which 2 were waited for; matrix products, arithmetic and copies ran while one was open for 0% of the time, Pallas kernels for 8%

profile of v6, /device:TPU:8, one launch (start us, length us, event | category | flops | bytes accessed | tf_op | source)
XLA Modules:
  0.0 47.9 jit_solution(3215620338362302297)
XLA Ops:
  0.6 1.4 %shard_map.131 = (f32[40,32,128]{2,1,0:T(8,128)S(1)}, f32[40,32,128]{2,1,0:T(8,128)S(1)}) custom-call(f32[1,16,32,128]{3,2,1,0:T(8,128)} %now_w.3, f32[1,16,32,128]{3,2,1,0:T(8,128)} %now_j.3, f32[1,16,32,128]{3,2,1,0:T(8,128)} %prev_w.3, f32[1,16,32,128]{3,2,1,0:T(8,128)} %prev_j.3), custom_call_target="tpu_custom_call" | custom-call | bytes 4194304 | tf_op jit(solution)/shard_map/pallas_call | solution.py:50
  2.1 0.1 collective-permute-start.2
  2.2 5.0 %collective-permute-start.3 = (f32[40,32,128]{2,1,0:T(8,128)S(1)}, f32[40,32,128]{2,1,0:T(8,128)S(1)}, u32[]{:S(2)}, u32[]{:S(2)}) collective-permute-start(f32[40,32,128]{2,1,0:T(8,128)S(1)} %get-tuple-element.28), channel_id=1, source_target_pairs={{1,2},{2,1},{5,6},{6,5},{9,10},{10,9},{13,14},{14,13},{17,18},{18,... | collective-permute-start | bytes 1966088 | tf_op jit(solution)/shard_map/ppermute | solution.py:21
  8.5 10.2 %all-gather = f32[128,8,128]{2,1,0:T(8,128)S(1)} all-gather(f32[16,8,128]{2,1,0:T(8,128)} %param.11), channel_id=2, replica_groups=mesh['shot'=8,'slab'=4] {'shot'}, dimensions={0}, use_global_device_ids=true | all-gather | bytes 589824 | tf_op jit(solution)/shard_map/all_gather | solution.py:490
  18.7 1.7 %shard_map.130 = (f32[16,32,128]{2,1,0:T(8,128)S(1)}, f32[16,32,128]{2,1,0:T(8,128)S(1)}, f32[4,2,48,8,128]{4,3,2,1,0:T(8,128)S(1)}, bf16[256,128]{1,0:T(8,128)(...) custom-call(s32[1]{0:T(128)S(6)} %copy.30.start.refs_0_, ...), custom_call_target="tpu_custom_call" | custom-call | flops 4194304 | bytes 4194304 | tf_op jit(solution)/shard_map/pallas_call | solution.py:218
  20.4 0.1 collective-permute-start
  20.4 1.9 %collective-permute-start.1 = (f32[16,32,128]{2,1,0:T(8,128)S(1)}, f32[16,32,128]{2,1,0:T(8,128)S(1)}, u32[]{:S(2)}, u32[]{:S(2)}) collective-permute-start(f32[16,32,128]{2,1,0:T(8,128)S(1)} %get-tuple-element.23), channel_id=1, source_target_pairs={{1,2},{2,1},{5,6},{6,5},{9,10},{10,9},{13,14},{14,13},{17,18},{18,... | collective-permute-start | bytes 786440 | tf_op jit(solution)/shard_map/ppermute | solution.py:21
  22.4 0.0 collective-permute-done.2.refs_1_
  22.4 0.0 collective-permute-done.3.refs_2_
  22.4 1.9 %shard_map.132 = (f32[2,48,48,128]{3,2,1,0:T(8,128)S(1)}, f32[2,48,48,128]{3,2,1,0:T(8,128)S(1)}, f32[16,32,128]{2,1,0:T(8,128)S(1)}, f32[2,16,32,128]{3,2,1,0:T(8,128)S(1)}, f32[8,16,8,128]{3,2,1,0:T(8,128)S(1)}) custom-call(s32[1]{0:T(128)S(6)} %copy.31.count.refs_0_.refs_1_, ...), custom_call_target="tpu_custom_call", output_to_operand_aliasing={{0}: (6, {}), {1}: (7, {}), {2}: (8, {})} | custom-call | flops 20971520 | bytes 4194304 | tf_op jit(solution)/shard_map/pallas_call | solution.py:433
  24.3 4.9 %collective-permute-done.refs_2_ = f32[16,32,128]{2,1,0:T(8,128)S(1)} collective-permute-done((f32[16,32,128]{2,1,0:T(8,128)S(1)}, f32[16,32,128]{2,1,0:T(8,128)S(1)}, u32[]{:S(2)}, u32[]{:S(2)}) %collective-permute-start) | collective-permute-done | bytes 262176 | tf_op jit(solution)/shard_map/ppermute | solution.py:21
  29.2 1.9 %collective-permute-done.1.refs_3_ = f32[16,32,128]{2,1,0:T(8,128)S(1)} collective-permute-done((f32[16,32,128]{2,1,0:T(8,128)S(1)}, f32[16,32,128]{2,1,0:T(8,128)S(1)}, u32[]{:S(2)}, u32[]{:S(2)}) %collective-permute-start.1) | collective-permute-done | bytes 262176 | tf_op jit(solution)/shard_map/ppermute | solution.py:21
  31.1 3.9 %shard_map.133 = (f32[1,16,32,128]{3,2,1,0:T(8,128)}, f32[1,16,32,128]{3,2,1,0:T(8,128)}, f32[2,48,48,128]{3,2,1,0:T(8,128)S(1)}, f32[2,48,48,128]{3,2,1,0:T(8,1...) custom-call(s32[1]{0:T(128)S(6)} %copy.30.start.refs_0_, ...), custom_call_target="tpu_custom_call", output_to_operand_aliasing={{2}: (8, {}), {3}: (9, {}), {4}: (10, {}), {5}: (11, {}), {... | custom-call | flops 41943040 | bytes 6291456 | tf_op jit(solution)/shard_map/pallas_call | solution.py:454
  35.0 12.2 %all_to_all.5 = f32[8,16,8,128]{3,2,1,0:T(8,128)S(1)} all-to-all(f32[8,16,8,128]{3,2,1,0:T(8,128)S(1)} %get-tuple-element.40), channel_id=1, replica_groups=mesh['shot'=8,'slab'=4] {'shot'}, dimensions={0} | all-to-all | bytes 1048576 | tf_op jit(solution)/shard_map/all_to_all | solution.py:518
  47.2 0.7 %reduce_sum.9 = f32[16,8,128]{2,1,0:T(8,128)} reduce(f32[8,16,8,128]{3,2,1,0:T(8,128)S(1)} %all_to_all.5, f32[]{:T(128)} %constant.0.clone.1), dimensions={0}, to_apply=%region_0.0 | reduce | flops 114688 | bytes 589828 | tf_op jit(solution)/shard_map/reduce_sum | solution.py:519
Async XLA Ops:
  2.1 20.3 %collective-permute-start.2 = (f32[40,32,128]{2,1,0:T(8,128)S(1)}, f32[40,32,128]{2,1,0:T(8,128)S(1)}, u32[]{:S(2)}, u32[]{:S(2)}) collective-permute-start(f32[40,32,128]{2,1,0:T(8,128)S(1)} %get-tuple-element.27), channel_id=1, source_target_pairs={{0,1},{1,0},{2,3},{3,2},{4,5},{5,4},{6,7},{7,6},{8,9},{9,8},{10,11... | collective-permute-start | bytes 1966088 | tf_op jit(solution)/shard_map/ppermute | solution.py:21
  2.2 20.2 %collective-permute-start.3 = (f32[40,32,128]{2,1,0:T(8,128)S(1)}, f32[40,32,128]{2,1,0:T(8,128)S(1)}, u32[]{:S(2)}, u32[]{:S(2)}) collective-permute-start(f32[40,32,128]{2,1,0:T(8,128)S(1)} %get-tuple-element.28), channel_id=1, source_target_pairs={{1,2},{2,1},{5,6},{6,5},{9,10},{10,9},{13,14},{14,13},{17,18},{18,... | collective-permute-start | bytes 1966088 | tf_op jit(solution)/shard_map/ppermute | solution.py:21
  20.4 8.9 %collective-permute-start = (f32[16,32,128]{2,1,0:T(8,128)S(1)}, f32[16,32,128]{2,1,0:T(8,128)S(1)}, u32[]{:S(2)}, u32[]{:S(2)}) collective-permute-start(f32[16,32,128]{2,1,0:T(8,128)S(1)} %get-tuple-element.22), channel_id=1, source_target_pairs={{0,1},{1,0},{2,3},{3,2},{4,5},{5,4},{6,7},{7,6},{8,9},{9,8},{10,11... | collective-permute-start | bytes 786440 | tf_op jit(solution)/shard_map/ppermute | solution.py:21
  20.4 10.7 %collective-permute-start.1 = (f32[16,32,128]{2,1,0:T(8,128)S(1)}, f32[16,32,128]{2,1,0:T(8,128)S(1)}, u32[]{:S(2)}, u32[]{:S(2)}) collective-permute-start(f32[16,32,128]{2,1,0:T(8,128)S(1)} %get-tuple-element.23), channel_id=1, source_target_pairs={{1,2},{2,1},{5,6},{6,5},{9,10},{10,9},{13,14},{14,13},{17,18},{18,... | collective-permute-start | bytes 786440 | tf_op jit(solution)/shard_map/ppermute | solution.py:21

commit v7 on v6

--- a/solution.py
+++ b/solution.py
@@ -29,7 +29,7 @@
     return pltpu.with_memory_space_constraint(array, pltpu.HBM)
 
 
-def packing_kernel(now_w, now_j, prev_w, prev_j, to_a, to_b, sems):
+def packing_kernel(now_w, now_j, prev_w, prev_j, to_a, to_b, drops, band, one, two, sems):
     cells = now_w.shape[1]
     deep_now = (to_a.shape[0] // 2 + REACH) // 2
     deep_prev = deep_now - REACH
@@ -40,20 +40,45 @@
         for field, deep in ((now_w, deep_now), (now_j, deep_now), (prev_w, deep_prev), (prev_j, deep_prev)):
             bring(field.at[0, pl.ds(side * (cells - deep), deep)], out.at[pl.ds(at, deep)])
             at += deep
+    steps, depth = drops.shape[0], drops.shape[4]
+    zero_tile = jnp.zeros((TILE, depth), jnp.float32)
+
+    def clear(x, carry):
+        for field in range(2):
+            for step in range(steps):
+                drops[step, field, x] = zero_tile
+            for buffer in (one, two):
+                buffer[field, x, pl.ds(0, TILE), :] = zero_tile
+                buffer[field, x, pl.ds(buffer.shape[2] - TILE, TILE), :] = zero_tile
+        return carry
+
+    lax.fori_loop(0, drops.shape[2], clear, 0)
+    away = lax.broadcasted_iota(jnp.int32, (depth, depth), 0) - lax.broadcasted_iota(jnp.int32, (depth, depth), 1)
+    matrix = jnp.zeros((depth, depth), jnp.float32)
+    for k in range(1, REACH + 1):
+        matrix = jnp.where((away == k) | (away == -k), scaled_weights[k], matrix)
+    band[pl.ds(0, depth), :] = matrix.astype(jnp.bfloat16)
+    band[pl.ds(depth, depth), :] = matrix.astype(jnp.bfloat16)
     for copy in copies:
         copy.wait()
 
 
-def pack(fields, deep):
-    rows, depth = fields[0].shape[2:]
-    out = pltpu.VMEM((4 * deep - 2 * REACH, rows, depth), jnp.float32)
+def pack(fields, steps):
+    cells, rows, depth = fields[0].shape[1:]
+    deep = steps * REACH
+    wide = cells + 2 * deep
+    message = pltpu.VMEM((4 * (deep - REACH) - 2 * REACH, rows, depth), jnp.float32)
+    drops = pltpu.VMEM((steps, 2, wide, TILE, depth), jnp.float32)
+    band = pltpu.VMEM((2 * depth, depth), jnp.bfloat16)
+    buffer = pltpu.VMEM((2, wide, rows + 2 * TILE, depth), jnp.float32)
+    vmem = pl.BlockSpec(memory_space=pltpu.VMEM)
     return pl.pallas_call(
         packing_kernel,
-        out_shape=(out, out),
+        out_shape=(message, message, drops, band, buffer, buffer),
         in_specs=[pl.BlockSpec(memory_space=pltpu.HBM)] * 4,
-        out_specs=(any_space(), any_space()),
+        out_specs=(vmem,) * 6,
         scratch_shapes=[pltpu.SemaphoreType.DMA((8,))],
-        compiler_params=pltpu.CompilerParams(vmem_limit_bytes=1 << 20),
+        compiler_params=pltpu.CompilerParams(vmem_limit_bytes=8 << 20),
         cost_estimate=pl.CostEstimate(flops=0, bytes_accessed=4 << 20, transcendentals=0),
     )(*map(in_hbm, fields))
 
@@ -67,6 +92,24 @@
         copies.append(copy)
 
     return copies, bring
+
+
+def inject(drops, slab_first, steps, field, places, amps):
+    row = lax.broadcasted_iota(jnp.int32, drops.shape[3:], 0)
+    col = lax.broadcasted_iota(jnp.int32, drops.shape[3:], 1)
+
+    def one_cell(s, carry):
+        x = places[0, 0, s] - slab_first
+
+        @pl.when((x >= 0) & (x < drops.shape[2]))
+        def _():
+            here = (row == places[1, 0, s]) & (col == places[2, 0, s])
+            for step in steps:
+                drops[step, field, x] = drops[step, field, x] + jnp.where(here, amps[0, step, s], 0.0)
+
+        return carry
+
+    lax.fori_loop(0, places.shape[2], one_cell, 0)
 
 
 def opening_kernel(
@@ -76,15 +119,16 @@
     cells_j_in,
     amps_w_in,
     amps_j_in,
-    now_w,
-    now_j,
-    prev_w,
-    prev_j,
+    sent_a,
+    sent_b,
     speeds,
+    band,
+    drops_in,
+    one_in,
+    two_in,
     to_a,
     to_b,
     drops,
-    band,
     one,
     two,
     courant,
@@ -101,38 +145,22 @@
     steps = drops.shape[0]
     deep = steps * REACH
     near = deep - 2 * REACH
-    wide = drops.shape[2]
-    slab = lax.axis_index("slab")
-    odd = slab % 2
+    held = near + REACH
+    half = cells // 2
+    odd = lax.axis_index("slab") % 2
     start_block = start[0]
     live = count[0]
     copies, bring = bringing(sems)
     for source, target in ((cells_w_in, cells_w), (cells_j_in, cells_j), (amps_w_in, amps_w), (amps_j_in, amps_j)):
         bring(source, target)
+    sides = ((sent_a, to_a, 1 - odd), (sent_b, to_b, odd))
     inner = pl.ds(TILE, rows)
-    for field, (now, prev) in enumerate(((now_w, prev_w), (now_j, prev_j))):
-        bring(now.at[0], one.at[field, pl.ds(deep, cells), inner])
-        bring(prev.at[0], two.at[field, pl.ds(deep, cells), inner])
-
-    zero_tile = jnp.zeros((TILE, depth), jnp.float32)
-
-    def clear(x, carry):
-        for step in range(steps):
-            for field in range(2):
-                drops[step, field, x] = zero_tile
-        for buffer in (one, two):
-            for field in range(2):
-                buffer[field, x, pl.ds(0, TILE), :] = zero_tile
-                buffer[field, x, pl.ds(TILE + rows, TILE), :] = zero_tile
-        return carry
-
-    lax.fori_loop(0, wide, clear, 0)
-    away = lax.broadcasted_iota(jnp.int32, (depth, depth), 0) - lax.broadcasted_iota(jnp.int32, (depth, depth), 1)
-    matrix = jnp.zeros((depth, depth), jnp.float32)
-    for k in range(1, REACH + 1):
-        matrix = jnp.where((away == k) | (away == -k), scaled_weights[k], matrix)
-    band[pl.ds(0, depth), :] = matrix.astype(jnp.bfloat16)
-    band[pl.ds(depth, depth), :] = matrix.astype(jnp.bfloat16)
+    for sent, _, side in sides:
+        for field in range(2):
+            for layer in range(half):
+                x = deep + side * half + layer
+                one[field, x, inner, :] = sent[field * held + layer + side * (held - half)]
+                two[field, x, inner, :] = sent[2 * held + field * near + layer + side * (near - half)]
 
     def factors(x, carry):
         for tile in range(tiles):
@@ -144,42 +172,20 @@
         return carry
 
     lax.fori_loop(0, cells, factors, 0, unroll=4)
-
-    for out, side in ((to_a, 1 - odd), (to_b, odd)):
+    for _, out, side in sides:
         for layer in range(near):
             for tile in range(tiles):
                 speed = speeds[start_block + tile, side * (cells - near) + layer]
                 out[layer, pl.ds(tile * TILE, TILE), :] = speed
-    for copy in copies[:4]:
+    clear_dead(one, two, live, deep, deep + cells)
+    for copy in copies:
         copy.wait()
-
-    row = lax.broadcasted_iota(jnp.int32, (TILE, depth), 0)
-    col = lax.broadcasted_iota(jnp.int32, (TILE, depth), 1)
-
-    def inject(field, places, amps):
-        def one_cell(s, carry):
-            x = places[0, 0, s] - (slab * cells - deep)
-
-            @pl.when((x >= 0) & (x < wide))
-            def _():
-                here = (row == places[1, 0, s]) & (col == places[2, 0, s])
-                for step in range(steps):
-                    drops[step, field, x] = drops[step, field, x] + jnp.where(here, amps[0, step, s], 0.0)
-
-            return carry
-
-        lax.fori_loop(0, places.shape[2], one_cell, 0)
-
-    inject(0, cells_w, amps_w)
-    inject(1, cells_j, amps_j)
-
-    for copy in copies[4:]:
-        copy.wait()
-    clear_dead(one, two, live, deep, deep + cells)
-
+    slab_first = lax.axis_index("slab") * cells - deep
+    inject(drops, slab_first, range(1), 0, cells_w, amps_w)
+    inject(drops, slab_first, range(1), 1, cells_j, amps_j)
     for groups in paired(range(deep + REACH, deep + cells - REACH, REACH)):
         advance(one, two, courant, drops, band, 0, groups, grad, True, deep)
-    for out, side in ((to_a, 1 - odd), (to_b, odd)):
+    for _, out, side in sides:
         for field in range(2):
             for i in range(REACH):
                 x = deep + REACH + (1 - side) * (cells - 3 * REACH) + i
@@ -203,28 +209,27 @@
             lax.fori_loop(first, last, clear, 0)
 
 
-def opening(start, count, small, fields, speeds, steps):
+def opening(start, count, small, sent_a, sent_b, speeds, band, drops, one, two):
     cells, depth = speeds.shape[1], speeds.shape[3]
-    rows = fields[0].shape[2]
-    deep = steps * REACH
-    wide = cells + 2 * deep
-    halo = pltpu.VMEM((deep, rows, depth), jnp.float32)
-    drops = pltpu.VMEM((steps, 2, wide, TILE, depth), jnp.float32)
-    band = pltpu.VMEM((2 * depth, depth), jnp.bfloat16)
-    buffer = pltpu.VMEM((2, wide, rows + 2 * TILE, depth), jnp.float32)
-    courant = pltpu.VMEM((wide, rows, depth), jnp.float32)
+    rows = sent_a.shape[1]
+    deep = drops.shape[0] * REACH
+    message = pltpu.VMEM((deep, rows, depth), jnp.float32)
+    courant = pltpu.VMEM((cells + 2 * deep, rows, depth), jnp.float32)
     layers = pltpu.VMEM((cells, rows, depth), jnp.float32)
+    same = [pltpu.VMEM(array.shape, array.dtype) for array in (drops, one, two)]
     vmem = pl.BlockSpec(memory_space=pltpu.VMEM)
     return pl.pallas_call(
         opening_kernel,
-        out_shape=(halo, halo, drops, band, buffer, buffer, courant, layers, layers),
-        in_specs=[pl.BlockSpec(memory_space=pltpu.SMEM)] * 2 + [pl.BlockSpec(memory_space=pltpu.HBM)] * 8 + [vmem],
-        out_specs=(vmem,) * 9,
-        scratch_shapes=[pltpu.SMEM(array.shape, array.dtype) for array in small]
-        + [pltpu.SemaphoreType.DMA((8,))],
+        out_shape=(message, message, *same, courant, layers, layers),
+        in_specs=[pl.BlockSpec(memory_space=pltpu.SMEM)] * 2
+        + [pl.BlockSpec(memory_space=pltpu.HBM)] * 4
+        + [vmem] * 7,
+        out_specs=(vmem,) * 8,
+        input_output_aliases={10: 2, 11: 3, 12: 4},
+        scratch_shapes=[pltpu.SMEM(array.shape, array.dtype) for array in small] + [pltpu.SemaphoreType.DMA((4,))],
         compiler_params=pltpu.CompilerParams(vmem_limit_bytes=8 << 20),
         cost_estimate=pl.CostEstimate(flops=4 << 20, bytes_accessed=4 << 20, transcendentals=0),
-    )(start, count, *map(in_hbm, small), *map(in_hbm, fields), speeds)
+    )(start, count, *map(in_hbm, small), sent_a, sent_b, speeds, band, drops, one, two)
 
 
 def along_z(now, band, field, x):
@@ -279,7 +284,33 @@
     each_tile(now, band, groups, visit)
 
 
-def early_kernel(steps, count, from_a, from_b, courant, drops, band, one_in, two_in, grad_in, one, two, grad, waiting, parts, sems):
+def early_kernel(
+    steps,
+    count,
+    cells_w_in,
+    cells_j_in,
+    amps_w_in,
+    amps_j_in,
+    from_a,
+    from_b,
+    courant,
+    band,
+    drops_in,
+    one_in,
+    two_in,
+    grad_in,
+    drops,
+    one,
+    two,
+    grad,
+    waiting,
+    parts,
+    cells_w,
+    cells_j,
+    amps_w,
+    amps_j,
+    sems,
+):
     cells, rows, depth = grad.shape
     deep = steps * REACH
     near = deep - 2 * REACH
@@ -289,6 +320,8 @@
 
     left_of_a = odd
     copies, bring = bringing(sems)
+    for source, target in ((cells_w_in, cells_w), (cells_j_in, cells_j), (amps_w_in, amps_w), (amps_j_in, amps_j)):
+        bring(source, target)
     inner = pl.ds(TILE, rows)
     for field in range(2):
         for buffer, on_left in ((from_a, left_of_a), (from_b, 1 - left_of_a)):
@@ -303,6 +336,9 @@
     lax.fori_loop(0, parts.shape[0], clear_parts, 0)
     for copy in copies:
         copy.wait()
+    slab_first = lax.axis_index("slab") * cells - deep
+    inject(drops, slab_first, range(1, steps), 0, cells_w, amps_w)
+    inject(drops, slab_first, range(1, steps), 1, cells_j, amps_j)
     clear_dead(one, two, count[0], 0, deep)
     clear_dead(one, two, count[0], deep + cells, wide)
 
@@ -419,13 +455,13 @@
         copy.wait()
 
 
-def early_steps(steps, count, from_a, from_b, courant, drops, band, one, two, grad, groups):
+def early_steps(count, small, from_a, from_b, courant, band, drops, one, two, grad, groups):
     cells, rows, depth = grad.shape
+    steps = drops.shape[0]
     waiting = pltpu.VMEM((2, 2 * (steps - 2) * REACH, rows, depth), jnp.float32)
     parts = pltpu.VMEM((groups, cells, TILE, depth), jnp.float32)
-    smem = pl.BlockSpec(memory_space=pltpu.SMEM)
     vmem = pl.BlockSpec(memory_space=pltpu.VMEM)
-    same = [pltpu.VMEM(array.shape, array.dtype) for array in (one, two, grad)]
+    same = [pltpu.VMEM(array.shape, array.dtype) for array in (drops, one, two, grad)]
 
     def kernel(*refs):
         early_kernel(steps, *refs)
@@ -433,13 +469,16 @@
     return pl.pallas_call(
         kernel,
         out_shape=(*same, waiting, parts),
-        in_specs=[smem, any_space(), any_space()] + [vmem] * 6,
-        out_specs=(vmem,) * 5,
-        input_output_aliases={6: 0, 7: 1, 8: 2},
-        scratch_shapes=[pltpu.SemaphoreType.DMA((8,))],
+        in_specs=[pl.BlockSpec(memory_space=pltpu.SMEM)]
+        + [pl.BlockSpec(memory_space=pltpu.HBM)] * 4
+        + [any_space()] * 2
+        + [vmem] * 6,
+        out_specs=(vmem,) * 6,
+        input_output_aliases={9: 0, 10: 1, 11: 2, 12: 3},
+        scratch_shapes=[pltpu.SMEM(array.shape, array.dtype) for array in small] + [pltpu.SemaphoreType.DMA((12,))],
         compiler_params=pltpu.CompilerParams(vmem_limit_bytes=8 << 20),
         cost_estimate=pl.CostEstimate(flops=20 << 20, bytes_accessed=4 << 20, transcendentals=0),
-    )(count, from_a, from_b, courant, drops, band, one, two, grad)
+    )(count, *map(in_hbm, small), from_a, from_b, courant, band, drops, one, two, grad)
 
 
 def late_steps(steps, start, count, next_a, next_b, drops, band, image, waiting, one, two, courant, grad, parts):
@@ -481,23 +520,22 @@
     trace,
 ):
     steps = wavelet.shape[1]
-    deep = steps * REACH
     fields = (wave_now, adjoint_now, wave_prev, adjoint_prev)
 
-    to_a, to_b = pack(fields, deep - REACH)
-    from_a = swap_pairs(to_a, "slab", 0)
-    from_b = swap_pairs(to_b, "slab", 1)
+    sent_a, sent_b, drops, band, one, two = pack(fields, steps)
+    from_a = swap_pairs(sent_a, "slab", 0)
+    from_b = swap_pairs(sent_b, "slab", 1)
     speeds = lax.all_gather(velocity, "shot")
 
     cells_w, cells_j = (jnp.transpose(places, (2, 0, 1)) for places in (source_cells, receiver_cells))
     small = (cells_w, cells_j, wavelet, trace)
-    to_a, to_b, drops, band, one, two, courant, image, grad = opening(
-        aperture_start, aperture_count, small, fields, speeds, steps
+    to_a, to_b, drops, one, two, courant, image, grad = opening(
+        aperture_start, aperture_count, small, sent_a, sent_b, speeds, band, drops, one, two
     )
     next_a = swap_pairs(to_a, "slab", 0)
     next_b = swap_pairs(to_b, "slab", 1)
-    one, two, grad, waiting, parts = early_steps(
-        steps, aperture_count, from_a, from_b, courant, drops, band, one, two, grad, lax.axis_size("shot")
+    drops, one, two, grad, waiting, parts = early_steps(
+        aperture_count, small, from_a, from_b, courant, band, drops, one, two, grad, lax.axis_size("shot")
     )
     final_w, final_j, parts = late_steps(
         steps,

time: 48.2 us -> 48 us (level)
  waiting for transfers between devices: 6.81 us -> 5.66 us
  Pallas kernels: 8.97 us -> 9.81 us
    ppermute x4, waiting for transfers between devices: 6.81 us -> 5.66 us  [swap_pairs(): return lax.ppermute(block, axis, route)]
    pallas_call x3, Pallas kernels: 5.06 us -> 5.91 us  [the longest x1 2.85 us: early_steps(): pl.pallas_call(kernel, out_shape=(*same, waiting, parts), in_specs=[pl.Bl...]
  transfers between devices with their start and end apart: 4 -> 4, of which waited for: 2 -> 2; matrix products, arithmetic and copies ran while one was open for 0% -> 0% of each run, Pallas kernels for 8% -> 9%
where the time goes in v7:
time: 48 us; the launch traced here: 47.7 us
  blocking collectives  22.4 us (47%)
  Pallas kernels  9.81 us (20%)
  starting transfers between devices  7.1 us (15%)
  waiting for transfers between devices  5.66 us (12%)
  between operations  2.01 us (4%)
  other arithmetic  0.66 us (1%)
    all_to_all x1, blocking collectives, per_device(): shares = lax.all_to_all(parts, 'shot', 0, 0, tiled=True)  12.3 us
    all_gather x1, blocking collectives, per_device(): speeds = lax.all_gather(velocity, 'shot')  10.2 us
    ppermute x4, starting transfers between devices, swap_pairs(): return lax.ppermute(block, axis, route)  7.1 us
    ppermute x4, waiting for transfers between devices, swap_pairs(): return lax.ppermute(block, axis, route)  5.66 us
    pallas_call x1, Pallas kernels, late_steps(): pl.pallas_call(kernel, out_shape=(final, final, *same), in_specs=[smem] *...  3.9 us
    pallas_call x1, Pallas kernels, early_steps(): pl.pallas_call(kernel, out_shape=(*same, waiting, parts), in_specs=[pl.Bl...  2.85 us
    pallas_call x1, Pallas kernels, opening(): pl.pallas_call(opening_kernel, out_shape=(message, message, *same, couran...  1.61 us
    pallas_call x1, Pallas kernels, pack(): pl.pallas_call(packing_kernel, out_shape=(message, message, drops, band,...  1.44 us
  transfers between devices with their start and end apart: 4, of which 2 were waited for; matrix products, arithmetic and copies ran while one was open for 0% of the time, Pallas kernels for 9%

profile of v7, /device:TPU:8, one launch (start us, length us, event | category | flops | bytes accessed | tf_op | source)
XLA Modules:
  0.0 47.7 jit_solution(972499867022766534)
XLA Ops:
  0.6 1.4 %shard_map.130 = (f32[40,32,128]{2,1,0:T(8,128)S(1)}, f32[40,32,128]{2,1,0:T(8,128)S(1)}, f32[4,2,48,8,128]{4,3,2,1,0:T(8,128)S(1)}, bf16[256,128]{1,0:T(8,128)(...) custom-call(f32[1,16,32,128]{3,2,1,0:T(8,128)} %now_w.1, f32[1,16,32,128]{3,2,1,0:T(8,128)} %now_j.1, ...), custom_call_target="tpu_custom_call" | custom-call | bytes 4194304 | tf_op jit(solution)/shard_map/pallas_call | solution.py:75
  2.1 0.1 collective-permute-start.2
  2.2 5.0 %collective-permute-start.3 = (f32[40,32,128]{2,1,0:T(8,128)S(1)}, f32[40,32,128]{2,1,0:T(8,128)S(1)}, u32[]{:S(2)}, u32[]{:S(2)}) collective-permute-start(f32[40,32,128]{2,1,0:T(8,128)S(1)} %get-tuple-element.27.sent_b), channel_id=1, source_target_pairs={{1,2},{2,1},{5,6},{6,5},{9,10},{10,9},{13,14},{14,13},{17,18},{18,... | collective-permute-start | bytes 1966088 | tf_op jit(solution)/shard_map/ppermute | solution.py:21
  8.5 10.2 %all-gather = f32[128,8,128]{2,1,0:T(8,128)S(1)} all-gather(f32[16,8,128]{2,1,0:T(8,128)} %param.11), channel_id=2, replica_groups=mesh['shot'=8,'slab'=4] {'shot'}, dimensions={0}, use_global_device_ids=true | all-gather | bytes 589824 | tf_op jit(solution)/shard_map/all_gather | solution.py:528
  18.7 1.6 %shard_map.131 = (f32[16,32,128]{2,1,0:T(8,128)S(1)}, f32[16,32,128]{2,1,0:T(8,128)S(1)}, f32[4,2,48,8,128]{4,3,2,1,0:T(8,128)S(1)}, f32[2,48,48,128]{3,2,1,0:T(...) custom-call(s32[1]{0:T(128)S(6)} %copy.38.start.refs_0_, ...), custom_call_target="tpu_custom_call", output_to_operand_aliasing={{2}: (10, {}), {3}: (11, {}), {4}: (12, {})} | custom-call | flops 4194304 | bytes 4194304 | tf_op jit(solution)/shard_map/pallas_call | solution.py:221
  20.3 0.1 collective-permute-start
  20.4 1.9 %collective-permute-start.1 = (f32[16,32,128]{2,1,0:T(8,128)S(1)}, f32[16,32,128]{2,1,0:T(8,128)S(1)}, u32[]{:S(2)}, u32[]{:S(2)}) collective-permute-start(f32[16,32,128]{2,1,0:T(8,128)S(1)} %get-tuple-element.33), channel_id=1, source_target_pairs={{1,2},{2,1},{5,6},{6,5},{9,10},{10,9},{13,14},{14,13},{17,18},{18,... | collective-permute-start | bytes 786440 | tf_op jit(solution)/shard_map/ppermute | solution.py:21
  22.3 0.0 collective-permute-done.2.refs_5_
  22.3 0.0 collective-permute-done.3.refs_6_
  22.3 2.8 %shard_map.132 = (f32[4,2,48,8,128]{4,3,2,1,0:T(8,128)S(1)}, f32[2,48,48,128]{3,2,1,0:T(8,128)S(1)}, f32[2,48,48,128]{3,2,1,0:T(8,128)S(1)}, f32[16,32,128]{2,1,...) custom-call(s32[1]{0:T(128)S(6)} %copy.39.count.refs_0_.refs_1_, ...), custom_call_target="tpu_custom_call", output_to_operand_aliasing={{0}: (9, {}), {1}: (10, {}), {2}: (11, {}), {3}: (12, {})} | custom-call | flops 20971520 | bytes 4194304 | tf_op jit(solution)/shard_map/pallas_call | solution.py:469
  25.2 3.8 %collective-permute-done.refs_2_ = f32[16,32,128]{2,1,0:T(8,128)S(1)} collective-permute-done((f32[16,32,128]{2,1,0:T(8,128)S(1)}, f32[16,32,128]{2,1,0:T(8,128)S(1)}, u32[]{:S(2)}, u32[]{:S(2)}) %collective-permute-start) | collective-permute-done | bytes 262176 | tf_op jit(solution)/shard_map/ppermute | solution.py:21
  28.9 1.9 %collective-permute-done.1.refs_3_ = f32[16,32,128]{2,1,0:T(8,128)S(1)} collective-permute-done((f32[16,32,128]{2,1,0:T(8,128)S(1)}, f32[16,32,128]{2,1,0:T(8,128)S(1)}, u32[]{:S(2)}, u32[]{:S(2)}) %collective-permute-start.1) | collective-permute-done | bytes 262176 | tf_op jit(solution)/shard_map/ppermute | solution.py:21
  30.8 3.9 %shard_map.133 = (f32[1,16,32,128]{3,2,1,0:T(8,128)}, f32[1,16,32,128]{3,2,1,0:T(8,128)}, f32[2,48,48,128]{3,2,1,0:T(8,128)S(1)}, f32[2,48,48,128]{3,2,1,0:T(8,1...) custom-call(s32[1]{0:T(128)S(6)} %copy.38.start.refs_0_, ...), custom_call_target="tpu_custom_call", output_to_operand_aliasing={{2}: (8, {}), {3}: (9, {}), {4}: (10, {}), {5}: (11, {}), {... | custom-call | flops 41943040 | bytes 6291456 | tf_op jit(solution)/shard_map/pallas_call | solution.py:493
  34.7 12.3 %all_to_all.5 = f32[8,16,8,128]{3,2,1,0:T(8,128)S(1)} all-to-all(f32[8,16,8,128]{3,2,1,0:T(8,128)S(1)} %get-tuple-element.48), channel_id=1, replica_groups=mesh['shot'=8,'slab'=4] {'shot'}, dimensions={0} | all-to-all | bytes 1048576 | tf_op jit(solution)/shard_map/all_to_all | solution.py:556
  47.0 0.7 %reduce_sum.9 = f32[16,8,128]{2,1,0:T(8,128)} reduce(f32[8,16,8,128]{3,2,1,0:T(8,128)S(1)} %all_to_all.5, f32[]{:T(128)} %constant.0.clone.1), dimensions={0}, to_apply=%region_0.0 | reduce | flops 114688 | bytes 589828 | tf_op jit(solution)/shard_map/reduce_sum | solution.py:557
Async XLA Ops:
  2.1 20.2 %collective-permute-start.2 = (f32[40,32,128]{2,1,0:T(8,128)S(1)}, f32[40,32,128]{2,1,0:T(8,128)S(1)}, u32[]{:S(2)}, u32[]{:S(2)}) collective-permute-start(f32[40,32,128]{2,1,0:T(8,128)S(1)} %get-tuple-element.26.sent_a), channel_id=1, source_target_pairs={{0,1},{1,0},{2,3},{3,2},{4,5},{5,4},{6,7},{7,6},{8,9},{9,8},{10,11... | collective-permute-start | bytes 1966088 | tf_op jit(solution)/shard_map/ppermute | solution.py:21
  2.2 20.1 %collective-permute-start.3 = (f32[40,32,128]{2,1,0:T(8,128)S(1)}, f32[40,32,128]{2,1,0:T(8,128)S(1)}, u32[]{:S(2)}, u32[]{:S(2)}) collective-permute-start(f32[40,32,128]{2,1,0:T(8,128)S(1)} %get-tuple-element.27.sent_b), channel_id=1, source_target_pairs={{1,2},{2,1},{5,6},{6,5},{9,10},{10,9},{13,14},{14,13},{17,18},{18,... | collective-permute-start | bytes 1966088 | tf_op jit(solution)/shard_map/ppermute | solution.py:21
  20.3 8.6 %collective-permute-start = (f32[16,32,128]{2,1,0:T(8,128)S(1)}, f32[16,32,128]{2,1,0:T(8,128)S(1)}, u32[]{:S(2)}, u32[]{:S(2)}) collective-permute-start(f32[16,32,128]{2,1,0:T(8,128)S(1)} %get-tuple-element.32), channel_id=1, source_target_pairs={{0,1},{1,0},{2,3},{3,2},{4,5},{5,4},{6,7},{7,6},{8,9},{9,8},{10,11... | collective-permute-start | bytes 786440 | tf_op jit(solution)/shard_map/ppermute | solution.py:21
  20.4 10.5 %collective-permute-start.1 = (f32[16,32,128]{2,1,0:T(8,128)S(1)}, f32[16,32,128]{2,1,0:T(8,128)S(1)}, u32[]{:S(2)}, u32[]{:S(2)}) collective-permute-start(f32[16,32,128]{2,1,0:T(8,128)S(1)} %get-tuple-element.33), channel_id=1, source_target_pairs={{1,2},{2,1},{5,6},{6,5},{9,10},{10,9},{13,14},{14,13},{17,18},{18,... | collective-permute-start | bytes 786440 | tf_op jit(solution)/shard_map/ppermute | solution.py:21

commit v8 on v7

--- a/solution.py
+++ b/solution.py
@@ -94,65 +94,50 @@
     return copies, bring
 
 
-def inject(drops, slab_first, steps, field, places, amps):
+def inject(drops, slab_first, field, places, amps):
     row = lax.broadcasted_iota(jnp.int32, drops.shape[3:], 0)
     col = lax.broadcasted_iota(jnp.int32, drops.shape[3:], 1)
 
     def one_cell(s, carry):
         x = places[0, 0, s] - slab_first
-
-        @pl.when((x >= 0) & (x < drops.shape[2]))
-        def _():
-            here = (row == places[1, 0, s]) & (col == places[2, 0, s])
-            for step in steps:
-                drops[step, field, x] = drops[step, field, x] + jnp.where(here, amps[0, step, s], 0.0)
-
-        return carry
-
-    lax.fori_loop(0, places.shape[2], one_cell, 0)
+        inside = (x >= 0) & (x < drops.shape[2])
+        x = jnp.clip(x, 0, drops.shape[2] - 1)
+        here = (row == places[1, 0, s]) & (col == places[2, 0, s])
+        tiles = [drops[step, field, x] for step in range(drops.shape[0])]
+        for step, tile in enumerate(tiles):
+            amp = jnp.where(inside, amps[0, step, s], 0.0)
+            drops[step, field, x] = tile + jnp.where(here, amp, 0.0)
+        return carry
+
+    lax.fori_loop(0, places.shape[2], one_cell, 0, unroll=4)
 
 
 def opening_kernel(
     start,
     count,
-    cells_w_in,
-    cells_j_in,
-    amps_w_in,
-    amps_j_in,
     sent_a,
     sent_b,
     speeds,
     band,
-    drops_in,
     one_in,
     two_in,
     to_a,
     to_b,
-    drops,
     one,
     two,
     courant,
     image,
     grad,
-    cells_w,
-    cells_j,
-    amps_w,
-    amps_j,
-    sems,
 ):
     cells, rows, depth = image.shape
     tiles = rows // TILE
-    steps = drops.shape[0]
-    deep = steps * REACH
+    deep = to_a.shape[0]
     near = deep - 2 * REACH
     held = near + REACH
     half = cells // 2
     odd = lax.axis_index("slab") % 2
     start_block = start[0]
     live = count[0]
-    copies, bring = bringing(sems)
-    for source, target in ((cells_w_in, cells_w), (cells_j_in, cells_j), (amps_w_in, amps_w), (amps_j_in, amps_j)):
-        bring(source, target)
     sides = ((sent_a, to_a, 1 - odd), (sent_b, to_b, odd))
     inner = pl.ds(TILE, rows)
     for sent, _, side in sides:
@@ -178,13 +163,8 @@
                 speed = speeds[start_block + tile, side * (cells - near) + layer]
                 out[layer, pl.ds(tile * TILE, TILE), :] = speed
     clear_dead(one, two, live, deep, deep + cells)
-    for copy in copies:
-        copy.wait()
-    slab_first = lax.axis_index("slab") * cells - deep
-    inject(drops, slab_first, range(1), 0, cells_w, amps_w)
-    inject(drops, slab_first, range(1), 1, cells_j, amps_j)
     for groups in paired(range(deep + REACH, deep + cells - REACH, REACH)):
-        advance(one, two, courant, drops, band, 0, groups, grad, True, deep)
+        advance(one, two, courant, None, band, 0, groups, grad, True, deep)
     for _, out, side in sides:
         for field in range(2):
             for i in range(REACH):
@@ -209,27 +189,24 @@
             lax.fori_loop(first, last, clear, 0)
 
 
-def opening(start, count, small, sent_a, sent_b, speeds, band, drops, one, two):
+def opening(start, count, sent_a, sent_b, speeds, band, one, two):
     cells, depth = speeds.shape[1], speeds.shape[3]
     rows = sent_a.shape[1]
-    deep = drops.shape[0] * REACH
-    message = pltpu.VMEM((deep, rows, depth), jnp.float32)
-    courant = pltpu.VMEM((cells + 2 * deep, rows, depth), jnp.float32)
+    wide = one.shape[1]
+    message = pltpu.VMEM(((wide - cells) // 2, rows, depth), jnp.float32)
+    courant = pltpu.VMEM((wide, rows, depth), jnp.float32)
     layers = pltpu.VMEM((cells, rows, depth), jnp.float32)
-    same = [pltpu.VMEM(array.shape, array.dtype) for array in (drops, one, two)]
+    same = [pltpu.VMEM(array.shape, array.dtype) for array in (one, two)]
     vmem = pl.BlockSpec(memory_space=pltpu.VMEM)
     return pl.pallas_call(
         opening_kernel,
         out_shape=(message, message, *same, courant, layers, layers),
-        in_specs=[pl.BlockSpec(memory_space=pltpu.SMEM)] * 2
-        + [pl.BlockSpec(memory_space=pltpu.HBM)] * 4
-        + [vmem] * 7,
-        out_specs=(vmem,) * 8,
-        input_output_aliases={10: 2, 11: 3, 12: 4},
-        scratch_shapes=[pltpu.SMEM(array.shape, array.dtype) for array in small] + [pltpu.SemaphoreType.DMA((4,))],
+        in_specs=[pl.BlockSpec(memory_space=pltpu.SMEM)] * 2 + [vmem] * 6,
+        out_specs=(vmem,) * 7,
+        input_output_aliases={6: 2, 7: 3},
         compiler_params=pltpu.CompilerParams(vmem_limit_bytes=8 << 20),
         cost_estimate=pl.CostEstimate(flops=4 << 20, bytes_accessed=4 << 20, transcendentals=0),
-    )(start, count, *map(in_hbm, small), sent_a, sent_b, speeds, band, drops, one, two)
+    )(start, count, sent_a, sent_b, speeds, band, one, two)
 
 
 def along_z(now, band, field, x):
@@ -271,7 +248,7 @@
         factor = courant[x, own, :]
         for field, (center, lap) in enumerate(pair):
             ahead = 2.0 * center - other[field, x, padded, :] + factor * lap
-            if tile == 0:
+            if tile == 0 and drops is not None:
                 ahead = ahead + drops[step, field, x]
             if finals is None:
                 other[field, x, padded, :] = ahead
@@ -282,6 +259,13 @@
             grad[x - deep, own, :] = term if fresh else grad[x - deep, own, :] + term
 
     each_tile(now, band, groups, visit)
+
+
+def add_drops(buffer, drops, layers):
+    for field in range(2):
+        for x in layers:
+            tile = buffer[field, x, pl.ds(TILE, TILE), :]
+            buffer[field, x, pl.ds(TILE, TILE), :] = tile + drops[0, field, x]
 
 
 def early_kernel(
@@ -337,8 +321,9 @@
     for copy in copies:
         copy.wait()
     slab_first = lax.axis_index("slab") * cells - deep
-    inject(drops, slab_first, range(1, steps), 0, cells_w, amps_w)
-    inject(drops, slab_first, range(1, steps), 1, cells_j, amps_j)
+    inject(drops, slab_first, 0, cells_w, amps_w)
+    inject(drops, slab_first, 1, cells_j, amps_j)
+    add_drops(two, drops, range(deep + REACH, deep + cells - REACH))
     clear_dead(one, two, count[0], 0, deep)
     clear_dead(one, two, count[0], deep + cells, wide)
 
@@ -426,6 +411,8 @@
             for i in range(REACH):
                 x = left * (deep - near - REACH) + (1 - left) * (deep + cells + near) + i
                 two[field, x, inner, :] = message[near + field * REACH + i]
+    add_drops(two, drops, range(deep - near - REACH, deep - near))
+    add_drops(two, drops, range(deep + cells + near, deep + cells + near + REACH))
 
     now, other = two, one
     for step in range(1, steps):
@@ -529,8 +516,8 @@
 
     cells_w, cells_j = (jnp.transpose(places, (2, 0, 1)) for places in (source_cells, receiver_cells))
     small = (cells_w, cells_j, wavelet, trace)
-    to_a, to_b, drops, one, two, courant, image, grad = opening(
-        aperture_start, aperture_count, small, sent_a, sent_b, speeds, band, drops, one, two
+    to_a, to_b, one, two, courant, image, grad = opening(
+        aperture_start, aperture_count, sent_a, sent_b, speeds, band, one, two
     )
     next_a = swap_pairs(to_a, "slab", 0)
     next_b = swap_pairs(to_b, "slab", 1)

time: 48 us -> 47.1 us (0.981)
  Pallas kernels: 9.81 us -> 8.58 us
    pallas_call x1, Pallas kernels: 1.61 us -> 0.59 us  [opening(): pl.pallas_call(opening_kernel, out_shape=(message, message, *same, couran...]
  transfers between devices with their start and end apart: 4 -> 4, of which waited for: 2 -> 3; matrix products, arithmetic and copies ran while one was open for 0% -> 0% of each run, Pallas kernels for 9% -> 7%
where the time goes in v8:
time: 47.1 us; the launch traced here: 46.8 us
  blocking collectives  22.3 us (47%)
  Pallas kernels  8.58 us (18%)
  starting transfers between devices  7.1 us (15%)
  waiting for transfers between devices  6.12 us (13%)
  between operations  1.99 us (4%)
  other arithmetic  0.66 us (1%)
    all_to_all x1, blocking collectives, per_device(): shares = lax.all_to_all(parts, 'shot', 0, 0, tiled=True)  12.2 us
    all_gather x1, blocking collectives, per_device(): speeds = lax.all_gather(velocity, 'shot')  10.2 us
    ppermute x4, starting transfers between devices, swap_pairs(): return lax.ppermute(block, axis, route)  7.1 us
    ppermute x4, waiting for transfers between devices, swap_pairs(): return lax.ppermute(block, axis, route)  6.12 us
    pallas_call x1, Pallas kernels, late_steps(): pl.pallas_call(kernel, out_shape=(final, final, *same), in_specs=[smem] *...  3.91 us
    pallas_call x1, Pallas kernels, early_steps(): pl.pallas_call(kernel, out_shape=(*same, waiting, parts), in_specs=[pl.Bl...  2.63 us
    pallas_call x1, Pallas kernels, pack(): pl.pallas_call(packing_kernel, out_shape=(message, message, drops, band,...  1.44 us
  transfers between devices with their start and end apart: 4, of which 3 were waited for; matrix products, arithmetic and copies ran while one was open for 0% of the time, Pallas kernels for 7%

profile of v8, /device:TPU:8, one launch (start us, length us, event | category | flops | bytes accessed | tf_op | source)
XLA Modules:
  0.0 46.8 jit_solution(5342114172225279719)
XLA Ops:
  0.6 1.4 %shard_map.130 = (f32[40,32,128]{2,1,0:T(8,128)S(1)}, f32[40,32,128]{2,1,0:T(8,128)S(1)}, f32[4,2,48,8,128]{4,3,2,1,0:T(8,128)S(1)}, bf16[256,128]{1,0:T(8,128)(...) custom-call(f32[1,16,32,128]{3,2,1,0:T(8,128)} %now_w.1, f32[1,16,32,128]{3,2,1,0:T(8,128)} %now_j.1, ...), custom_call_target="tpu_custom_call" | custom-call | bytes 4194304 | tf_op jit(solution)/shard_map/pallas_call | solution.py:75
  2.1 0.1 collective-permute-start.2
  2.2 5.0 %collective-permute-start.3 = (f32[40,32,128]{2,1,0:T(8,128)S(1)}, f32[40,32,128]{2,1,0:T(8,128)S(1)}, u32[]{:S(2)}, u32[]{:S(2)}) collective-permute-start(f32[40,32,128]{2,1,0:T(8,128)S(1)} %get-tuple-element.26.sent_b), channel_id=1, source_target_pairs={{1,2},{2,1},{5,6},{6,5},{9,10},{10,9},{13,14},{14,13},{17,18},{18,... | collective-permute-start | bytes 1966088 | tf_op jit(solution)/shard_map/ppermute | solution.py:21
  8.5 10.2 %all-gather = f32[128,8,128]{2,1,0:T(8,128)S(1)} all-gather(f32[16,8,128]{2,1,0:T(8,128)} %param.11), channel_id=2, replica_groups=mesh['shot'=8,'slab'=4] {'shot'}, dimensions={0}, use_global_device_ids=true | all-gather | bytes 589824 | tf_op jit(solution)/shard_map/all_gather | solution.py:515
  18.7 0.6 %shard_map.131 = (f32[16,32,128]{2,1,0:T(8,128)S(1)}, f32[16,32,128]{2,1,0:T(8,128)S(1)}, f32[2,48,48,128]{3,2,1,0:T(8,128)S(1)}, f32[2,48,48,128]{3,2,1,0:T(8,1...) custom-call(s32[1]{0:T(128)S(6)} %copy.36.start.refs_0_, ...), custom_call_target="tpu_custom_call", output_to_operand_aliasing={{2}: (6, {}), {3}: (7, {})} | custom-call | flops 4194304 | bytes 4194304 | tf_op jit(solution)/shard_map/pallas_call | solution.py:201
  19.2 0.1 collective-permute-start
  19.3 1.9 %collective-permute-start.1 = (f32[16,32,128]{2,1,0:T(8,128)S(1)}, f32[16,32,128]{2,1,0:T(8,128)S(1)}, u32[]{:S(2)}, u32[]{:S(2)}) collective-permute-start(f32[16,32,128]{2,1,0:T(8,128)S(1)} %get-tuple-element.31), channel_id=1, source_target_pairs={{1,2},{2,1},{5,6},{6,5},{9,10},{10,9},{13,14},{14,13},{17,18},{18,... | collective-permute-start | bytes 786440 | tf_op jit(solution)/shard_map/ppermute | solution.py:21
  21.3 0.0 collective-permute-done.2.refs_5_
  21.3 0.4 collective-permute-done.3.refs_6_
  21.6 2.6 %shard_map.132 = (f32[4,2,48,8,128]{4,3,2,1,0:T(8,128)S(1)}, f32[2,48,48,128]{3,2,1,0:T(8,128)S(1)}, f32[2,48,48,128]{3,2,1,0:T(8,128)S(1)}, f32[16,32,128]{2,1,...) custom-call(s32[1]{0:T(128)S(6)} %copy.37.count.refs_0_.refs_1_, ...), custom_call_target="tpu_custom_call", output_to_operand_aliasing={{0}: (9, {}), {1}: (10, {}), {2}: (11, {}), {3}: (12, {})} | custom-call | flops 20971520 | bytes 4194304 | tf_op jit(solution)/shard_map/pallas_call | solution.py:456
  24.3 3.8 %collective-permute-done.refs_2_ = f32[16,32,128]{2,1,0:T(8,128)S(1)} collective-permute-done((f32[16,32,128]{2,1,0:T(8,128)S(1)}, f32[16,32,128]{2,1,0:T(8,128)S(1)}, u32[]{:S(2)}, u32[]{:S(2)}) %collective-permute-start) | collective-permute-done | bytes 262176 | tf_op jit(solution)/shard_map/ppermute | solution.py:21
  28.1 1.9 %collective-permute-done.1.refs_3_ = f32[16,32,128]{2,1,0:T(8,128)S(1)} collective-permute-done((f32[16,32,128]{2,1,0:T(8,128)S(1)}, f32[16,32,128]{2,1,0:T(8,128)S(1)}, u32[]{:S(2)}, u32[]{:S(2)}) %collective-permute-start.1) | collective-permute-done | bytes 262176 | tf_op jit(solution)/shard_map/ppermute | solution.py:21
  30.0 3.9 %shard_map.133 = (f32[1,16,32,128]{3,2,1,0:T(8,128)}, f32[1,16,32,128]{3,2,1,0:T(8,128)}, f32[2,48,48,128]{3,2,1,0:T(8,128)S(1)}, f32[2,48,48,128]{3,2,1,0:T(8,1...) custom-call(s32[1]{0:T(128)S(6)} %copy.36.start.refs_0_, ...), custom_call_target="tpu_custom_call", output_to_operand_aliasing={{2}: (8, {}), {3}: (9, {}), {4}: (10, {}), {5}: (11, {}), {... | custom-call | flops 41943040 | bytes 6291456 | tf_op jit(solution)/shard_map/pallas_call | solution.py:480
  33.9 12.2 %all_to_all.5 = f32[8,16,8,128]{3,2,1,0:T(8,128)S(1)} all-to-all(f32[8,16,8,128]{3,2,1,0:T(8,128)S(1)} %get-tuple-element.46), channel_id=1, replica_groups=mesh['shot'=8,'slab'=4] {'shot'}, dimensions={0} | all-to-all | bytes 1048576 | tf_op jit(solution)/shard_map/all_to_all | solution.py:543
  46.1 0.7 %reduce_sum.9 = f32[16,8,128]{2,1,0:T(8,128)} reduce(f32[8,16,8,128]{3,2,1,0:T(8,128)S(1)} %all_to_all.5, f32[]{:T(128)} %constant.0.clone.1), dimensions={0}, to_apply=%region_0.0 | reduce | flops 114688 | bytes 589828 | tf_op jit(solution)/shard_map/reduce_sum | solution.py:544
Async XLA Ops:
  2.1 19.2 %collective-permute-start.2 = (f32[40,32,128]{2,1,0:T(8,128)S(1)}, f32[40,32,128]{2,1,0:T(8,128)S(1)}, u32[]{:S(2)}, u32[]{:S(2)}) collective-permute-start(f32[40,32,128]{2,1,0:T(8,128)S(1)} %get-tuple-element.25.sent_a), channel_id=1, source_target_pairs={{0,1},{1,0},{2,3},{3,2},{4,5},{5,4},{6,7},{7,6},{8,9},{9,8},{10,11... | collective-permute-start | bytes 1966088 | tf_op jit(solution)/shard_map/ppermute | solution.py:21
  2.2 19.5 %collective-permute-start.3 = (f32[40,32,128]{2,1,0:T(8,128)S(1)}, f32[40,32,128]{2,1,0:T(8,128)S(1)}, u32[]{:S(2)}, u32[]{:S(2)}) collective-permute-start(f32[40,32,128]{2,1,0:T(8,128)S(1)} %get-tuple-element.26.sent_b), channel_id=1, source_target_pairs={{1,2},{2,1},{5,6},{6,5},{9,10},{10,9},{13,14},{14,13},{17,18},{18,... | collective-permute-start | bytes 1966088 | tf_op jit(solution)/shard_map/ppermute | solution.py:21
  19.2 8.9 %collective-permute-start = (f32[16,32,128]{2,1,0:T(8,128)S(1)}, f32[16,32,128]{2,1,0:T(8,128)S(1)}, u32[]{:S(2)}, u32[]{:S(2)}) collective-permute-start(f32[16,32,128]{2,1,0:T(8,128)S(1)} %get-tuple-element.30), channel_id=1, source_target_pairs={{0,1},{1,0},{2,3},{3,2},{4,5},{5,4},{6,7},{7,6},{8,9},{9,8},{10,11... | collective-permute-start | bytes 786440 | tf_op jit(solution)/shard_map/ppermute | solution.py:21
  19.3 10.7 %collective-permute-start.1 = (f32[16,32,128]{2,1,0:T(8,128)S(1)}, f32[16,32,128]{2,1,0:T(8,128)S(1)}, u32[]{:S(2)}, u32[]{:S(2)}) collective-permute-start(f32[16,32,128]{2,1,0:T(8,128)S(1)} %get-tuple-element.31), channel_id=1, source_target_pairs={{1,2},{2,1},{5,6},{6,5},{9,10},{10,9},{13,14},{14,13},{17,18},{18,... | collective-permute-start | bytes 786440 | tf_op jit(solution)/shard_map/ppermute | solution.py:21

commit v9 on v8

--- a/solution.py
+++ b/solution.py
@@ -367,15 +367,12 @@
     courant_in,
     grad_in,
     parts_in,
-    final_w,
-    final_j,
+    finals,
     one,
     two,
     courant,
     grad,
     parts,
-    finals,
-    sems,
 ):
     cells, rows, depth = image.shape
     deep = steps * REACH
@@ -384,8 +381,6 @@
     odd = lax.axis_index("slab") % 2
     start_block = start[0]
     live = count[0]
-
-    copies, bring = bringing(sems)
 
     def finish(h, carry):
         right = h >= near
@@ -425,10 +420,6 @@
         last = finals if step == steps - 1 else None
         for pair in paired(groups):
             advance(now, other, courant, drops, band, step, pair, grad, False, deep, last)
-            if last is not None:
-                done = pl.ds(pair[0] - deep, len(pair) * REACH)
-                bring(finals.at[0, done], final_w.at[0, done])
-                bring(finals.at[1, done], final_j.at[0, done])
         now, other = other, now
 
     def place(x, carry):
@@ -438,8 +429,6 @@
         return carry
 
     lax.fori_loop(0, cells, place, 0, unroll=4)
-    for copy in copies:
-        copy.wait()
 
 
 def early_steps(count, small, from_a, from_b, courant, band, drops, one, two, grad, groups):
@@ -471,7 +460,7 @@
 def late_steps(steps, start, count, next_a, next_b, drops, band, image, waiting, one, two, courant, grad, parts):
     smem = pl.BlockSpec(memory_space=pltpu.SMEM)
     vmem = pl.BlockSpec(memory_space=pltpu.VMEM)
-    final = jax.ShapeDtypeStruct((1, *image.shape), jnp.float32)
+    finals = pltpu.VMEM((2, *image.shape), jnp.float32)
     same = [pltpu.VMEM(array.shape, array.dtype) for array in (one, two, courant, grad, parts)]
 
     def kernel(*refs):
@@ -479,18 +468,41 @@
 
     results = pl.pallas_call(
         kernel,
-        out_shape=(final, final, *same),
+        out_shape=(finals, *same),
         in_specs=[smem] * 2 + [vmem] * 11,
-        out_specs=(any_space(), any_space()) + (vmem,) * 5,
-        input_output_aliases={8: 2, 9: 3, 10: 4, 11: 5, 12: 6},
-        scratch_shapes=[
-            pltpu.VMEM((2, *image.shape), jnp.float32),
-            pltpu.SemaphoreType.DMA((2 * image.shape[0] // REACH,)),
-        ],
+        out_specs=(vmem,) * 6,
+        input_output_aliases={8: 1, 9: 2, 10: 3, 11: 4, 12: 5},
         compiler_params=pltpu.CompilerParams(vmem_limit_bytes=8 << 20),
         cost_estimate=pl.CostEstimate(flops=40 << 20, bytes_accessed=6 << 20, transcendentals=0),
     )(start, count, next_a, next_b, drops, band, image, waiting, one, two, courant, grad, parts)
-    return results[0], results[1], results[6]
+    return results[0], results[5]
+
+
+def closing_kernel(finals, shares, final_w, final_j, gradient, total, sems):
+    copies, bring = bringing(sems)
+    bring(finals.at[0], final_w.at[0])
+    bring(finals.at[1], final_j.at[0])
+    value = shares[0]
+    for group in range(1, shares.shape[0]):
+        value = value + shares[group]
+    total[...] = value
+    bring(total, gradient)
+    for copy in copies:
+        copy.wait()
+
+
+def closing(finals, shares):
+    final = jax.ShapeDtypeStruct((1, *finals.shape[1:]), jnp.float32)
+    block = shares.shape[1:]
+    return pl.pallas_call(
+        closing_kernel,
+        out_shape=(final, final, jax.ShapeDtypeStruct(block, jnp.float32)),
+        in_specs=[pl.BlockSpec(memory_space=pltpu.VMEM)] * 2,
+        out_specs=(any_space(),) * 3,
+        scratch_shapes=[pltpu.VMEM(block, jnp.float32), pltpu.SemaphoreType.DMA((3,))],
+        compiler_params=pltpu.CompilerParams(vmem_limit_bytes=8 << 20),
+        cost_estimate=pl.CostEstimate(flops=1 << 20, bytes_accessed=2 << 20, transcendentals=0),
+    )(finals, shares)
 
 
 def per_device(
@@ -524,7 +536,7 @@
     drops, one, two, grad, waiting, parts = early_steps(
         aperture_count, small, from_a, from_b, courant, band, drops, one, two, grad, lax.axis_size("shot")
     )
-    final_w, final_j, parts = late_steps(
+    finals, parts = late_steps(
         steps,
         aperture_start,
         aperture_count,
@@ -541,7 +553,7 @@
         parts,
     )
     shares = lax.all_to_all(parts, "shot", 0, 0, tiled=True)
-    return final_w, final_j, jnp.sum(shares, axis=0)
+    return closing(finals, shares)
 
 
 def solution(mesh):

time: 47.1 us -> 46.5 us (0.987)
  other arithmetic: 0.66 us -> 0 us
    reduce_sum x1 -> x0, other arithmetic: 0.66 us -> none  [per_device(): return (final_w, final_j, jnp.sum(shares, axis=0))]
    pallas_call x1 -> x2, Pallas kernels: 3.91 us -> 4 us  [the longest x1 3.17 us: late_steps(): pl.pallas_call(kernel, out_shape=(finals, *same), in_specs=[smem] * 2 + [...]
where the time goes in v9:
time: 46.5 us; the launch traced here: 46.3 us
  blocking collectives  22.5 us (48%)
  Pallas kernels  8.67 us (19%)
  starting transfers between devices  7.1 us (15%)
  waiting for transfers between devices  6.04 us (13%)
  between operations  1.99 us (4%)
    all_to_all x1, blocking collectives, per_device(): shares = lax.all_to_all(parts, 'shot', 0, 0, tiled=True)  12.4 us
    all_gather x1, blocking collectives, per_device(): speeds = lax.all_gather(velocity, 'shot')  10.2 us
    ppermute x4, starting transfers between devices, swap_pairs(): return lax.ppermute(block, axis, route)  7.1 us
    ppermute x4, waiting for transfers between devices, swap_pairs(): return lax.ppermute(block, axis, route)  6.04 us
    pallas_call x1, Pallas kernels, late_steps(): pl.pallas_call(kernel, out_shape=(finals, *same), in_specs=[smem] * 2 + [...  3.17 us
    pallas_call x1, Pallas kernels, early_steps(): pl.pallas_call(kernel, out_shape=(*same, waiting, parts), in_specs=[pl.Bl...  2.63 us
    pallas_call x1, Pallas kernels, pack(): pl.pallas_call(packing_kernel, out_shape=(message, message, drops, band,...  1.44 us
  transfers between devices with their start and end apart: 4, of which 3 were waited for; matrix products, arithmetic and copies ran while one was open for 0% of the time, Pallas kernels for 7%

profile of v9, /device:TPU:8, one launch (start us, length us, event | category | flops | bytes accessed | tf_op | source)
XLA Modules:
  0.0 46.3 jit_solution(4270781696817736523)
XLA Ops:
  0.6 1.4 %shard_map.130 = (f32[40,32,128]{2,1,0:T(8,128)S(1)}, f32[40,32,128]{2,1,0:T(8,128)S(1)}, f32[4,2,48,8,128]{4,3,2,1,0:T(8,128)S(1)}, bf16[256,128]{1,0:T(8,128)(...) custom-call(f32[1,16,32,128]{3,2,1,0:T(8,128)} %now_w.1, f32[1,16,32,128]{3,2,1,0:T(8,128)} %now_j.1, ...), custom_call_target="tpu_custom_call" | custom-call | bytes 4194304 | tf_op jit(solution)/shard_map/pallas_call | solution.py:75
  2.1 0.1 collective-permute-start.2
  2.2 5.0 %collective-permute-start.3 = (f32[40,32,128]{2,1,0:T(8,128)S(1)}, f32[40,32,128]{2,1,0:T(8,128)S(1)}, u32[]{:S(2)}, u32[]{:S(2)}) collective-permute-start(f32[40,32,128]{2,1,0:T(8,128)S(1)} %get-tuple-element.25.sent_b), channel_id=1, source_target_pairs={{1,2},{2,1},{5,6},{6,5},{9,10},{10,9},{13,14},{14,13},{17,18},{18,... | collective-permute-start | bytes 1966088 | tf_op jit(solution)/shard_map/ppermute | solution.py:21
  8.5 10.2 %all-gather = f32[128,8,128]{2,1,0:T(8,128)S(1)} all-gather(f32[16,8,128]{2,1,0:T(8,128)} %param.11), channel_id=2, replica_groups=mesh['shot'=8,'slab'=4] {'shot'}, dimensions={0}, use_global_device_ids=true | all-gather | bytes 589824 | tf_op jit(solution)/shard_map/all_gather | solution.py:527
  18.7 0.6 %shard_map.131 = (f32[16,32,128]{2,1,0:T(8,128)S(1)}, f32[16,32,128]{2,1,0:T(8,128)S(1)}, f32[2,48,48,128]{3,2,1,0:T(8,128)S(1)}, f32[2,48,48,128]{3,2,1,0:T(8,1...) custom-call(s32[1]{0:T(128)S(6)} %copy.36.start.refs_0_, ...), custom_call_target="tpu_custom_call", output_to_operand_aliasing={{2}: (6, {}), {3}: (7, {})} | custom-call | flops 4194304 | bytes 4194304 | tf_op jit(solution)/shard_map/pallas_call | solution.py:201
  19.2 0.1 collective-permute-start
  19.3 1.9 %collective-permute-start.1 = (f32[16,32,128]{2,1,0:T(8,128)S(1)}, f32[16,32,128]{2,1,0:T(8,128)S(1)}, u32[]{:S(2)}, u32[]{:S(2)}) collective-permute-start(f32[16,32,128]{2,1,0:T(8,128)S(1)} %get-tuple-element.30), channel_id=1, source_target_pairs={{1,2},{2,1},{5,6},{6,5},{9,10},{10,9},{13,14},{14,13},{17,18},{18,... | collective-permute-start | bytes 786440 | tf_op jit(solution)/shard_map/ppermute | solution.py:21
  21.3 0.0 collective-permute-done.2.refs_5_
  21.3 0.4 collective-permute-done.3.refs_6_
  21.6 2.6 %shard_map.132 = (f32[4,2,48,8,128]{4,3,2,1,0:T(8,128)S(1)}, f32[2,48,48,128]{3,2,1,0:T(8,128)S(1)}, f32[2,48,48,128]{3,2,1,0:T(8,128)S(1)}, f32[16,32,128]{2,1,...) custom-call(s32[1]{0:T(128)S(6)} %copy.37.count.refs_0_.refs_1_, ...), custom_call_target="tpu_custom_call", output_to_operand_aliasing={{0}: (9, {}), {1}: (10, {}), {2}: (11, {}), {3}: (12, {})} | custom-call | flops 20971520 | bytes 4194304 | tf_op jit(solution)/shard_map/pallas_call | solution.py:445
  24.3 3.8 %collective-permute-done.refs_2_ = f32[16,32,128]{2,1,0:T(8,128)S(1)} collective-permute-done((f32[16,32,128]{2,1,0:T(8,128)S(1)}, f32[16,32,128]{2,1,0:T(8,128)S(1)}, u32[]{:S(2)}, u32[]{:S(2)}) %collective-permute-start) | collective-permute-done | bytes 262176 | tf_op jit(solution)/shard_map/ppermute | solution.py:21
  28.0 1.9 %collective-permute-done.1.refs_3_ = f32[16,32,128]{2,1,0:T(8,128)S(1)} collective-permute-done((f32[16,32,128]{2,1,0:T(8,128)S(1)}, f32[16,32,128]{2,1,0:T(8,128)S(1)}, u32[]{:S(2)}, u32[]{:S(2)}) %collective-permute-start.1) | collective-permute-done | bytes 262176 | tf_op jit(solution)/shard_map/ppermute | solution.py:21
  29.9 3.2 %shard_map.133 = (f32[2,16,32,128]{3,2,1,0:T(8,128)S(1)}, f32[2,48,48,128]{3,2,1,0:T(8,128)S(1)}, f32[2,48,48,128]{3,2,1,0:T(8,128)S(1)}, f32[48,32,128]{2,1,0:T...) custom-call(s32[1]{0:T(128)S(6)} %copy.36.start.refs_0_, ...), custom_call_target="tpu_custom_call", output_to_operand_aliasing={{1}: (8, {}), {2}: (9, {}), {3}: (10, {}), {4}: (11, {}), {... | custom-call | flops 41943040 | bytes 6291456 | tf_op jit(solution)/shard_map/pallas_call | solution.py:469
  33.1 12.4 %all_to_all.5.shares = f32[8,16,8,128]{3,2,1,0:T(8,128)S(1)} all-to-all(f32[8,16,8,128]{3,2,1,0:T(8,128)S(1)} %get-tuple-element.44), channel_id=1, replica_groups=mesh['shot'=8,'slab'=4] {'shot'}, dimensions={0} | all-to-all | bytes 1048576 | tf_op jit(solution)/shard_map/all_to_all | solution.py:555
  45.5 0.8 %shard_map.134 = (f32[1,16,32,128]{3,2,1,0:T(8,128)}, f32[1,16,32,128]{3,2,1,0:T(8,128)}, f32[16,8,128]{2,1,0:T(8,128)}) custom-call(f32[2,16,32,128]{3,2,1,0:T(8,128)S(1)} %get-tuple-element.43.finals, f32[8,16,8,128]{3,2,1,0:T(8,128)S(1)} %all_to_all.5.shares), custom_call_target="tpu_custom_call" | custom-call | flops 1048576 | bytes 2097152 | tf_op jit(solution)/shard_map/pallas_call | solution.py:497
Async XLA Ops:
  2.1 19.2 %collective-permute-start.2 = (f32[40,32,128]{2,1,0:T(8,128)S(1)}, f32[40,32,128]{2,1,0:T(8,128)S(1)}, u32[]{:S(2)}, u32[]{:S(2)}) collective-permute-start(f32[40,32,128]{2,1,0:T(8,128)S(1)} %get-tuple-element.24.sent_a), channel_id=1, source_target_pairs={{0,1},{1,0},{2,3},{3,2},{4,5},{5,4},{6,7},{7,6},{8,9},{9,8},{10,11... | collective-permute-start | bytes 1966088 | tf_op jit(solution)/shard_map/ppermute | solution.py:21
  2.2 19.5 %collective-permute-start.3 = (f32[40,32,128]{2,1,0:T(8,128)S(1)}, f32[40,32,128]{2,1,0:T(8,128)S(1)}, u32[]{:S(2)}, u32[]{:S(2)}) collective-permute-start(f32[40,32,128]{2,1,0:T(8,128)S(1)} %get-tuple-element.25.sent_b), channel_id=1, source_target_pairs={{1,2},{2,1},{5,6},{6,5},{9,10},{10,9},{13,14},{14,13},{17,18},{18,... | collective-permute-start | bytes 1966088 | tf_op jit(solution)/shard_map/ppermute | solution.py:21
  19.2 8.8 %collective-permute-start = (f32[16,32,128]{2,1,0:T(8,128)S(1)}, f32[16,32,128]{2,1,0:T(8,128)S(1)}, u32[]{:S(2)}, u32[]{:S(2)}) collective-permute-start(f32[16,32,128]{2,1,0:T(8,128)S(1)} %get-tuple-element.29), channel_id=1, source_target_pairs={{0,1},{1,0},{2,3},{3,2},{4,5},{5,4},{6,7},{7,6},{8,9},{9,8},{10,11... | collective-permute-start | bytes 786440 | tf_op jit(solution)/shard_map/ppermute | solution.py:21
  19.3 10.6 %collective-permute-start.1 = (f32[16,32,128]{2,1,0:T(8,128)S(1)}, f32[16,32,128]{2,1,0:T(8,128)S(1)}, u32[]{:S(2)}, u32[]{:S(2)}) collective-permute-start(f32[16,32,128]{2,1,0:T(8,128)S(1)} %get-tuple-element.30), channel_id=1, source_target_pairs={{1,2},{2,1},{5,6},{6,5},{9,10},{10,9},{13,14},{14,13},{17,18},{18,... | collective-permute-start | bytes 786440 | tf_op jit(solution)/shard_map/ppermute | solution.py:21

commit v10 on v9

--- a/solution.py
+++ b/solution.py
@@ -352,16 +352,80 @@
     return [starts[i : i + 2] for i in range(0, len(starts), 2)]
 
 
-def late_kernel(
-    steps,
+def take_side(on_left, live, message, drops, band, waiting, finals, one, two, courant, grad):
+    cells = grad.shape[0]
+    rows = grad.shape[1]
+    deep = message.shape[0]
+    near = deep - 2 * REACH
+    steps = deep // REACH
+
+    def place(left, right):
+        return on_left * left + (1 - on_left) * right
+
+    def finish(layer, carry):
+        x = place(deep - near, deep + cells) + layer
+        h = place(0, near) + layer
+        for tile in range(rows // TILE):
+            alive = jnp.where(tile < live, time_step * time_step / SCALE, 0.0)
+            own = pl.ds(tile * TILE, TILE)
+            padded = pl.ds(TILE + tile * TILE, TILE)
+            speed = message[layer, own, :]
+            factor = alive * (speed * speed)
+            courant[x, own, :] = factor
+            for field in range(2):
+                change = factor * waiting[field, h, own, :]
+                two[field, x, padded, :] = two[field, x, padded, :] + change
+        return carry
+
+    lax.fori_loop(0, near, finish, 0, unroll=4)
+    first = place(deep - near - REACH, deep + cells + near)
+    for field in range(2):
+        for i in range(REACH):
+            two[field, first + i, pl.ds(TILE, rows), :] = message[near + field * REACH + i]
+    add_drops(two, drops, [first + i for i in range(REACH)])
+
+    now, other = two, one
+    for step in range(1, steps):
+        inner = REACH if step == 1 else cells // 2 - REACH * (step - 2)
+        depths = range(REACH * (step + 1) - deep, inner, REACH)
+        halo = [place(deep + d, deep + cells - REACH - d) for d in depths if d < 0]
+        own = [place(deep + d, deep + cells - REACH - d) for d in depths if d >= 0]
+        last = finals if step == steps - 1 else None
+        if halo:
+            advance(now, other, courant, drops, band, step, halo, None, False, deep)
+        advance(now, other, courant, drops, band, step, own, grad, False, deep, last)
+        now, other = other, now
+
+
+def first_side_kernel(
+    count,
+    message,
+    drops,
+    band,
+    waiting,
+    one_in,
+    two_in,
+    courant_in,
+    grad_in,
+    finals,
+    one,
+    two,
+    courant,
+    grad,
+):
+    odd = lax.axis_index("slab") % 2
+    take_side(odd, count[0], message, drops, band, waiting, finals, one, two, courant, grad)
+
+
+def second_side_kernel(
     start,
     count,
-    next_a,
-    next_b,
+    message,
     drops,
     band,
+    waiting,
     image,
-    waiting,
+    finals_in,
     one_in,
     two_in,
     courant_in,
@@ -374,56 +438,20 @@
     grad,
     parts,
 ):
-    cells, rows, depth = image.shape
-    deep = steps * REACH
-    near = deep - 2 * REACH
-    tiles = rows // TILE
+    cells, rows, _ = image.shape
+    deep = message.shape[0]
+    steps = deep // REACH
     odd = lax.axis_index("slab") % 2
     start_block = start[0]
-    live = count[0]
-
-    def finish(h, carry):
-        right = h >= near
-        layer = jnp.where(right, h - near, h)
-        x = jnp.where(right, deep + cells, deep - near) + layer
-        use_a = jnp.where(right, 1 - odd, odd) == 1
-        for tile in range(tiles):
-            alive = jnp.where(tile < live, time_step * time_step / SCALE, 0.0)
-            own = pl.ds(tile * TILE, TILE)
-            speed = jnp.where(use_a, next_a[layer, own, :], next_b[layer, own, :])
-            factor = alive * (speed * speed)
-            courant[x, own, :] = factor
-            for field in range(2):
-                at = pl.ds(TILE + tile * TILE, TILE)
-                change = factor * waiting[field, h, own, :]
-                two[field, x, at, :] = two[field, x, at, :] + change
-        return carry
-
-    lax.fori_loop(0, 2 * near, finish, 0, unroll=4)
-    inner = pl.ds(TILE, rows)
-    for message, left in ((next_a, odd), (next_b, 1 - odd)):
-        for field in range(2):
-            for i in range(REACH):
-                x = left * (deep - near - REACH) + (1 - left) * (deep + cells + near) + i
-                two[field, x, inner, :] = message[near + field * REACH + i]
-    add_drops(two, drops, range(deep - near - REACH, deep - near))
-    add_drops(two, drops, range(deep + cells + near, deep + cells + near + REACH))
-
-    now, other = two, one
-    for step in range(1, steps):
-        edge = range(REACH * (step + 1), deep, REACH)
-        groups = list(edge) + [x + cells + deep - REACH * (step + 1) for x in edge]
-        for pair in paired(groups):
-            advance(now, other, courant, drops, band, step, pair, None, False, deep)
-        own = range(deep, deep + cells, REACH)
-        groups = [own[0], own[-1]] if step == 1 else own
-        last = finals if step == steps - 1 else None
-        for pair in paired(groups):
-            advance(now, other, courant, drops, band, step, pair, grad, False, deep, last)
-        now, other = other, now
+    take_side(1 - odd, count[0], message, drops, band, waiting, finals, one, two, courant, grad)
+    now, other = (one, two) if steps % 2 else (two, one)
+    for step in range(3, steps):
+        reach = cells // 2 - REACH * (step - 2)
+        for groups in paired(range(deep + reach, deep + cells - reach, REACH)):
+            advance(now, other, courant, drops, band, step, groups, grad, False, deep, finals)
 
     def place(x, carry):
-        for tile in range(tiles):
+        for tile in range(rows // TILE):
             at = pl.ds(tile * TILE, TILE)
             parts[start_block + tile, x] = image[x, at, :] * grad[x, at, :]
         return carry
@@ -457,24 +485,33 @@
     )(count, *map(in_hbm, small), from_a, from_b, courant, band, drops, one, two, grad)
 
 
-def late_steps(steps, start, count, next_a, next_b, drops, band, image, waiting, one, two, courant, grad, parts):
-    smem = pl.BlockSpec(memory_space=pltpu.SMEM)
+def first_side(count, message, drops, band, waiting, one, two, courant, grad):
     vmem = pl.BlockSpec(memory_space=pltpu.VMEM)
-    finals = pltpu.VMEM((2, *image.shape), jnp.float32)
-    same = [pltpu.VMEM(array.shape, array.dtype) for array in (one, two, courant, grad, parts)]
-
-    def kernel(*refs):
-        late_kernel(steps, *refs)
-
+    finals = pltpu.VMEM((2, *grad.shape), jnp.float32)
+    same = [pltpu.VMEM(array.shape, array.dtype) for array in (one, two, courant, grad)]
+    return pl.pallas_call(
+        first_side_kernel,
+        out_shape=(finals, *same),
+        in_specs=[pl.BlockSpec(memory_space=pltpu.SMEM)] + [vmem] * 8,
+        out_specs=(vmem,) * 5,
+        input_output_aliases={5: 1, 6: 2, 7: 3, 8: 4},
+        compiler_params=pltpu.CompilerParams(vmem_limit_bytes=8 << 20),
+        cost_estimate=pl.CostEstimate(flops=20 << 20, bytes_accessed=3 << 20, transcendentals=0),
+    )(count, message, drops, band, waiting, one, two, courant, grad)
+
+
+def second_side(start, count, message, drops, band, waiting, image, finals, one, two, courant, grad, parts):
+    vmem = pl.BlockSpec(memory_space=pltpu.VMEM)
+    same = [pltpu.VMEM(array.shape, array.dtype) for array in (finals, one, two, courant, grad, parts)]
     results = pl.pallas_call(
-        kernel,
-        out_shape=(finals, *same),
-        in_specs=[smem] * 2 + [vmem] * 11,
+        second_side_kernel,
+        out_shape=tuple(same),
+        in_specs=[pl.BlockSpec(memory_space=pltpu.SMEM)] * 2 + [vmem] * 11,
         out_specs=(vmem,) * 6,
-        input_output_aliases={8: 1, 9: 2, 10: 3, 11: 4, 12: 5},
+        input_output_aliases={7: 0, 8: 1, 9: 2, 10: 3, 11: 4, 12: 5},
         compiler_params=pltpu.CompilerParams(vmem_limit_bytes=8 << 20),
-        cost_estimate=pl.CostEstimate(flops=40 << 20, bytes_accessed=6 << 20, transcendentals=0),
-    )(start, count, next_a, next_b, drops, band, image, waiting, one, two, courant, grad, parts)
+        cost_estimate=pl.CostEstimate(flops=20 << 20, bytes_accessed=3 << 20, transcendentals=0),
+    )(start, count, message, drops, band, waiting, image, finals, one, two, courant, grad, parts)
     return results[0], results[5]
 
 
@@ -536,16 +573,18 @@
     drops, one, two, grad, waiting, parts = early_steps(
         aperture_count, small, from_a, from_b, courant, band, drops, one, two, grad, lax.axis_size("shot")
     )
-    finals, parts = late_steps(
-        steps,
+    finals, one, two, courant, grad = first_side(
+        aperture_count, next_a, drops, band, waiting, one, two, courant, grad
+    )
+    finals, parts = second_side(
         aperture_start,
         aperture_count,
-        next_a,
         next_b,
         drops,
         band,
+        waiting,
         image,
-        waiting,
+        finals,
         one,
         two,
         courant,

time: 46.5 us -> 45.9 us (0.987)
  the two profiles are of different devices: /device:TPU:8 before, /device:TPU:0 now
where the time goes in v10:
time: 45.9 us; the launch traced here: 45.5 us
  blocking collectives  22.3 us (49%)
  starting transfers between devices  8.87 us (19%)
  Pallas kernels  8.72 us (19%)
  waiting for transfers between devices  3.63 us (8%)
  between operations  2 us (4%)
    all_to_all x1, blocking collectives, per_device(): shares = lax.all_to_all(parts, 'shot', 0, 0, tiled=True)  12.2 us
    all_gather x1, blocking collectives, per_device(): speeds = lax.all_gather(velocity, 'shot')  10.2 us
    ppermute x4, starting transfers between devices, swap_pairs(): return lax.ppermute(block, axis, route)  8.87 us
    ppermute x4, waiting for transfers between devices, swap_pairs(): return lax.ppermute(block, axis, route)  3.63 us
    pallas_call x1, Pallas kernels, early_steps(): pl.pallas_call(kernel, out_shape=(*same, waiting, parts), in_specs=[pl.Bl...  2.65 us
    pallas_call x1, Pallas kernels, second_side(): pl.pallas_call(second_side_kernel, out_shape=tuple(same), in_specs=[pl.Bl...  1.83 us
    pallas_call x1, Pallas kernels, pack(): pl.pallas_call(packing_kernel, out_shape=(message, message, drops, band,...  1.44 us
    pallas_call x1, Pallas kernels, first_side(): pl.pallas_call(first_side_kernel, out_shape=(finals, *same), in_specs=[pl...  1.38 us
  transfers between devices with their start and end apart: 4, of which 1 were waited for; matrix products, arithmetic and copies ran while one was open for 0% of the time, Pallas kernels for 10%

profile of v10, /device:TPU:0, one launch (start us, length us, event | category | flops | bytes accessed | tf_op | source)
XLA Modules:
  0.0 45.5 jit_solution(7965888668908893395)
XLA Ops:
  0.6 1.4 %shard_map.130 = (f32[40,32,128]{2,1,0:T(8,128)S(1)}, f32[40,32,128]{2,1,0:T(8,128)S(1)}, f32[4,2,48,8,128]{4,3,2,1,0:T(8,128)S(1)}, bf16[256,128]{1,0:T(8,128)(...) custom-call(f32[1,16,32,128]{3,2,1,0:T(8,128)} %now_w.1, f32[1,16,32,128]{3,2,1,0:T(8,128)} %now_j.1, ...), custom_call_target="tpu_custom_call" | custom-call | bytes 4194304 | tf_op jit(solution)/shard_map/pallas_call | solution.py:75
  2.1 3.1 %collective-permute-start.1 = (f32[40,32,128]{2,1,0:T(8,128)S(1)}, f32[40,32,128]{2,1,0:T(8,128)S(1)}, u32[]{:S(2)}, u32[]{:S(2)}) collective-permute-start(f32[40,32,128]{2,1,0:T(8,128)S(1)} %get-tuple-element.29.sent_a), channel_id=1, source_target_pairs={{0,1},{1,0},{2,3},{3,2},{4,5},{5,4},{6,7},{7,6},{8,9},{9,8},{10,11... | collective-permute-start | bytes 1966088 | tf_op jit(solution)/shard_map/ppermute | solution.py:21
  5.2 0.7 %collective-permute-start.2 = (f32[40,32,128]{2,1,0:T(8,128)S(1)}, f32[40,32,128]{2,1,0:T(8,128)S(1)}, u32[]{:S(2)}, u32[]{:S(2)}) collective-permute-start(f32[40,32,128]{2,1,0:T(8,128)S(1)} %get-tuple-element.30.sent_b), channel_id=1, source_target_pairs={{1,2},{2,1},{5,6},{6,5},{9,10},{10,9},{13,14},{14,13},{17,18},{18,... | collective-permute-start | bytes 1966088 | tf_op jit(solution)/shard_map/ppermute | solution.py:21
  7.2 10.2 %all-gather = f32[128,8,128]{2,1,0:T(8,128)S(1)} all-gather(f32[16,8,128]{2,1,0:T(8,128)} %param.11), channel_id=2, replica_groups=mesh['shot'=8,'slab'=4] {'shot'}, dimensions={0}, use_global_device_ids=true | all-gather | bytes 589824 | tf_op jit(solution)/shard_map/all_gather | solution.py:564
  17.3 0.6 %shard_map.131 = (f32[16,32,128]{2,1,0:T(8,128)S(1)}, f32[16,32,128]{2,1,0:T(8,128)S(1)}, f32[2,48,48,128]{3,2,1,0:T(8,128)S(1)}, f32[2,48,48,128]{3,2,1,0:T(8,1...) custom-call(s32[1]{0:T(128)S(6)} %copy.46.start, ...), custom_call_target="tpu_custom_call", output_to_operand_aliasing={{2}: (6, {}), {3}: (7, {})} | custom-call | flops 4194304 | bytes 4194304 | tf_op jit(solution)/shard_map/pallas_call | solution.py:201
  17.9 4.4 %collective-permute-start.3 = (f32[16,32,128]{2,1,0:T(8,128)S(1)}, f32[16,32,128]{2,1,0:T(8,128)S(1)}, u32[]{:S(2)}, u32[]{:S(2)}) collective-permute-start(f32[16,32,128]{2,1,0:T(8,128)S(1)} %get-tuple-element.43), channel_id=1, source_target_pairs={{0,1},{1,0},{2,3},{3,2},{4,5},{5,4},{6,7},{7,6},{8,9},{9,8},{10,11... | collective-permute-start | bytes 786440 | tf_op jit(solution)/shard_map/ppermute | solution.py:21
  22.3 0.7 %collective-permute-start = (f32[16,32,128]{2,1,0:T(8,128)S(1)}, f32[16,32,128]{2,1,0:T(8,128)S(1)}, u32[]{:S(2)}, u32[]{:S(2)}) collective-permute-start(f32[16,32,128]{2,1,0:T(8,128)S(1)} %get-tuple-element.34), channel_id=1, source_target_pairs={{1,2},{2,1},{5,6},{6,5},{9,10},{10,9},{13,14},{14,13},{17,18},{18,... | collective-permute-start | bytes 786440 | tf_op jit(solution)/shard_map/ppermute | solution.py:21
  23.0 0.0 collective-permute-done.1.refs_5_
  23.0 0.0 collective-permute-done.2.refs_6_
  23.0 2.7 %shard_map.132 = (f32[4,2,48,8,128]{4,3,2,1,0:T(8,128)S(1)}, f32[2,48,48,128]{3,2,1,0:T(8,128)S(1)}, f32[2,48,48,128]{3,2,1,0:T(8,128)S(1)}, f32[16,32,128]{2,1,...) custom-call(s32[1]{0:T(128)S(6)} %copy.47.count.refs_0_, ...), custom_call_target="tpu_custom_call", output_to_operand_aliasing={{0}: (9, {}), {1}: (10, {}), {2}: (11, {}), {3}: (12, {})} | custom-call | flops 20971520 | bytes 4194304 | tf_op jit(solution)/shard_map/pallas_call | solution.py:473
  25.7 3.6 %collective-permute-done.3.message = f32[16,32,128]{2,1,0:T(8,128)S(1)} collective-permute-done((f32[16,32,128]{2,1,0:T(8,128)S(1)}, f32[16,32,128]{2,1,0:T(8,128)S(1)}, u32[]{:S(2)}, u32[]{:S(2)}) %collective-permute-start.3) | collective-permute-done | bytes 262176 | tf_op jit(solution)/shard_map/ppermute | solution.py:21
  29.3 1.4 %shard_map.133 = (f32[2,16,32,128]{3,2,1,0:T(8,128)S(1)}, f32[2,48,48,128]{3,2,1,0:T(8,128)S(1)}, f32[2,48,48,128]{3,2,1,0:T(8,128)S(1)}, f32[48,32,128]{2,1,0:T(8,128)S(1)}, f32[16,32,128]{2,1,0:T(8,128)S(1)}) custom-call(s32[1]{0:T(128)S(6)} %copy.47.count.refs_0_, ...), custom_call_target="tpu_custom_call", output_to_operand_aliasing={{1}: (5, {}), {2}: (6, {}), {3}: (7, {}), {4}: (8, {})} | custom-call | flops 20971520 | bytes 3145728 | tf_op jit(solution)/shard_map/pallas_call | solution.py:492
  30.7 0.0 collective-permute-done.message
  30.7 1.8 %shard_map.134 = (f32[2,16,32,128]{3,2,1,0:T(8,128)S(1)}, f32[2,48,48,128]{3,2,1,0:T(8,128)S(1)}, f32[2,48,48,128]{3,2,1,0:T(8,128)S(1)}, f32[48,32,128]{2,1,0:T...) custom-call(s32[1]{0:T(128)S(6)} %copy.46.start, ...), custom_call_target="tpu_custom_call", output_to_operand_aliasing={{0}: (7, {}), {1}: (8, {}), {2}: (9, {}), {3}: (10, {}), {4... | custom-call | flops 20971520 | bytes 3145728 | tf_op jit(solution)/shard_map/pallas_call | solution.py:506
  32.6 12.2 %all_to_all.5.shares = f32[8,16,8,128]{3,2,1,0:T(8,128)S(1)} all-to-all(f32[8,16,8,128]{3,2,1,0:T(8,128)S(1)} %get-tuple-element.54), channel_id=1, replica_groups=mesh['shot'=8,'slab'=4] {'shot'}, dimensions={0} | all-to-all | bytes 1048576 | tf_op jit(solution)/shard_map/all_to_all | solution.py:594
  44.7 0.8 %shard_map.135 = (f32[1,16,32,128]{3,2,1,0:T(8,128)}, f32[1,16,32,128]{3,2,1,0:T(8,128)}, f32[16,8,128]{2,1,0:T(8,128)}) custom-call(f32[2,16,32,128]{3,2,1,0:T(8,128)S(1)} %get-tuple-element.53.finals, f32[8,16,8,128]{3,2,1,0:T(8,128)S(1)} %all_to_all.5.shares), custom_call_target="tpu_custom_call" | custom-call | flops 1048576 | bytes 2097152 | tf_op jit(solution)/shard_map/pallas_call | solution.py:534
Async XLA Ops:
  2.1 20.9 %collective-permute-start.1 = (f32[40,32,128]{2,1,0:T(8,128)S(1)}, f32[40,32,128]{2,1,0:T(8,128)S(1)}, u32[]{:S(2)}, u32[]{:S(2)}) collective-permute-start(f32[40,32,128]{2,1,0:T(8,128)S(1)} %get-tuple-element.29.sent_a), channel_id=1, source_target_pairs={{0,1},{1,0},{2,3},{3,2},{4,5},{5,4},{6,7},{7,6},{8,9},{9,8},{10,11... | collective-permute-start | bytes 1966088 | tf_op jit(solution)/shard_map/ppermute | solution.py:21
  5.2 17.9 %collective-permute-start.2 = (f32[40,32,128]{2,1,0:T(8,128)S(1)}, f32[40,32,128]{2,1,0:T(8,128)S(1)}, u32[]{:S(2)}, u32[]{:S(2)}) collective-permute-start(f32[40,32,128]{2,1,0:T(8,128)S(1)} %get-tuple-element.30.sent_b), channel_id=1, source_target_pairs={{1,2},{2,1},{5,6},{6,5},{9,10},{10,9},{13,14},{14,13},{17,18},{18,... | collective-permute-start | bytes 1966088 | tf_op jit(solution)/shard_map/ppermute | solution.py:21
  17.9 11.4 %collective-permute-start.3 = (f32[16,32,128]{2,1,0:T(8,128)S(1)}, f32[16,32,128]{2,1,0:T(8,128)S(1)}, u32[]{:S(2)}, u32[]{:S(2)}) collective-permute-start(f32[16,32,128]{2,1,0:T(8,128)S(1)} %get-tuple-element.43), channel_id=1, source_target_pairs={{0,1},{1,0},{2,3},{3,2},{4,5},{5,4},{6,7},{7,6},{8,9},{9,8},{10,11... | collective-permute-start | bytes 786440 | tf_op jit(solution)/shard_map/ppermute | solution.py:21
  22.3 8.4 %collective-permute-start = (f32[16,32,128]{2,1,0:T(8,128)S(1)}, f32[16,32,128]{2,1,0:T(8,128)S(1)}, u32[]{:S(2)}, u32[]{:S(2)}) collective-permute-start(f32[16,32,128]{2,1,0:T(8,128)S(1)} %get-tuple-element.34), channel_id=1, source_target_pairs={{1,2},{2,1},{5,6},{6,5},{9,10},{10,9},{13,14},{14,13},{17,18},{18,... | collective-permute-start | bytes 786440 | tf_op jit(solution)/shard_map/ppermute | solution.py:21

commit v11 on v10

--- a/solution.py
+++ b/solution.py
@@ -277,18 +277,20 @@
     amps_j_in,
     from_a,
     from_b,
-    courant,
     band,
     drops_in,
     one_in,
     two_in,
+    courant_in,
     grad_in,
     drops,
     one,
     two,
+    courant,
     grad,
     waiting,
     parts,
+    finals,
     cells_w,
     cells_j,
     amps_w,
@@ -346,10 +348,20 @@
     for groups in paired(range(deep + REACH, deep + cells - REACH, REACH)):
         advance(two, one, courant, drops, band, 1, groups, grad, False, deep)
 
+    @pl.when(no_second_partner())
+    def _():
+        nothing = from_b.at[pl.ds(0, deep)]
+        take_side(1 - odd, count[0], nothing, drops, band, waiting, finals, one, two, courant, grad)
+
 
 def paired(starts):
     starts = list(starts)
     return [starts[i : i + 2] for i in range(0, len(starts), 2)]
+
+
+def no_second_partner():
+    slab = lax.axis_index("slab")
+    return (slab == 0) | ((slab % 2 == 1) & (slab == lax.axis_size("slab") - 1))
 
 
 def take_side(on_left, live, message, drops, band, waiting, finals, one, two, courant, grad):
@@ -403,6 +415,7 @@
     drops,
     band,
     waiting,
+    finals_in,
     one_in,
     two_in,
     courant_in,
@@ -443,7 +456,11 @@
     steps = deep // REACH
     odd = lax.axis_index("slab") % 2
     start_block = start[0]
-    take_side(1 - odd, count[0], message, drops, band, waiting, finals, one, two, courant, grad)
+
+    @pl.when(jnp.logical_not(no_second_partner()))
+    def _():
+        take_side(1 - odd, count[0], message, drops, band, waiting, finals, one, two, courant, grad)
+
     now, other = (one, two) if steps % 2 else (two, one)
     for step in range(3, steps):
         reach = cells // 2 - REACH * (step - 2)
@@ -464,40 +481,39 @@
     steps = drops.shape[0]
     waiting = pltpu.VMEM((2, 2 * (steps - 2) * REACH, rows, depth), jnp.float32)
     parts = pltpu.VMEM((groups, cells, TILE, depth), jnp.float32)
+    finals = pltpu.VMEM((2, *grad.shape), jnp.float32)
     vmem = pl.BlockSpec(memory_space=pltpu.VMEM)
-    same = [pltpu.VMEM(array.shape, array.dtype) for array in (drops, one, two, grad)]
+    same = [pltpu.VMEM(array.shape, array.dtype) for array in (drops, one, two, courant, grad)]
 
     def kernel(*refs):
         early_kernel(steps, *refs)
 
     return pl.pallas_call(
         kernel,
-        out_shape=(*same, waiting, parts),
+        out_shape=(*same, waiting, parts, finals),
         in_specs=[pl.BlockSpec(memory_space=pltpu.SMEM)]
         + [pl.BlockSpec(memory_space=pltpu.HBM)] * 4
-        + [any_space()] * 2
-        + [vmem] * 6,
-        out_specs=(vmem,) * 6,
-        input_output_aliases={9: 0, 10: 1, 11: 2, 12: 3},
+        + [vmem] * 8,
+        out_specs=(vmem,) * 8,
+        input_output_aliases={8: 0, 9: 1, 10: 2, 11: 3, 12: 4},
         scratch_shapes=[pltpu.SMEM(array.shape, array.dtype) for array in small] + [pltpu.SemaphoreType.DMA((12,))],
         compiler_params=pltpu.CompilerParams(vmem_limit_bytes=8 << 20),
         cost_estimate=pl.CostEstimate(flops=20 << 20, bytes_accessed=4 << 20, transcendentals=0),
-    )(count, *map(in_hbm, small), from_a, from_b, courant, band, drops, one, two, grad)
-
-
-def first_side(count, message, drops, band, waiting, one, two, courant, grad):
+    )(count, *map(in_hbm, small), from_a, from_b, band, drops, one, two, courant, grad)
+
+
+def first_side(count, message, drops, band, waiting, finals, one, two, courant, grad):
     vmem = pl.BlockSpec(memory_space=pltpu.VMEM)
-    finals = pltpu.VMEM((2, *grad.shape), jnp.float32)
-    same = [pltpu.VMEM(array.shape, array.dtype) for array in (one, two, courant, grad)]
+    same = [pltpu.VMEM(array.shape, array.dtype) for array in (finals, one, two, courant, grad)]
     return pl.pallas_call(
         first_side_kernel,
-        out_shape=(finals, *same),
-        in_specs=[pl.BlockSpec(memory_space=pltpu.SMEM)] + [vmem] * 8,
+        out_shape=tuple(same),
+        in_specs=[pl.BlockSpec(memory_space=pltpu.SMEM)] + [vmem] * 9,
         out_specs=(vmem,) * 5,
-        input_output_aliases={5: 1, 6: 2, 7: 3, 8: 4},
+        input_output_aliases={5: 0, 6: 1, 7: 2, 8: 3, 9: 4},
         compiler_params=pltpu.CompilerParams(vmem_limit_bytes=8 << 20),
         cost_estimate=pl.CostEstimate(flops=20 << 20, bytes_accessed=3 << 20, transcendentals=0),
-    )(count, message, drops, band, waiting, one, two, courant, grad)
+    )(count, message, drops, band, waiting, finals, one, two, courant, grad)
 
 
 def second_side(start, count, message, drops, band, waiting, image, finals, one, two, courant, grad, parts):
@@ -570,11 +586,11 @@
     )
     next_a = swap_pairs(to_a, "slab", 0)
     next_b = swap_pairs(to_b, "slab", 1)
-    drops, one, two, grad, waiting, parts = early_steps(
+    drops, one, two, courant, grad, waiting, parts, finals = early_steps(
         aperture_count, small, from_a, from_b, courant, band, drops, one, two, grad, lax.axis_size("shot")
     )
     finals, one, two, courant, grad = first_side(
-        aperture_count, next_a, drops, band, waiting, one, two, courant, grad
+        aperture_count, next_a, drops, band, waiting, finals, one, two, courant, grad
     )
     finals, parts = second_side(
         aperture_start,

time: 45.9 us -> 45.2 us (0.985)
  the two profiles are of different devices: /device:TPU:0 before, /device:TPU:8 now
where the time goes in v11:
time: 45.2 us; the launch traced here: 45 us
  blocking collectives  22.6 us (50%)
  Pallas kernels  8.72 us (19%)
  starting transfers between devices  7.1 us (16%)
  waiting for transfers between devices  4.56 us (10%)
  between operations  2 us (4%)
    all_to_all x1, blocking collectives, per_device(): shares = lax.all_to_all(parts, 'shot', 0, 0, tiled=True)  12.4 us
    all_gather x1, blocking collectives, per_device(): speeds = lax.all_gather(velocity, 'shot')  10.2 us
    ppermute x4, starting transfers between devices, swap_pairs(): return lax.ppermute(block, axis, route)  7.1 us
    ppermute x4, waiting for transfers between devices, swap_pairs(): return lax.ppermute(block, axis, route)  4.56 us
    pallas_call x1, Pallas kernels, early_steps(): pl.pallas_call(kernel, out_shape=(*same, waiting, parts, finals), in_spec...  2.65 us
    pallas_call x1, Pallas kernels, second_side(): pl.pallas_call(second_side_kernel, out_shape=tuple(same), in_specs=[pl.Bl...  1.83 us
    pallas_call x1, Pallas kernels, pack(): pl.pallas_call(packing_kernel, out_shape=(message, message, drops, band,...  1.44 us
    pallas_call x1, Pallas kernels, first_side(): pl.pallas_call(first_side_kernel, out_shape=tuple(same), in_specs=[pl.Blo...  1.39 us
  transfers between devices with their start and end apart: 4, of which 3 were waited for; matrix products, arithmetic and copies ran while one was open for 0% of the time, Pallas kernels for 10%

profile of v11, /device:TPU:8, one launch (start us, length us, event | category | flops | bytes accessed | tf_op | source)
XLA Modules:
  0.0 45.0 jit_solution(3060786028789862812)
XLA Ops:
  0.6 1.4 %shard_map.130 = (f32[40,32,128]{2,1,0:T(8,128)S(1)}, f32[40,32,128]{2,1,0:T(8,128)S(1)}, f32[4,2,48,8,128]{4,3,2,1,0:T(8,128)S(1)}, bf16[256,128]{1,0:T(8,128)(...) custom-call(f32[1,16,32,128]{3,2,1,0:T(8,128)} %now_w.1, f32[1,16,32,128]{3,2,1,0:T(8,128)} %now_j.1, ...), custom_call_target="tpu_custom_call" | custom-call | bytes 4194304 | tf_op jit(solution)/shard_map/pallas_call | solution.py:75
  2.1 0.1 collective-permute-start.1
  2.2 5.0 %collective-permute-start.2 = (f32[40,32,128]{2,1,0:T(8,128)S(1)}, f32[40,32,128]{2,1,0:T(8,128)S(1)}, u32[]{:S(2)}, u32[]{:S(2)}) collective-permute-start(f32[40,32,128]{2,1,0:T(8,128)S(1)} %get-tuple-element.32.sent_b), channel_id=1, source_target_pairs={{1,2},{2,1},{5,6},{6,5},{9,10},{10,9},{13,14},{14,13},{17,18},{18,... | collective-permute-start | bytes 1966088 | tf_op jit(solution)/shard_map/ppermute | solution.py:21
  8.5 10.2 %all-gather = f32[128,8,128]{2,1,0:T(8,128)S(1)} all-gather(f32[16,8,128]{2,1,0:T(8,128)} %param.11), channel_id=2, replica_groups=mesh['shot'=8,'slab'=4] {'shot'}, dimensions={0}, use_global_device_ids=true | all-gather | bytes 589824 | tf_op jit(solution)/shard_map/all_gather | solution.py:580
  18.7 0.6 %shard_map.131 = (f32[16,32,128]{2,1,0:T(8,128)S(1)}, f32[16,32,128]{2,1,0:T(8,128)S(1)}, f32[2,48,48,128]{3,2,1,0:T(8,128)S(1)}, f32[2,48,48,128]{3,2,1,0:T(8,1...) custom-call(s32[1]{0:T(128)S(6)} %copy.50.start, ...), custom_call_target="tpu_custom_call", output_to_operand_aliasing={{2}: (6, {}), {3}: (7, {})} | custom-call | flops 4194304 | bytes 4194304 | tf_op jit(solution)/shard_map/pallas_call | solution.py:201
  19.2 0.1 collective-permute-start.3
  19.3 1.9 %collective-permute-start = (f32[16,32,128]{2,1,0:T(8,128)S(1)}, f32[16,32,128]{2,1,0:T(8,128)S(1)}, u32[]{:S(2)}, u32[]{:S(2)}) collective-permute-start(f32[16,32,128]{2,1,0:T(8,128)S(1)} %get-tuple-element.36), channel_id=1, source_target_pairs={{1,2},{2,1},{5,6},{6,5},{9,10},{10,9},{13,14},{14,13},{17,18},{18,... | collective-permute-start | bytes 786440 | tf_op jit(solution)/shard_map/ppermute | solution.py:21
  21.3 0.0 collective-permute-done.1.refs_5_
  21.3 0.4 collective-permute-done.2.refs_6_
  21.6 2.6 %shard_map.132 = (f32[4,2,48,8,128]{4,3,2,1,0:T(8,128)S(1)}, f32[2,48,48,128]{3,2,1,0:T(8,128)S(1)}, f32[2,48,48,128]{3,2,1,0:T(8,128)S(1)}, f32[48,32,128]{2,1,...) custom-call(s32[1]{0:T(128)S(6)} %copy.51.count.refs_0_, ...), custom_call_target="tpu_custom_call", output_to_operand_aliasing={{0}: (8, {}), {1}: (9, {}), {2}: (10, {}), {3}: (11, {}), {... | custom-call | flops 20971520 | bytes 4194304 | tf_op jit(solution)/shard_map/pallas_call | solution.py:491
  24.3 3.7 %collective-permute-done.3.message = f32[16,32,128]{2,1,0:T(8,128)S(1)} collective-permute-done((f32[16,32,128]{2,1,0:T(8,128)S(1)}, f32[16,32,128]{2,1,0:T(8,128)S(1)}, u32[]{:S(2)}, u32[]{:S(2)}) %collective-permute-start.3) | collective-permute-done | bytes 262176 | tf_op jit(solution)/shard_map/ppermute | solution.py:21
  28.0 1.4 %shard_map.133 = (f32[2,16,32,128]{3,2,1,0:T(8,128)S(1)}, f32[2,48,48,128]{3,2,1,0:T(8,128)S(1)}, f32[2,48,48,128]{3,2,1,0:T(8,128)S(1)}, f32[48,32,128]{2,1,0:T(8,128)S(1)}, f32[16,32,128]{2,1,0:T(8,128)S(1)}) custom-call(s32[1]{0:T(128)S(6)} %copy.51.count.refs_0_, ...), custom_call_target="tpu_custom_call", output_to_operand_aliasing={{0}: (5, {}), {1}: (6, {}), {2}: (7, {}), {3}: (8, {}), {4}... | custom-call | flops 20971520 | bytes 3145728 | tf_op jit(solution)/shard_map/pallas_call | solution.py:508
  29.4 0.5 %collective-permute-done.message = f32[16,32,128]{2,1,0:T(8,128)S(1)} collective-permute-done((f32[16,32,128]{2,1,0:T(8,128)S(1)}, f32[16,32,128]{2,1,0:T(8,128)S(1)}, u32[]{:S(2)}, u32[]{:S(2)}) %collective-permute-start) | collective-permute-done | bytes 262176 | tf_op jit(solution)/shard_map/ppermute | solution.py:21
  29.9 1.8 %shard_map.134 = (f32[2,16,32,128]{3,2,1,0:T(8,128)S(1)}, f32[2,48,48,128]{3,2,1,0:T(8,128)S(1)}, f32[2,48,48,128]{3,2,1,0:T(8,128)S(1)}, f32[48,32,128]{2,1,0:T...) custom-call(s32[1]{0:T(128)S(6)} %copy.50.start, ...), custom_call_target="tpu_custom_call", output_to_operand_aliasing={{0}: (7, {}), {1}: (8, {}), {2}: (9, {}), {3}: (10, {}), {4... | custom-call | flops 20971520 | bytes 3145728 | tf_op jit(solution)/shard_map/pallas_call | solution.py:522
  31.7 12.4 %all_to_all.5.shares = f32[8,16,8,128]{3,2,1,0:T(8,128)S(1)} all-to-all(f32[8,16,8,128]{3,2,1,0:T(8,128)S(1)} %get-tuple-element.58), channel_id=1, replica_groups=mesh['shot'=8,'slab'=4] {'shot'}, dimensions={0} | all-to-all | bytes 1048576 | tf_op jit(solution)/shard_map/all_to_all | solution.py:610
  44.2 0.8 %shard_map.135 = (f32[1,16,32,128]{3,2,1,0:T(8,128)}, f32[1,16,32,128]{3,2,1,0:T(8,128)}, f32[16,8,128]{2,1,0:T(8,128)}) custom-call(f32[2,16,32,128]{3,2,1,0:T(8,128)S(1)} %get-tuple-element.57.finals, f32[8,16,8,128]{3,2,1,0:T(8,128)S(1)} %all_to_all.5.shares), custom_call_target="tpu_custom_call" | custom-call | flops 1048576 | bytes 2097152 | tf_op jit(solution)/shard_map/pallas_call | solution.py:550
Async XLA Ops:
  2.1 19.2 %collective-permute-start.1 = (f32[40,32,128]{2,1,0:T(8,128)S(1)}, f32[40,32,128]{2,1,0:T(8,128)S(1)}, u32[]{:S(2)}, u32[]{:S(2)}) collective-permute-start(f32[40,32,128]{2,1,0:T(8,128)S(1)} %get-tuple-element.31.sent_a), channel_id=1, source_target_pairs={{0,1},{1,0},{2,3},{3,2},{4,5},{5,4},{6,7},{7,6},{8,9},{9,8},{10,11... | collective-permute-start | bytes 1966088 | tf_op jit(solution)/shard_map/ppermute | solution.py:21
  2.2 19.5 %collective-permute-start.2 = (f32[40,32,128]{2,1,0:T(8,128)S(1)}, f32[40,32,128]{2,1,0:T(8,128)S(1)}, u32[]{:S(2)}, u32[]{:S(2)}) collective-permute-start(f32[40,32,128]{2,1,0:T(8,128)S(1)} %get-tuple-element.32.sent_b), channel_id=1, source_target_pairs={{1,2},{2,1},{5,6},{6,5},{9,10},{10,9},{13,14},{14,13},{17,18},{18,... | collective-permute-start | bytes 1966088 | tf_op jit(solution)/shard_map/ppermute | solution.py:21
  19.2 8.7 %collective-permute-start.3 = (f32[16,32,128]{2,1,0:T(8,128)S(1)}, f32[16,32,128]{2,1,0:T(8,128)S(1)}, u32[]{:S(2)}, u32[]{:S(2)}) collective-permute-start(f32[16,32,128]{2,1,0:T(8,128)S(1)} %get-tuple-element.45), channel_id=1, source_target_pairs={{0,1},{1,0},{2,3},{3,2},{4,5},{5,4},{6,7},{7,6},{8,9},{9,8},{10,11... | collective-permute-start | bytes 786440 | tf_op jit(solution)/shard_map/ppermute | solution.py:21
  19.3 10.6 %collective-permute-start = (f32[16,32,128]{2,1,0:T(8,128)S(1)}, f32[16,32,128]{2,1,0:T(8,128)S(1)}, u32[]{:S(2)}, u32[]{:S(2)}) collective-permute-start(f32[16,32,128]{2,1,0:T(8,128)S(1)} %get-tuple-element.36), channel_id=1, source_target_pairs={{1,2},{2,1},{5,6},{6,5},{9,10},{10,9},{13,14},{14,13},{17,18},{18,... | collective-permute-start | bytes 786440 | tf_op jit(solution)/shard_map/ppermute | solution.py:21
